TPU v7x, 32 devices: a whole 2x2x4 slice. The times are simulated.
32 devices in a mesh: dom: 8 (over z, x), rep: 4 (over y, core).
Axes of the slice: x: 2, y: 2, z: 4, core: 2. Of those that a mesh axis runs over, the one named last changes fastest.
Arguments:
- features: bfloat16 [32768, 1024], P(('dom', 'rep')), may hold values from -6 to 6
- node_type: int32 [32768], P(('dom', 'rep')), may hold values 0 or 1
- neighbours: int32 [32768, 50], P(('dom', 'rep')), may hold values from 0 to 1535, as said below
- importance: float32 [32768, 50], P(('dom', 'rep')), may hold values from 0 to 1, as said below
- send_rows: int32 [16384], P(('dom', 'rep')), may hold values from 0 to 1023, as said below
- live_rows: int32 [32], P(('dom', 'rep')), may hold values from 512 to 1024, as said below
- proj_board: bfloat16 [512, 1024], replicated, may hold values from -0.25 to 0.25
- q_weight: bfloat16 [1024, 1024], replicated, may hold values from -0.1875 to 0.1875
- q_bias: float32 [1024], replicated, may hold values from -3 to 3
- w_weight: bfloat16 [2048, 1024], replicated, may hold values from -0.125 to 0.125
- w_bias: float32 [1024], replicated, may hold values from -3 to 3
- cotangent: bfloat16 [32768, 1024], P(('dom', 'rep')), may hold values from -6 to 6
Outputs:
- embedding: float32 [32768, 1024], P(('dom', 'rep'))
- grad_features: float32 [32768, 1024], P(('dom', 'rep'))
- grad_proj: float32 [512, 1024], replicated
- grad_q: float32 [1024, 1024], replicated
- grad_q_bias: float32 [1024], replicated
- grad_w: float32 [2048, 1024], replicated
- grad_w_bias: float32 [1024], replicated
Inputs may be any that keep to these rules, and one draw needn't show every extreme that they name: `live_rows`: live rows of a device lie between half of 1024 and 1024; the first device has all 1024 live. `send_rows`: every entry names a live row of the sending device; every peer receives exactly 64 rows. `neighbours`: Own-row entries name live rows; padded slots hold 0. `importance`: each node has at least one slot with a positive weight; padded slots weigh 0.
All inputs are finite; a program needn't handle non-finite values. No bound on the sum of `node_type` on one device may be relied on, other than what follows from the above.
Results may differ from a plain program's by a relative error of at most 0.0075.
Values may be sent and summed in bfloat16 or wider, within the bound.
No kernel may reach another device: no remote copies, remote signals or barrier semaphores. Data moves between devices by JAX's collectives and lax.ppermute only.
A program may use at most 192 MiB of HBM per device.

v0:
```python
import jax
import jax.numpy as jnp
from jax import lax
from jax.sharding import PartitionSpec as P


def contract_rows(left, right):
    return lax.dot_general(
        left, right, (((0,), (0,)), ((), ())), preferred_element_type=jnp.float32
    )


def contract_cols(left, right):
    return lax.dot_general(
        left, right, (((1,), (1,)), ((), ())), preferred_element_type=jnp.float32
    )


def silu_slope(value):
    sigma = jax.nn.sigmoid(value)
    return sigma * (1.0 + value * (1.0 - sigma))


def build_adjacency(neighbours, importance, columns):
    rows, slots = neighbours.shape
    block = min(256, rows)
    column_ids = lax.iota(jnp.int32, columns)

    def build_one_block(pair):
        index, weight = pair
        match = index[:, :, None] == column_ids[None, None, :]
        return jnp.sum(jnp.where(match, weight[:, :, None], 0.0), axis=1)

    blocks = lax.map(
        build_one_block,
        (
            neighbours.reshape(rows // block, block, slots),
            importance.reshape(rows // block, block, slots),
        ),
    )
    return blocks.reshape(rows, columns)


def send_table(send_rows, rows):
    halo = send_rows.shape[0]
    block = min(256, halo)
    row_ids = lax.iota(jnp.int32, rows)

    def send_one_block(index):
        return (index[:, None] == row_ids[None, :]).astype(jnp.bfloat16)

    blocks = lax.map(send_one_block, send_rows.reshape(halo // block, block))
    return blocks.reshape(halo, rows)


def per_device(
    features,
    node_type,
    neighbours,
    importance,
    send_rows,
    live_rows,
    proj_board,
    q_weight,
    q_bias,
    w_weight,
    w_bias,
    cotangent,
):
    rows = features.shape[0]
    width = q_weight.shape[0]
    board_width = proj_board.shape[0]
    live = (lax.iota(jnp.int32, rows) < live_rows[0])[:, None]
    board = (node_type == 1)[:, None]
    lowered = features[:, :board_width]
    projected = jnp.dot(lowered, proj_board, preferred_element_type=jnp.float32)
    hidden = jnp.where(board, projected, features.astype(jnp.float32)).astype(jnp.bfloat16)
    pre = jnp.dot(hidden, q_weight, preferred_element_type=jnp.float32) + q_bias
    active = jax.nn.silu(pre).astype(jnp.bfloat16)
    incoming = lax.all_to_all(active[send_rows], "dom", split_axis=0, concat_axis=0, tiled=True)
    table = jnp.concatenate([active, incoming], axis=0)
    columns = table.shape[0]
    total = jnp.sum(importance, axis=1, keepdims=True)
    adjacency = build_adjacency(neighbours, importance, columns)
    upper = adjacency.astype(jnp.bfloat16)
    lower = (adjacency - upper.astype(jnp.float32)).astype(jnp.bfloat16)
    agg = jnp.dot(upper, table, preferred_element_type=jnp.float32) + jnp.dot(
        lower, table, preferred_element_type=jnp.float32
    )
    mean = agg / total
    joined = jnp.concatenate([hidden, mean.astype(jnp.bfloat16)], axis=1)
    pre2 = jnp.dot(joined, w_weight, preferred_element_type=jnp.float32) + w_bias
    post = jax.nn.silu(pre2)
    scale = lax.rsqrt(jnp.sum(post * post, axis=1, keepdims=True) + 1e-06)
    embedding = jnp.where(live, post * scale, 0.0)
    grad_out = jnp.where(live, cotangent.astype(jnp.float32), 0.0)
    dpost = scale * grad_out - post * (scale * scale * scale) * jnp.sum(
        post * grad_out, axis=1, keepdims=True
    )
    dpre2 = (dpost * silu_slope(pre2)).astype(jnp.bfloat16)
    grad_w = contract_rows(joined, dpre2)
    grad_w_bias = jnp.sum(dpre2.astype(jnp.float32), axis=0)
    djoined = contract_cols(dpre2, w_weight)
    dagg = djoined[:, width:] / total
    dtable = lax.dot_general(
        adjacency,
        dagg,
        (((0,), (0,)), ((), ())),
        precision=lax.Precision.HIGHEST,
        preferred_element_type=jnp.float32,
    )
    returned = lax.all_to_all(
        dtable[rows:].astype(jnp.bfloat16), "dom", split_axis=0, concat_axis=0, tiled=True
    ).astype(jnp.float32)
    onehot = send_table(send_rows, rows)
    high_part = returned.astype(jnp.bfloat16)
    rest = returned - high_part.astype(jnp.float32)
    middle_part = rest.astype(jnp.bfloat16)
    low_part = (rest - middle_part.astype(jnp.float32)).astype(jnp.bfloat16)
    owned = (
        contract_rows(onehot, high_part)
        + contract_rows(onehot, middle_part)
        + contract_rows(onehot, low_part)
    )
    dactive = dtable[:rows] + owned
    dpre = (dactive * silu_slope(pre)).astype(jnp.bfloat16)
    grad_q = contract_rows(hidden, dpre)
    grad_q_bias = jnp.sum(dpre.astype(jnp.float32), axis=0)
    dhidden = (contract_cols(dpre, q_weight) + djoined[:, :width]).astype(jnp.bfloat16)
    board_part = contract_cols(dhidden, proj_board)
    board_full = jnp.concatenate(
        [board_part, jnp.zeros((rows, width - board_width), jnp.float32)], axis=1
    )
    grad_features = jnp.where(board, board_full, dhidden.astype(jnp.float32))
    grad_proj = contract_rows(lowered, jnp.where(board, dhidden, jnp.zeros_like(dhidden)))
    summed = lax.psum((grad_proj, grad_q, grad_q_bias, grad_w, grad_w_bias), ("dom", "rep"))
    return (embedding, grad_features, summed[0], summed[1], summed[2], summed[3], summed[4])


def solution(mesh):
    placed = (
        P(("dom", "rep"), None),
        P(("dom", "rep")),
        P(("dom", "rep"), None),
        P(("dom", "rep"), None),
        P(("dom", "rep")),
        P(("dom", "rep")),
        P(),
        P(),
        P(),
        P(),
        P(),
        P(("dom", "rep"), None),
    )
    return jax.shard_map(
        per_device,
        mesh=mesh,
        in_specs=placed,
        out_specs=(P(("dom", "rep"), None), P(("dom", "rep"), None), P(), P(), P(), P(), P()),
        check_vma=False,
    )
```

profile of v0, /device:TPU:0, one launch (start us, length us, event | category | flops | bytes accessed | tf_op | source)
XLA Modules:
  0.0 492.0 jit_solution(1489269421360150495)
XLA Ops:
  8.1 4.0 copy.37
  12.1 3.2 select_convert_fusion
  15.3 5.7 %multiply_convert_fusion.1 = (bf16[1024,1024]{1,0:T(8,128)(2,1)}, f32[1024,1024]{1,0:T(8,128)}) fusion(f32[1024]{0:T(1024)S(1)} %copy-done.18, bf16[1024,1024]{0,1:T(8,128)(2,1)S(1)} %select_convert_fusion, bf16[1024,1024]{1,0:T(8,128)(2,1)S(1)} %copy-done), kind=kOutput, calls=%fused_computation.34 | convolution fusion | flops 2153775104 | bytes 10489856 | tf_op jit(solution)/shard_map/dot_general | solution.py:78
  21.0 5.3 %gather_fusion = bf16[512,1024]{1,0:T(8,128)(2,1)} fusion(bf16[1024,1024]{1,0:T(8,128)(2,1)} %get-tuple-element.129, s32[1024]{0:T(1024)S(1)} %pad_clamp_fusion), kind=kCustom, calls=%fused_computation | custom fusion | bytes 2099200 | tf_op jit(solution)/shard_map/gather | solution.py:80
  26.4 7.5 %all-to-all-start = ((bf16[8,64,1024]{2,1,0:T(8,128)(2,1)}), bf16[8,64,1024]{2,1,0:T(8,128)(2,1)S(1)}, u32[]{:S(2)}, u32[]{:S(2)}) async-start(bf16[8,64,1024]{2,1,0:T(8,128)(2,1)} %bitcast.2), calls=%async_computation | async-start | bytes 2097152 | tf_op jit(solution)/shard_map/all_to_all | solution.py:80
  33.9 1.0 reshape.115
  34.9 1.0 reshape.116
  36.0 49.9 %while.22 = (s32[]{:T(128)}, f32[4,256,1536]{2,1,0:T(8,128)}, s32[4,256,50]{1,0,2:T(4,128)S(1)}, f32[4,256,50]{1,0,2:T(4,128)S(1)}, s32[]{:T(128)}) while((s32[]{:T(128)}, f32[4,256,1536]{2,1,0:T(8,128)}, s32[4,256,50]{1,0,2:T(4,128)S(1)}, f32[4,256,50]{1,0,2:T(4,128)S(1)}, s32[]{:T(128)}) %tuple.53), condition=%wide.region_2.3_spmd.clone, body=%wide.region_0.2_spmd.clone.sunk | while | flops 58589184 | bytes 5231173 | solution.py:34
  36.1 11.1 %select_reduce_fusion.2 = f32[256,1536]{1,0:T(8,128)S(1)} fusion(f32[256,50]{0,1:T(8,128)S(1)} %bitcast.57, s32[256,50]{0,1:T(8,128)S(1)} %bitcast.58), kind=kLoop, calls=%fused_computation.4.clone.1 | loop fusion | flops 58589184 | bytes 1675264 | tf_op jit(solution)/shard_map/while/body/eval_jaxpr/reduce_sum | solution.py:32
  47.2 1.3 bitcast_dynamic-update-slice_fusion.2
  48.6 11.1 %select_reduce_fusion.2 = f32[256,1536]{1,0:T(8,128)S(1)} fusion(f32[256,50]{0,1:T(8,128)S(1)} %bitcast.57, s32[256,50]{0,1:T(8,128)S(1)} %bitcast.58), kind=kLoop, calls=%fused_computation.4.clone.1 | loop fusion | flops 58589184 | bytes 1675264 | tf_op jit(solution)/shard_map/while/body/eval_jaxpr/reduce_sum | solution.py:32
  59.7 1.3 bitcast_dynamic-update-slice_fusion.2
  61.1 11.1 %select_reduce_fusion.2 = f32[256,1536]{1,0:T(8,128)S(1)} fusion(f32[256,50]{0,1:T(8,128)S(1)} %bitcast.57, s32[256,50]{0,1:T(8,128)S(1)} %bitcast.58), kind=kLoop, calls=%fused_computation.4.clone.1 | loop fusion | flops 58589184 | bytes 1675264 | tf_op jit(solution)/shard_map/while/body/eval_jaxpr/reduce_sum | solution.py:32
  72.2 1.3 bitcast_dynamic-update-slice_fusion.2
  73.5 11.1 %select_reduce_fusion.2 = f32[256,1536]{1,0:T(8,128)S(1)} fusion(f32[256,50]{0,1:T(8,128)S(1)} %bitcast.57, s32[256,50]{0,1:T(8,128)S(1)} %bitcast.58), kind=kLoop, calls=%fused_computation.4.clone.1 | loop fusion | flops 58589184 | bytes 1675264 | tf_op jit(solution)/shard_map/while/body/eval_jaxpr/reduce_sum | solution.py:32
  84.6 1.3 bitcast_dynamic-update-slice_fusion.2
  85.9 1.0 reduce_sum.54
  87.6 9.0 %fusion.19 = f32[1024,1024]{0,1:T(8,128)} fusion(bf16[512,1024]{1,0:T(8,128)(2,1)S(1)} %bitcast.62, bf16[1024,1024]{1,0:T(8,128)(2,1)} %get-tuple-element.129, f32[1024,1536]{1,0:T(8,128)} %bitcast.67), kind=kOutput, calls=%fused_computation.49 | convolution fusion | flops 3229089792 | bytes 13631488 | tf_op jit(solution)/shard_map/dot_general | solution.py:87
  96.6 6.0 %divide_convert_fusion = bf16[1024,1024]{0,1:T(8,128)(2,1)S(1)} fusion(f32[1024,1024]{0,1:T(8,128)} %fusion.19, f32[1024,1536]{1,0:T(8,128)S(1)} %bitcast.68, f32[1024]{0:T(1024)S(1)} %reduce_sum.54, bf16[512,1024]{1,0:T(8,128)(2,1)S(1)} %bitcast.63, bf16[1024,1024]{1,0:T(8,128)(2,1)S(1)} %copy-done.1), kind=kOutput, calls=%fused_computation.33 | convolution fusion | flops 3236954112 | bytes 15732736 | tf_op jit(solution)/shard_map/dot_general | solution.py:87
  102.7 6.2 %multiply_reduce_fusion = (f32[1024]{0:T(1024)S(1)}, f32[1024]{0:T(1024)S(1)}, f32[1024,1024]{1,0:T(8,128)S(1)}) fusion(bf16[1024,1024]{1,0:T(8,128)(2,1)S(1)} %copy-done.7, pred[1024]{0:T(1024)(128)(4,1)S(1)} %iota_compare_fusion.2, f32[1024]{0:T(1024)S(1)} %copy-done.12, bf16[2048,1024]{1,0:T(8,128)(2,1)S(1)} %copy-done.16, ...), kind=kOutput, calls=%fused_computation.27 | convolution fusion | flops 4314888192 | bytes 14693376 | tf_op jit(solution)/shard_map/dot_general | solution.py:92
  108.9 4.6 convert_reduce_fusion
  113.5 1.3 copy-done.8
  114.8 4.7 fusion.33
  119.5 41.2 %fusion.9 = f32[1536,1024]{1,0:T(8,128)S(1)} fusion(f32[1024,1536]{1,0:T(8,128)S(1)} %bitcast.69, f32[1024,2048]{0,1:T(8,128)S(1)} %fusion.33, f32[1024]{0:T(1024)S(1)} %reduce_sum.54), kind=kOutput, calls=%fused_computation.21 | convolution fusion | flops 19328401408 | bytes 16781312 | tf_op jit(solution)/shard_map/dot_general | solution.py:105
  160.8 2.7 copy-done.9
  163.5 1.2 slice.42
  164.6 6.0 %all-to-all-start.1 = ((bf16[8,64,1024]{2,1,0:T(8,128)(2,1)}), bf16[8,64,1024]{2,1,0:T(8,128)(2,1)S(1)}, u32[]{:S(2)}, u32[]{:S(2)}) async-start(bf16[8,64,1024]{2,1,0:T(8,128)(2,1)} %bitcast.59), calls=%async_computation.1 | async-start | bytes 2097152 | tf_op jit(solution)/shard_map/all_to_all | solution.py:112
  170.7 1.9 while.23
  170.7 1.0 fusion.59
  171.7 0.9 fusion.59
  172.6 10.6 %fusion.12 = f32[2048,1024]{1,0:T(8,128)} fusion(bf16[1024,1024]{1,0:T(8,128)(2,1)} %copy-done.8, bf16[1024,1024]{0,1:T(8,128)(2,1)} %copy-done.25, bf16[1024,1024]{0,1:T(8,128)(2,1)} %copy-done.20), kind=kOutput, calls=%fused_computation.39 | convolution fusion | flops 4303355904 | bytes 14680064 | tf_op jit(solution)/shard_map/dot_general | solution.py:8
  183.3 12.8 %all-to-all-done.1 = bf16[8,64,1024]{2,1,0:T(8,128)(2,1)S(1)} async-done(((bf16[8,64,1024]{2,1,0:T(8,128)(2,1)}), bf16[8,64,1024]{2,1,0:T(8,128)(2,1)S(1)}, u32[]{:S(2)}, u32[]{:S(2)}) %all-to-all-start.1) | async-done | bytes 1048608 | tf_op jit(solution)/shard_map/all_to_all | solution.py:112
  196.4 2.7 fusion.35
  199.1 1.3 fusion.34
  201.9 3.0 convert_reduce_fusion.1
  204.9 4.3 fusion.36
  209.3 4.7 fusion.6
  214.0 1.3 copy-done.4
  215.3 2.6 fusion.20
  217.9 3.3 fusion.37
  221.2 2.7 convert_select_fusion
  224.0 5.4 %copy.45 = f32[1024,1024]{1,0:T(8,128)} copy(f32[1024,1024]{0,1:T(8,128)} %convert_select_fusion) | data formatting | bytes 8388608
  229.3 39.7 %all-reduce.1 = (f32[1024]{0:T(1024)}, f32[1024]{0:T(1024)}) all-reduce(f32[1024]{0:T(1024)S(1)} %get-tuple-element.132, f32[1024]{0:T(1024)S(1)} %get-tuple-element.122), channel_id=1, replica_groups=mesh['dom'=8,'rep'=4] {'dom','rep'}, use_global_device_ids=true, to_apply=%region_11.12 | all-reduce | flops 2048 | bytes 16384 | tf_op jit(solution)/shard_map/psum | solution.py:136
  269.0 203.3 %all-reduce.5.cloned.1.call-done = (f32[512,1024]{0,1:T(8,128)}, f32[1024,1024]{1,0:T(8,128)}, f32[2048,1024]{1,0:T(8,128)}) async-done(((f32[512,1024]{0,1:T(8,128)}, f32[1024,1024]{1,0:T(8,128)}, f32[2048,1024]{1,0:T(8,128)}), (f32[512,1024]{0,1:T(8,128)}, f32[1024,1024]{1,0:T(8,128)}, f32[2048,1024]{1,0:T(8,128)})) %all-reduce.5.cloned.1.call-update) | async-done | bytes 14680080 | tf_op jit(solution)/shard_map/psum | solution.py:136
  472.3 2.9 copy.46
  475.2 5.1 %copy.80 = f32[1024,1024]{1,0:T(8,128)} copy(f32[1024,1024]{1,0:T(8,128)} %get-tuple-element.208) | data formatting | bytes 8388608
  480.3 1.1 copy-done.2
  481.3 3.4 copy.81
  (83 shorter events, 3.3 us)
Async XLA Ops:
  7.2 8.1 %copy-start = (bf16[1024,1024]{1,0:T(8,128)(2,1)S(1)}, bf16[1024,1024]{1,0:T(8,128)(2,1)}, u32[]{:S(2)}) copy-start(bf16[1024,1024]{1,0:T(8,128)(2,1)} %param.23) | copy-start | bytes 6291460
  7.2 4.9 copy-start.10
  7.2 4.9 copy-start.17
  8.0 7.2 %copy-start.13 = (pred[1024]{0:T(1024)(128)(4,1)}, pred[1024]{0:T(1024)(128)(4,1)S(1)}, u32[]{:S(2)}) copy-start(pred[1024]{0:T(1024)(128)(4,1)S(1)} %broadcast_compare_fusion) | copy-start | bytes 3076
  12.0 3.3 copy-start.18
  15.3 5.7 %copy-start.20 = (bf16[1024,1024]{0,1:T(8,128)(2,1)}, bf16[1024,1024]{0,1:T(8,128)(2,1)S(1)}, u32[]{:S(2)}) copy-start(bf16[1024,1024]{0,1:T(8,128)(2,1)S(1)} %select_convert_fusion) | copy-start | bytes 6291460
  26.4 61.1 %all-to-all-start = ((bf16[8,64,1024]{2,1,0:T(8,128)(2,1)}), bf16[8,64,1024]{2,1,0:T(8,128)(2,1)S(1)}, u32[]{:S(2)}, u32[]{:S(2)}) async-start(bf16[8,64,1024]{2,1,0:T(8,128)(2,1)} %bitcast.2), calls=%async_computation | async-start | bytes 2097152 | tf_op jit(solution)/shard_map/all_to_all | solution.py:80
  87.5 9.1 %copy-start.1 = (bf16[1024,1024]{1,0:T(8,128)(2,1)S(1)}, bf16[1024,1024]{1,0:T(8,128)(2,1)}, u32[]{:S(2)}) copy-start(bf16[1024,1024]{1,0:T(8,128)(2,1)} %get-tuple-element.129) | copy-start | bytes 6291460
  87.5 9.1 %copy-start.15 = (f32[4,256,1536]{2,1,0:T(8,128)S(1)}, f32[4,256,1536]{2,1,0:T(8,128)}, u32[]{:S(2)}) copy-start(f32[4,256,1536]{2,1,0:T(8,128)} %get-tuple-element.56) | copy-start | bytes 18874372
  96.6 6.1 %copy-start.7 = (bf16[1024,1024]{1,0:T(8,128)(2,1)S(1)}, bf16[1024,1024]{1,0:T(8,128)(2,1)}, u32[]{:S(2)}) copy-start(bf16[1024,1024]{1,0:T(8,128)(2,1)} %param.27) | copy-start | bytes 6291460
  96.6 6.1 %copy-start.12 = (f32[1024]{0:T(1024)S(1)}, f32[1024]{0:T(1024)}, u32[]{:S(2)}) copy-start(f32[1024]{0:T(1024)} %param.26) | copy-start | bytes 12292
  96.6 6.1 %copy-start.16 = (bf16[2048,1024]{1,0:T(8,128)(2,1)S(1)}, bf16[2048,1024]{1,0:T(8,128)(2,1)}, u32[]{:S(2)}) copy-start(bf16[2048,1024]{1,0:T(8,128)(2,1)} %param.25) | copy-start | bytes 12582916
  96.6 6.1 %copy-start.21 = (bf16[1024,1024]{0,1:T(8,128)(2,1)S(1)}, bf16[1024,1024]{0,1:T(8,128)(2,1)}, u32[]{:S(2)}) copy-start(bf16[1024,1024]{0,1:T(8,128)(2,1)} %copy-done.20) | copy-start | bytes 6291460
  102.7 6.2 %copy-start.25 = (bf16[1024,1024]{0,1:T(8,128)(2,1)}, bf16[1024,1024]{0,1:T(8,128)(2,1)S(1)}, u32[]{:S(2)}) copy-start(bf16[1024,1024]{0,1:T(8,128)(2,1)S(1)} %divide_convert_fusion) | copy-start | bytes 6291460
  113.5 1.3 copy-start.8
  119.5 41.3 %copy-start.23 = (f32[1024,2048]{0,1:T(8,128)}, f32[1024,2048]{0,1:T(8,128)S(1)}, u32[]{:S(2)}) copy-start(f32[1024,2048]{0,1:T(8,128)S(1)} %fusion.33) | copy-start | bytes 25165828
  160.7 2.7 copy-start.9
  163.5 7.2 %copy-start.11 = (s32[512]{0:T(512)S(1)}, s32[512]{0:T(512)}, u32[]{:S(2)}) copy-start(s32[512]{0:T(512)} %param.20) | copy-start | bytes 6148
  164.6 31.4 %all-to-all-start.1 = ((bf16[8,64,1024]{2,1,0:T(8,128)(2,1)}), bf16[8,64,1024]{2,1,0:T(8,128)(2,1)S(1)}, u32[]{:S(2)}, u32[]{:S(2)}) async-start(bf16[8,64,1024]{2,1,0:T(8,128)(2,1)} %bitcast.59), calls=%async_computation.1 | async-start | bytes 2097152 | tf_op jit(solution)/shard_map/all_to_all | solution.py:112
  170.6 301.7 %all-reduce.5.cloned.1.call-start = ((), (), s32[]{:S(2)}) async-start(), calls=%async_computation.2 | async-start | bytes 29360128 | tf_op jit(solution)/shard_map/psum | solution.py:136
  196.4 2.7 copy-start.3
  196.4 4.1 slice-start
  199.1 1.4 copy-start.19
  199.1 2.2 copy-start.24
  199.1 2.8 slice-start.1
  201.9 3.0 copy-start.22
  209.2 6.1 %copy-start.6 = (bf16[1024,1024]{1,0:T(8,128)(2,1)S(1)}, bf16[1024,1024]{1,0:T(8,128)(2,1)}, u32[]{:S(2)}) copy-start(bf16[1024,1024]{1,0:T(8,128)(2,1)} %param.16) | copy-start | bytes 6291460
  209.3 6.1 %copy-start.14 = (pred[1024]{0:T(1024)(128)(4,1)S(1)}, pred[1024]{0:T(1024)(128)(4,1)}, u32[]{:S(2)}) copy-start(pred[1024]{0:T(1024)(128)(4,1)} %copy-done.13) | copy-start | bytes 3076
  214.0 1.3 copy-start.4
  217.9 3.3 copy-start.5
  475.2 6.2 %copy-start.2 = (f32[2048,1024]{1,0:T(8,128)S(1)}, f32[2048,1024]{1,0:T(8,128)}, u32[]{:S(2)}) copy-start(f32[2048,1024]{1,0:T(8,128)} %get-tuple-element.210) | copy-start | bytes 25165828
Sparse Core Ops, SparseCore 0:
  218.0 254.2 all-reduce.4
where the time goes:
time: 497 us; the launch traced here: 492 us
  waiting for transfers between devices  216 us (43%)
  matrix products  109 us (22%)
  other arithmetic  55.7 us (11%)
  local copies, waits for them, and re-layouts  42.7 us (9%)
  blocking collectives  39.7 us (8%)
  between operations  15.5 us (3%)
  starting transfers between devices  13.5 us (3%)
    psum x1, waiting for transfers between devices, per_device(): lax.psum((grad_proj, grad_q, grad_q_bias, grad_w, grad_w_bias), ('dom', '...  203 us
    reduce_sum x4, other arithmetic, build_one_block(): return jnp.sum(jnp.where(match, weight[:, :, None], 0.0), axis=1)  44.3 us
    dot_general x1, matrix products, per_device(): lax.dot_general(adjacency, dagg, (((0,), (0,)), ((), ())), precision=lax....  41.2 us
    psum x1, blocking collectives, per_device(): lax.psum((grad_proj, grad_q, grad_q_bias, grad_w, grad_w_bias), ('dom', '...  39.7 us
    unnamed x61, local copies, waits for them, and re-layouts  28.7 us
    dot_general x6, matrix products, contract_rows(): lax.dot_general(left, right, (((0,), (0,)), ((), ())), preferred_element_...  24.5 us
    all_to_all x1, waiting for transfers between devices, per_device(): lax.all_to_all(dtable[rows:].astype(jnp.bfloat16), 'dom', split_axis=0, c...  12.8 us
    dot_general x3, matrix products, contract_cols(): lax.dot_general(left, right, (((1,), (1,)), ((), ())), preferred_element_...  12.7 us
  transfers between devices with their start and end apart: 3, of which 2 were waited for; matrix products, arithmetic and copies ran while one was open for 16% of the time, Pallas kernels for 0%

commit v1 on v0

--- a/solution.py
+++ b/solution.py
@@ -3,6 +3,9 @@
 from jax import lax
 from jax.sharding import PartitionSpec as P
 
+F32 = jnp.float32
+BF16 = jnp.bfloat16
+
 
 def contract_rows(left, right):
     return lax.dot_general(
@@ -19,6 +22,87 @@
 def silu_slope(value):
     sigma = jax.nn.sigmoid(value)
     return sigma * (1.0 + value * (1.0 - sigma))
+
+
+def swap(value, axis, mask):
+    size = lax.axis_size(axis)
+    return lax.ppermute(value, axis, [(s, s ^ mask) for s in range(size)])
+
+
+def bit_of(axis, mask):
+    return (lax.axis_index(axis) // mask) % 2
+
+
+def pack_bias(bias):
+    high = bias.astype(BF16)
+    low = (bias - high.astype(F32)).astype(BF16)
+    return jnp.concatenate([high[None], low[None], jnp.zeros((14,) + bias.shape, BF16)], axis=0)
+
+
+def read_bias(packed):
+    return packed[0].astype(F32) + packed[1].astype(F32)
+
+
+def halve(value, bias, axis, mask):
+    half = value.shape[0] // 2
+    bit = bit_of(axis, mask)
+    keep = lax.dynamic_slice_in_dim(value, bit * half, half)
+    send = lax.dynamic_slice_in_dim(value, (1 - bit) * half, half).astype(BF16)
+    got = swap(send if bias is None else jnp.concatenate([send, bias], axis=0), axis, mask)
+    total = keep + got[:half].astype(F32)
+    if bias is None:
+        return total, None
+    return total, pack_bias(read_bias(bias) + read_bias(got[half:]))
+
+
+def double(value, axis, mask):
+    got = swap(value, axis, mask)
+    bit = bit_of(axis, mask)
+    return jnp.where(
+        bit == 0, jnp.concatenate([value, got], axis=0), jnp.concatenate([got, value], axis=0)
+    )
+
+
+def all_sum(value, bias):
+    rows, columns = value.shape
+    bias = pack_bias(bias)
+    value, bias = halve(value, bias, "rep", 1)
+    first, second = jnp.split(value, 2, axis=0)
+    first, bias = halve(first, bias, "dom", 1)
+    second, _ = halve(second, None, "rep", 2)
+    first, bias = halve(first, bias, "rep", 2)
+    second, _ = halve(second, None, "dom", 1)
+    part = first.shape[0] // 4
+    block = jnp.stack(
+        [first.reshape(4, part, columns), second.reshape(4, part, columns)], axis=1
+    ).reshape(4, 2 * part, columns)
+    mine = lax.axis_index("dom") // 2 % 4
+    total = lax.dynamic_index_in_dim(block, mine, 0, keepdims=False)
+    sums = [read_bias(bias)]
+    for step in (1, 2, 3):
+        send = lax.dynamic_index_in_dim(block, mine ^ step, 0, keepdims=False).astype(BF16)
+        got = swap(jnp.concatenate([send, bias], axis=0), "dom", 2 * step)
+        total = total + got[: 2 * part].astype(F32)
+        sums.append(read_bias(got[2 * part :]))
+    bias_sum = (sums[0] + sums[1]) + (sums[2] + sums[3])
+    mask = 8
+    while mask < lax.axis_size("dom"):
+        total = total.astype(BF16).astype(F32)
+        total = total + swap(total, "dom", mask)
+        bias_sum = bias_sum + swap(bias_sum, "dom", mask)
+        mask *= 2
+    total = total.astype(BF16)
+    gathered = jnp.zeros((4, 2 * part, columns), BF16)
+    gathered = lax.dynamic_update_index_in_dim(gathered, total, mine, 0)
+    for step in (1, 2, 3):
+        got = swap(total, "dom", 2 * step)
+        gathered = lax.dynamic_update_index_in_dim(gathered, got, mine ^ step, 0)
+    gathered = gathered.reshape(4, 2, part, columns)
+    first = double(gathered[:, 0].reshape(4 * part, columns), "rep", 2)
+    second = double(gathered[:, 1].reshape(4 * part, columns), "dom", 1)
+    first = double(first, "dom", 1)
+    second = double(second, "rep", 2)
+    return double(jnp.concatenate([first, second], axis=0), "rep", 1).astype(F32), bias_sum
 
 
 def build_adjacency(neighbours, importance, columns):
@@ -42,15 +126,8 @@
 
 
 def send_table(send_rows, rows):
-    halo = send_rows.shape[0]
-    block = min(256, halo)
     row_ids = lax.iota(jnp.int32, rows)
-
-    def send_one_block(index):
-        return (index[:, None] == row_ids[None, :]).astype(jnp.bfloat16)
-
-    blocks = lax.map(send_one_block, send_rows.reshape(halo // block, block))
-    return blocks.reshape(halo, rows)
+    return (send_rows[:, None] == row_ids[None, :]).astype(BF16)
 
 
 def per_device(
@@ -77,16 +154,15 @@
     hidden = jnp.where(board, projected, features.astype(jnp.float32)).astype(jnp.bfloat16)
     pre = jnp.dot(hidden, q_weight, preferred_element_type=jnp.float32) + q_bias
     active = jax.nn.silu(pre).astype(jnp.bfloat16)
-    incoming = lax.all_to_all(active[send_rows], "dom", split_axis=0, concat_axis=0, tiled=True)
+    onehot = send_table(send_rows, rows)
+    outgoing = jnp.dot(onehot, active, preferred_element_type=F32).astype(BF16)
+    incoming = lax.all_to_all(outgoing, "dom", split_axis=0, concat_axis=0, tiled=True)
     table = jnp.concatenate([active, incoming], axis=0)
     columns = table.shape[0]
-    total = jnp.sum(importance, axis=1, keepdims=True)
-    adjacency = build_adjacency(neighbours, importance, columns)
-    upper = adjacency.astype(jnp.bfloat16)
-    lower = (adjacency - upper.astype(jnp.float32)).astype(jnp.bfloat16)
-    agg = jnp.dot(upper, table, preferred_element_type=jnp.float32) + jnp.dot(
-        lower, table, preferred_element_type=jnp.float32
-    )
+    weights = importance.astype(BF16).astype(F32)
+    total = jnp.sum(weights, axis=1, keepdims=True)
+    adjacency = build_adjacency(neighbours, weights, columns).astype(BF16)
+    agg = jnp.dot(adjacency, table, preferred_element_type=jnp.float32)
     mean = agg / total
     joined = jnp.concatenate([hidden, mean.astype(jnp.bfloat16)], axis=1)
     pre2 = jnp.dot(joined, w_weight, preferred_element_type=jnp.float32) + w_bias
@@ -101,27 +177,13 @@
     grad_w = contract_rows(joined, dpre2)
     grad_w_bias = jnp.sum(dpre2.astype(jnp.float32), axis=0)
     djoined = contract_cols(dpre2, w_weight)
-    dagg = djoined[:, width:] / total
-    dtable = lax.dot_general(
-        adjacency,
-        dagg,
-        (((0,), (0,)), ((), ())),
-        precision=lax.Precision.HIGHEST,
-        preferred_element_type=jnp.float32,
-    )
+    dagg = (djoined[:, width:] / total).astype(BF16)
+    dtable = contract_rows(adjacency, dagg)
     returned = lax.all_to_all(
         dtable[rows:].astype(jnp.bfloat16), "dom", split_axis=0, concat_axis=0, tiled=True
-    ).astype(jnp.float32)
-    onehot = send_table(send_rows, rows)
-    high_part = returned.astype(jnp.bfloat16)
-    rest = returned - high_part.astype(jnp.float32)
-    middle_part = rest.astype(jnp.bfloat16)
-    low_part = (rest - middle_part.astype(jnp.float32)).astype(jnp.bfloat16)
-    owned = (
-        contract_rows(onehot, high_part)
-        + contract_rows(onehot, middle_part)
-        + contract_rows(onehot, low_part)
-    )
+    )
+    grad_w, grad_w_bias = all_sum(grad_w, grad_w_bias)
+    owned = contract_rows(onehot, returned)
     dactive = dtable[:rows] + owned
     dpre = (dactive * silu_slope(pre)).astype(jnp.bfloat16)
     grad_q = contract_rows(hidden, dpre)
@@ -133,8 +195,8 @@
     )
     grad_features = jnp.where(board, board_full, dhidden.astype(jnp.float32))
     grad_proj = contract_rows(lowered, jnp.where(board, dhidden, jnp.zeros_like(dhidden)))
-    summed = lax.psum((grad_proj, grad_q, grad_q_bias, grad_w, grad_w_bias), ("dom", "rep"))
-    return (embedding, grad_features, summed[0], summed[1], summed[2], summed[3], summed[4])
+    late, grad_q_bias = all_sum(jnp.concatenate([grad_q, grad_proj], axis=0), grad_q_bias)
+    return (embedding, grad_features, late[width:], late[:width], grad_q_bias, grad_w, grad_w_bias)
 
 
 def solution(mesh):

time: 497 us -> 315 us (0.63)
  waiting for transfers between devices: 216 us -> 65.7 us
  matrix products: 109 us -> 53.2 us
  blocking collectives: 39.7 us -> 0 us
  starting transfers between devices: 13.5 us -> 51.5 us
  other arithmetic: 55.7 us -> 88.7 us
  between operations: 15.5 us -> 2.84 us
    psum x1 -> x0, waiting for transfers between devices: 203 us -> none  [per_device(): lax.psum((grad_proj, grad_q, grad_q_bias, grad_w, grad_w_bias), ('dom', '...]
    ppermute x0 -> x32, waiting for transfers between devices: none -> 63.9 us  [swap(): return lax.ppermute(value, axis, [(s, s ^ mask) for s in range(size)])]
    dot_general x3 -> x2, matrix products: 56.3 us -> 8.43 us  [the longest x1 6.14 us: per_device(): agg = jnp.dot(adjacency, table, preferred_element_type=jnp.float32)]
    psum x1 -> x0, blocking collectives: 39.7 us -> none  [per_device(): lax.psum((grad_proj, grad_q, grad_q_bias, grad_w, grad_w_bias), ('dom', '...]
    ppermute x0 -> x32, starting transfers between devices: none -> 37.8 us  [swap(): return lax.ppermute(value, axis, [(s, s ^ mask) for s in range(size)])]
    convert_element_type x1 -> x20, other arithmetic: 0.3 us -> 14.6 us  [the longest x2 7.46 us: all_sum(): double(jnp.concatenate([first, second], axis=0), 'rep', 1).astype(F32)]
    add x0 -> x16, other arithmetic: none -> 11.6 us  [the longest x10 7.13 us: halve(): total = keep + got[:half].astype(F32)]
    concatenate x0 -> x1, local copies, waits for them, and re-layouts: none -> 11.5 us  [halve(): jnp.concatenate([send, bias], axis=0)]
  transfers between devices with their start and end apart: 3 -> 34, of which waited for: 2 -> 18; matrix products, arithmetic and copies ran while one was open for 16% -> 41% of each run, Pallas kernels for 0% -> 0%
where the time goes in v1:
time: 315 us; the launch traced here: 309 us
  other arithmetic  88.7 us (28%)
  waiting for transfers between devices  65.7 us (21%)
  matrix products  53.2 us (17%)
  starting transfers between devices  51.5 us (16%)
  local copies, waits for them, and re-layouts  47 us (15%)
    ppermute x32, waiting for transfers between devices, swap(): return lax.ppermute(value, axis, [(s, s ^ mask) for s in range(size)])  63.9 us
    reduce_sum x4, other arithmetic, build_one_block(): return jnp.sum(jnp.where(match, weight[:, :, None], 0.0), axis=1)  44.7 us
    ppermute x32, starting transfers between devices, swap(): return lax.ppermute(value, axis, [(s, s ^ mask) for s in range(size)])  37.8 us
    dot_general x5, matrix products, contract_rows(): lax.dot_general(left, right, (((0,), (0,)), ((), ())), preferred_element_...  19.5 us
    unnamed x88, local copies, waits for them, and re-layouts  17.9 us
    concatenate x1, local copies, waits for them, and re-layouts, halve(): jnp.concatenate([send, bias], axis=0)  11.5 us
    dot_general x3, matrix products, contract_cols(): lax.dot_general(left, right, (((1,), (1,)), ((), ())), preferred_element_...  10.7 us
    all_to_all x1, starting transfers between devices, per_device(): lax.all_to_all(outgoing, 'dom', split_axis=0, concat_axis=0, tiled=True)  7.73 us
  transfers between devices with their start and end apart: 34, of which 18 were waited for; matrix products, arithmetic and copies ran while one was open for 41% of the time, Pallas kernels for 0%

profile of v1, /device:TPU:0, one launch (start us, length us, event | category | flops | bytes accessed | tf_op | source)
XLA Modules:
  0.0 309.2 jit_solution(10555075933219620335)
XLA Ops:
  0.7 4.1 %copy.52 = bf16[1024,1024]{0,1:T(8,128)(2,1)} copy(bf16[1024,1024]{1,0:T(8,128)(2,1)} %param.14) | data formatting | bytes 4194304 | tf_op args[0]
  4.8 3.2 %select_convert_fusion = bf16[1024,1024]{0,1:T(8,128)(2,1)S(1)} fusion(bf16[1024,1024]{0,1:T(8,128)(2,1)} %copy.52, bf16[512,1024]{1,0:T(8,128)(2,1)S(1)} %copy-done.29, pred[1024]{0:T(1024)(128)(4,1)S(1)} %broadcast_compare_fusion, bf16[1024,1024]{1,0:T(8,128)(2,1)} %param.14), kind=kOutput, calls=%fused_computation.37 | convolution fusion | flops 1076887552 | bytes 6292480 | tf_op jit(solution)/shard_map/dot_general | solution.py:153
  8.1 5.0 %multiply_convert_fusion.1 = (bf16[1024,1024]{1,0:T(8,128)(2,1)S(1)}, f32[1024,1024]{1,0:T(8,128)}) fusion(f32[1024]{0:T(1024)S(1)} %copy-done.31, bf16[1024,1024]{0,1:T(8,128)(2,1)S(1)} %select_convert_fusion, bf16[1024,1024]{1,0:T(8,128)(2,1)S(1)} %copy-done), kind=kOutput, calls=%fused_computation.35 | convolution fusion | flops 2153775104 | bytes 10489856 | tf_op jit(solution)/shard_map/dot_general | solution.py:155
  13.1 2.3 fusion.31
  15.4 7.7 %all-to-all-start = ((bf16[8,64,1024]{2,1,0:T(8,128)(2,1)}), bf16[8,64,1024]{2,1,0:T(8,128)(2,1)S(1)}, u32[]{:S(2)}, u32[]{:S(2)}) async-start(bf16[8,64,1024]{2,1,0:T(8,128)(2,1)} %bitcast.138), calls=%async_computation | async-start | bytes 2097152 | tf_op jit(solution)/shard_map/all_to_all | solution.py:159
  26.6 49.0 %while.11 = (s32[]{:T(128)}, bf16[4,256,1536]{2,1,0:T(8,128)(2,1)}, s32[4,256,50]{1,0,2:T(4,128)S(1)}, f32[4,256,50]{1,0,2:T(4,128)S(1)}, s32[]{:T(128)}) while((s32[]{:T(128)}, bf16[4,256,1536]{2,1,0:T(8,128)(2,1)}, s32[4,256,50]{1,0,2:T(4,128)S(1)}, f32[4,256,50]{1,0,2:T(4,128)S(1)}, s32[]{:T(128)}) %tuple.62), condition=%wide.region_2.3_spmd.clone, body=%wide.region_0.2_spmd.clone.sunk | while | flops 58589184 | bytes 2871377 | solution.py:118
  26.7 11.2 %select_reduce_fusion.2 = bf16[256,1536]{1,0:T(8,128)(2,1)S(1)} fusion(f32[256,50]{0,1:T(8,128)S(1)} %bitcast.122, s32[256,50]{0,1:T(8,128)S(1)} %bitcast.123), kind=kLoop, calls=%fused_computation.2.clone.1 | loop fusion | flops 58589184 | bytes 888832 | tf_op jit(solution)/shard_map/while/body/eval_jaxpr/reduce_sum | solution.py:116
  39.0 11.2 %select_reduce_fusion.2 = bf16[256,1536]{1,0:T(8,128)(2,1)S(1)} fusion(f32[256,50]{0,1:T(8,128)S(1)} %bitcast.122, s32[256,50]{0,1:T(8,128)S(1)} %bitcast.123), kind=kLoop, calls=%fused_computation.2.clone.1 | loop fusion | flops 58589184 | bytes 888832 | tf_op jit(solution)/shard_map/while/body/eval_jaxpr/reduce_sum | solution.py:116
  51.2 11.2 %select_reduce_fusion.2 = bf16[256,1536]{1,0:T(8,128)(2,1)S(1)} fusion(f32[256,50]{0,1:T(8,128)S(1)} %bitcast.122, s32[256,50]{0,1:T(8,128)S(1)} %bitcast.123), kind=kLoop, calls=%fused_computation.2.clone.1 | loop fusion | flops 58589184 | bytes 888832 | tf_op jit(solution)/shard_map/while/body/eval_jaxpr/reduce_sum | solution.py:116
  63.5 11.2 %select_reduce_fusion.2 = bf16[256,1536]{1,0:T(8,128)(2,1)S(1)} fusion(f32[256,50]{0,1:T(8,128)S(1)} %bitcast.122, s32[256,50]{0,1:T(8,128)S(1)} %bitcast.123), kind=kLoop, calls=%fused_computation.2.clone.1 | loop fusion | flops 58589184 | bytes 888832 | tf_op jit(solution)/shard_map/while/body/eval_jaxpr/reduce_sum | solution.py:116
  76.3 6.1 %divide_convert_fusion = bf16[1024,1024]{0,1:T(8,128)(2,1)S(1)} fusion(f32[1024]{0:T(1024)} %get-tuple-element.125, bf16[1024,1536]{1,0:T(8,128)(2,1)} %bitcast.163, bf16[512,1024]{1,0:T(8,128)(2,1)S(1)} %bitcast.137, bf16[1024,1024]{1,0:T(8,128)(2,1)} %copy-done.39), kind=kOutput, calls=%fused_computation.34 | convolution fusion | flops 3229614080 | bytes 8392704 | tf_op jit(solution)/shard_map/dot_general | solution.py:165
  82.5 6.3 %multiply_reduce_fusion = (f32[1024]{0:T(1024)S(1)}, f32[1024]{0:T(1024)S(1)}, f32[1024,1024]{1,0:T(8,128)S(1)}) fusion(bf16[1024,1024]{1,0:T(8,128)(2,1)S(1)} %copy-done.10, pred[1024]{0:T(1024)(128)(4,1)S(1)} %iota_compare_fusion.6, f32[1024]{0:T(1024)S(1)} %copy-done.21, bf16[2048,1024]{1,0:T(8,128)(2,1)S(1)} %copy-done.27, ...), kind=kOutput, calls=%fused_computation.28 | convolution fusion | flops 4314888192 | bytes 14693376 | tf_op jit(solution)/shard_map/dot_general | solution.py:168
  88.9 4.8 %convert_reduce_fusion = (f32[1024]{0:T(1024)S(1)}, bf16[1024,1024]{1,0:T(8,128)(2,1)S(1)}, f32[1024,1024]{1,0:T(8,128)}) fusion(f32[1024]{0:T(1024)S(1)} %get-tuple-element.77, f32[1024]{0:T(1024)S(1)} %get-tuple-element.132, f32[1024,1024]{1,0:T(8,128)S(1)} %get-tuple-element.136, f32[1024]{0:T(1024)S(1)} %copy-done.21, ...), kind=kLoop, calls=%fused_computation.23 | loop fusion | flops 22019072 | bytes 12604416 | tf_op jit(solution)/shard_map/reduce_sum | solution.py:178
  93.7 4.6 %fusion.104 = f32[1024,2048]{0,1:T(8,128)S(1)} fusion(bf16[1024,1024]{1,0:T(8,128)(2,1)S(1)} %get-tuple-element.98, bf16[2048,1024]{1,0:T(8,128)(2,1)S(1)} %copy-done.27), kind=kOutput, calls=%fused_computation.250 | convolution fusion | flops 4294967296 | bytes 14680064 | tf_op jit(solution)/shard_map/dot_general | solution.py:17
  98.3 3.6 %fusion.19 = f32[1536,1024]{1,0:T(8,128)S(1)} fusion(bf16[1024,1536]{1,0:T(8,128)(2,1)S(1)} %bitcast.164, f32[1024,2048]{0,1:T(8,128)S(1)} %fusion.104, f32[1024]{0:T(1024)S(1)} %copy-done.22), kind=kOutput, calls=%fused_computation.50 | convolution fusion | flops 3223322624 | bytes 13635584 | tf_op jit(solution)/shard_map/dot_general | solution.py:11
  101.9 2.7 copy-done.13
  105.8 6.0 %all-to-all-start.1 = ((bf16[8,64,1024]{2,1,0:T(8,128)(2,1)}), bf16[8,64,1024]{2,1,0:T(8,128)(2,1)S(1)}, u32[]{:S(2)}, u32[]{:S(2)}) async-start(bf16[8,64,1024]{2,1,0:T(8,128)(2,1)} %bitcast.4), calls=%async_computation.1 | async-start | bytes 2097152 | tf_op jit(solution)/shard_map/all_to_all | solution.py:182
  111.8 7.1 %fusion.17 = f32[2048,1024]{1,0:T(8,128)S(1)} fusion(bf16[1024,1024]{1,0:T(8,128)(2,1)} %copy-done.11, bf16[1024,1024]{0,1:T(8,128)(2,1)} %copy-done.40, bf16[1024,1024]{0,1:T(8,128)(2,1)} %copy-done.35), kind=kOutput, calls=%fused_computation.48 | convolution fusion | flops 4303355904 | bytes 14680064 | tf_op jit(solution)/shard_map/dot_general | solution.py:11
  118.9 3.4 %copy-done.5 = f32[2048,1024]{1,0:T(8,128)} copy-done((f32[2048,1024]{1,0:T(8,128)}, f32[2048,1024]{1,0:T(8,128)S(1)}, u32[]{:S(2)}) %copy-start.5) | copy-done | bytes 8388632
  123.9 11.5 %concatenate.147 = bf16[1040,1024]{1,0:T(8,128)(2,1)} concatenate(bf16[1024,1024]{1,0:T(8,128)(2,1)} %dynamic-slice_convert_fusion, bf16[1,1024]{1,0:T(2,128)(2,1)S(1)} %convert_element_type.769, bf16[1,1024]{1,0:T(2,128)(2,1)S(1)} %subtract_convert_fusion.3, bf16[14,1024]{1,0:T(8,128)(2,1)S(1)} %broadcast.36), dimensions={0} | concatenate | bytes 4259840 | tf_op jit(solution)/shard_map/concatenate | solution.py:51
  135.4 1.8 all-to-all-done.1
  137.2 5.2 %convert_reduce_fusion.1 = (f32[1024]{0:T(1024)S(1)}, bf16[1024,1024]{1,0:T(8,128)(2,1)S(1)}) fusion(f32[1024,1024]{1,0:T(8,128)} %get-tuple-element.135, f32[1024]{0:T(1024)S(1)} %copy-done.32, bf16[512,1024]{1,0:T(8,128)(2,1)S(1)} %bitcast.136, s32[512]{0:T(512)S(1)} %copy-done.34, f32[1536,1024]{1,0:T(8,128)} %copy-done.13), kind=kOutput, calls=%fused_computation.25 | convolution fusion | flops 1087896576 | bytes 11544576 | tf_op jit(solution)/shard_map/dot_general | solution.py:11
  142.5 4.8 %fusion.2 = bf16[1024,1024]{0,1:T(8,128)(2,1)S(1)} fusion(f32[1024,2048]{0,1:T(8,128)} %copy-done.38, bf16[1024,1024]{1,0:T(8,128)(2,1)S(1)} %get-tuple-element.138, bf16[1024,1024]{1,0:T(8,128)(2,1)S(1)} %copy-done), kind=kOutput, calls=%fused_computation.13 | convolution fusion | flops 2149580800 | bytes 10485760 | tf_op jit(solution)/shard_map/dot_general | solution.py:17
  149.6 2.3 fusion.105
  152.0 2.0 fusion.92
  154.0 2.6 convert_add_fusion
  161.5 8.4 %collective-permute-done.19 = bf16[256,1024]{1,0:T(8,128)(2,1)S(1)} collective-permute-done((bf16[256,1024]{1,0:T(8,128)(2,1)S(1)}, bf16[256,1024]{1,0:T(8,128)(2,1)S(1)}, u32[]{:S(2)}, u32[]{:S(2)}) %collective-permute-start.19) | collective-permute-done | bytes 524320 | tf_op jit(solution)/shard_map/ppermute | solution.py:29
  170.1 2.1 collective-permute-start.20
  175.9 2.0 collective-permute-done.20
  178.0 2.5 collective-permute-done.18
  181.5 4.5 %collective-permute-start.23 = (bf16[80,1024]{1,0:T(8,128)(2,1)}, bf16[80,1024]{1,0:T(8,128)(2,1)}, u32[]{:S(2)}, u32[]{:S(2)}) collective-permute-start(bf16[80,1024]{1,0:T(8,128)(2,1)} %get-tuple-element.128), channel_id=1, source_target_pairs={{0,24},{4,28},{8,16},{12,20},{16,8},{20,12},{24,0},{28,4},{1,25},{... | collective-permute-start | bytes 491528 | tf_op jit(solution)/shard_map/ppermute | solution.py:29
  186.6 4.9 %collective-permute-done.23 = bf16[80,1024]{1,0:T(8,128)(2,1)} collective-permute-done((bf16[80,1024]{1,0:T(8,128)(2,1)}, bf16[80,1024]{1,0:T(8,128)(2,1)}, u32[]{:S(2)}, u32[]{:S(2)}) %collective-permute-start.23) | collective-permute-done | bytes 163872 | tf_op jit(solution)/shard_map/ppermute | solution.py:29
  191.4 7.6 %collective-permute-done.22 = bf16[80,1024]{1,0:T(8,128)(2,1)} collective-permute-done((bf16[80,1024]{1,0:T(8,128)(2,1)S(1)}, bf16[80,1024]{1,0:T(8,128)(2,1)}, u32[]{:S(2)}, u32[]{:S(2)}) %collective-permute-start.22) | collective-permute-done | bytes 163872 | tf_op jit(solution)/shard_map/ppermute | solution.py:29
  201.0 2.9 collective-permute-start.25
  205.4 2.2 collective-permute-done.24
  208.3 5.4 %collective-permute-done.25 = bf16[64,1024]{1,0:T(8,128)(2,1)S(1)} collective-permute-done((bf16[64,1024]{1,0:T(8,128)(2,1)S(1)}, bf16[64,1024]{1,0:T(8,128)(2,1)S(1)}, u32[]{:S(2)}, u32[]{:S(2)}) %collective-permute-start.25) | collective-permute-done | bytes 131104 | tf_op jit(solution)/shard_map/ppermute | solution.py:29
  218.2 3.5 %fusion.11 = f32[768,1024]{1,0:T(8,128)S(1)} fusion(s32[]{:T(128)S(6)} %select_n.276, f32[1024,1024]{1,0:T(8,128)} %copy-done.1, f32[512,1024]{1,0:T(8,128)} %copy-done.4, bf16[784,1024]{1,0:T(8,128)(2,1)} %collective-permute-done), kind=kLoop, calls=%fused_computation.41 | loop fusion | flops 2359296 | bytes 11010052 | tf_op jit(solution)/shard_map/add | solution.py:52
  227.1 8.1 %collective-permute-done.3 = bf16[192,1024]{1,0:T(8,128)(2,1)S(1)} collective-permute-done((bf16[192,1024]{1,0:T(8,128)(2,1)S(1)}, bf16[192,1024]{1,0:T(8,128)(2,1)S(1)}, u32[]{:S(2)}, u32[]{:S(2)}) %collective-permute-start.3) | collective-permute-done | bytes 393248 | tf_op jit(solution)/shard_map/ppermute | solution.py:29
  238.3 2.8 collective-permute-done.4
  241.1 6.8 %collective-permute-done.2 = bf16[112,1024]{1,0:T(8,128)(2,1)S(1)} collective-permute-done((bf16[112,1024]{1,0:T(8,128)(2,1)S(1)}, bf16[112,1024]{1,0:T(8,128)(2,1)S(1)}, u32[]{:S(2)}, u32[]{:S(2)}) %collective-permute-start.2) | collective-permute-done | bytes 229408 | tf_op jit(solution)/shard_map/ppermute | solution.py:29
  249.1 2.6 collective-permute-start.6
  256.0 4.5 %collective-permute-done.6 = bf16[64,1024]{1,0:T(8,128)(2,1)S(1)} collective-permute-done((bf16[64,1024]{1,0:T(8,128)(2,1)S(1)}, bf16[64,1024]{1,0:T(8,128)(2,1)S(1)}, u32[]{:S(2)}, u32[]{:S(2)}) %collective-permute-start.6) | collective-permute-done | bytes 131104 | tf_op jit(solution)/shard_map/ppermute | solution.py:29
  263.1 2.6 collective-permute-start.10
  266.1 5.3 %collective-permute-done.9 = bf16[48,1024]{1,0:T(8,128)(2,1)S(1)} collective-permute-done((bf16[48,1024]{1,0:T(8,128)(2,1)S(1)}, bf16[48,1024]{1,0:T(8,128)(2,1)S(1)}, u32[]{:S(2)}, u32[]{:S(2)}) %collective-permute-start.9) | collective-permute-done | bytes 98336 | tf_op jit(solution)/shard_map/ppermute | solution.py:29
  281.2 2.6 convert_select_fusion
  283.8 5.3 %copy.64 = f32[1024,1024]{1,0:T(8,128)} copy(f32[1024,1024]{0,1:T(8,128)} %convert_select_fusion) | data formatting | bytes 8388608
  297.1 5.9 %fusion.6 = f32[2048,1024]{1,0:T(8,128)} fusion(bf16[1024,1024]{1,0:T(8,128)(2,1)} %collective-permute-done.31, bf16[512,1024]{1,0:T(8,128)(2,1)S(1)} %maximum_select_fusion.3, bf16[512,1024]{1,0:T(8,128)(2,1)S(1)} %copy-done.3, pred[]{:T(512)S(6)} %eq.78), kind=kLoop, calls=%fused_computation.21 | loop fusion | flops 29360128 | bytes 12582913 | tf_op jit(solution)/shard_map/convert_element_type | solution.py:105
  306.2 2.6 slice.244
  (240 shorter events, 69.1 us)
Async XLA Ops:
  0.6 7.4 %copy-start = (bf16[1024,1024]{1,0:T(8,128)(2,1)S(1)}, bf16[1024,1024]{1,0:T(8,128)(2,1)}, u32[]{:S(2)}) copy-start(bf16[1024,1024]{1,0:T(8,128)(2,1)} %param.21) | copy-start | bytes 6291460
  13.1 10.0 %copy-start.12 = (f32[1024,50]{0,1:T(8,128)S(1)}, f32[1024,50]{0,1:T(8,128)}, u32[]{:S(2)}) copy-start(f32[1024,50]{0,1:T(8,128)} %param.17) | copy-start | bytes 614404
  15.4 60.8 %all-to-all-start = ((bf16[8,64,1024]{2,1,0:T(8,128)(2,1)}), bf16[8,64,1024]{2,1,0:T(8,128)(2,1)S(1)}, u32[]{:S(2)}, u32[]{:S(2)}) async-start(bf16[8,64,1024]{2,1,0:T(8,128)(2,1)} %bitcast.138), calls=%async_computation | async-start | bytes 2097152 | tf_op jit(solution)/shard_map/all_to_all | solution.py:159
  105.8 31.4 %all-to-all-start.1 = ((bf16[8,64,1024]{2,1,0:T(8,128)(2,1)}), bf16[8,64,1024]{2,1,0:T(8,128)(2,1)S(1)}, u32[]{:S(2)}, u32[]{:S(2)}) async-start(bf16[8,64,1024]{2,1,0:T(8,128)(2,1)} %bitcast.4), calls=%async_computation.1 | async-start | bytes 2097152 | tf_op jit(solution)/shard_map/all_to_all | solution.py:182
  123.9 13.3 %copy-start.32 = (f32[1024]{0:T(1024)S(1)}, f32[1024]{0:T(1024)}, u32[]{:S(2)}) copy-start(f32[1024]{0:T(1024)} %param.22) | copy-start | bytes 12292
  123.9 13.3 %copy-start.34 = (s32[512]{0:T(512)S(1)}, s32[512]{0:T(512)}, u32[]{:S(2)}) copy-start(s32[512]{0:T(512)} %param.18) | copy-start | bytes 6148
  135.4 16.6 %collective-permute-start.16 = (bf16[1040,1024]{1,0:T(8,128)(2,1)}, bf16[1040,1024]{1,0:T(8,128)(2,1)}, u32[]{:S(2)}, u32[]{:S(2)}) collective-permute-start(bf16[1040,1024]{1,0:T(8,128)(2,1)} %concatenate.147), channel_id=1, source_target_pairs={{0,1},{1,0},{2,3},{3,2},{4,5},{5,4},{6,7},{7,6},{8,9},{9,8},{10,11... | collective-permute-start | bytes 6389768 | tf_op jit(solution)/shard_map/ppermute | solution.py:29
  147.3 6.7 %slice-start = ((s8[8388608]{0:T(1024)(128)(4,1)}), s8[4194304]{0:T(1024)(128)(4,1)S(1)}, s32[]{:S(2)}) async-start(s8[8388608]{0:T(1024)(128)(4,1)} %bitcast.124), calls=%async_computation.2 | async-start | bytes 8388608
  149.6 10.6 %copy-start.4 = (f32[512,1024]{1,0:T(8,128)}, f32[512,1024]{1,0:T(8,128)S(1)}, u32[]{:S(2)}) copy-start(f32[512,1024]{1,0:T(8,128)S(1)} %fusion.28) | copy-start | bytes 6291460
  152.0 8.3 %copy-start.1 = (f32[1024,1024]{1,0:T(8,128)}, f32[1024,1024]{1,0:T(8,128)S(1)}, u32[]{:S(2)}) copy-start(f32[1024,1024]{1,0:T(8,128)S(1)} %fusion.105) | copy-start | bytes 12582916
  157.2 12.6 %collective-permute-start.19 = (bf16[256,1024]{1,0:T(8,128)(2,1)S(1)}, bf16[256,1024]{1,0:T(8,128)(2,1)S(1)}, u32[]{:S(2)}, u32[]{:S(2)}) collective-permute-start(bf16[256,1024]{1,0:T(8,128)(2,1)S(1)} %dynamic-slice_convert_fusion.1), channel_id=1, source_target_pairs={{0,2},{1,3},{2,0},{3,1},{4,6},{5,7},{6,4},{7,5},{8,10},{9,11},{10,... | collective-permute-start | bytes 1572872 | tf_op jit(solution)/shard_map/ppermute | solution.py:29
  159.0 13.9 %collective-permute-start.17 = (bf16[272,1024]{1,0:T(8,128)(2,1)S(1)}, bf16[272,1024]{1,0:T(8,128)(2,1)S(1)}, u32[]{:S(2)}, u32[]{:S(2)}) collective-permute-start(bf16[272,1024]{1,0:T(8,128)(2,1)S(1)} %pad_maximum_fusion.8), channel_id=1, source_target_pairs={{0,4},{4,0},{8,12},{12,8},{16,20},{20,16},{24,28},{28,24},{1,5},{5... | collective-permute-start | bytes 1671176 | tf_op jit(solution)/shard_map/ppermute | solution.py:29
  170.1 7.8 %collective-permute-start.20 = (bf16[128,1024]{1,0:T(8,128)(2,1)S(1)}, bf16[128,1024]{1,0:T(8,128)(2,1)S(1)}, u32[]{:S(2)}, u32[]{:S(2)}) collective-permute-start(bf16[128,1024]{1,0:T(8,128)(2,1)S(1)} %dynamic-slice_convert_fusion.5), channel_id=1, source_target_pairs={{0,4},{4,0},{8,12},{12,8},{16,20},{20,16},{24,28},{28,24},{1,5},{5... | collective-permute-start | bytes 786440 | tf_op jit(solution)/shard_map/ppermute | solution.py:29
  173.7 6.8 %collective-permute-start.18 = (bf16[144,1024]{1,0:T(8,128)(2,1)S(1)}, bf16[144,1024]{1,0:T(8,128)(2,1)S(1)}, u32[]{:S(2)}, u32[]{:S(2)}) collective-permute-start(bf16[144,1024]{1,0:T(8,128)(2,1)S(1)} %pad_maximum_fusion.10), channel_id=1, source_target_pairs={{0,2},{1,3},{2,0},{3,1},{4,6},{5,7},{6,4},{7,5},{8,10},{9,11},{10,... | collective-permute-start | bytes 884744 | tf_op jit(solution)/shard_map/ppermute | solution.py:29
  175.9 42.3 %collective-permute-start = (bf16[784,1024]{1,0:T(8,128)(2,1)}, bf16[784,1024]{1,0:T(8,128)(2,1)}, u32[]{:S(2)}, u32[]{:S(2)}) collective-permute-start(bf16[784,1024]{1,0:T(8,128)(2,1)} %pad_maximum_fusion.4), channel_id=1, source_target_pairs={{0,1},{1,0},{2,3},{3,2},{4,5},{5,4},{6,7},{7,6},{8,9},{9,8},{10,11... | collective-permute-start | bytes 4816904 | tf_op jit(solution)/shard_map/ppermute | solution.py:29
  181.5 10.0 %collective-permute-start.23 = (bf16[80,1024]{1,0:T(8,128)(2,1)}, bf16[80,1024]{1,0:T(8,128)(2,1)}, u32[]{:S(2)}, u32[]{:S(2)}) collective-permute-start(bf16[80,1024]{1,0:T(8,128)(2,1)} %get-tuple-element.128), channel_id=1, source_target_pairs={{0,24},{4,28},{8,16},{12,20},{16,8},{20,12},{24,0},{28,4},{1,25},{... | collective-permute-start | bytes 491528 | tf_op jit(solution)/shard_map/ppermute | solution.py:29
  186.0 13.1 %collective-permute-start.22 = (bf16[80,1024]{1,0:T(8,128)(2,1)S(1)}, bf16[80,1024]{1,0:T(8,128)(2,1)}, u32[]{:S(2)}, u32[]{:S(2)}) collective-permute-start(bf16[80,1024]{1,0:T(8,128)(2,1)S(1)} %get-tuple-element.127), channel_id=1, source_target_pairs={{0,16},{4,20},{8,24},{12,28},{16,0},{20,4},{24,8},{28,12},{1,17},{... | collective-permute-start | bytes 491528 | tf_op jit(solution)/shard_map/ppermute | solution.py:29
  186.0 13.1 %collective-permute-start.21 = (bf16[80,1024]{1,0:T(8,128)(2,1)S(1)}, bf16[80,1024]{1,0:T(8,128)(2,1)}, u32[]{:S(2)}, u32[]{:S(2)}) collective-permute-start(bf16[80,1024]{1,0:T(8,128)(2,1)S(1)} %get-tuple-element.126), channel_id=1, source_target_pairs={{0,8},{4,12},{8,0},{12,4},{16,24},{20,28},{24,16},{28,20},{1,9},{5... | collective-permute-start | bytes 491528 | tf_op jit(solution)/shard_map/ppermute | solution.py:29
  201.0 6.6 %collective-permute-start.24 = (bf16[64,1024]{1,0:T(8,128)(2,1)S(1)}, bf16[64,1024]{1,0:T(8,128)(2,1)S(1)}, u32[]{:S(2)}, u32[]{:S(2)}) collective-permute-start(bf16[64,1024]{1,0:T(8,128)(2,1)S(1)} %get-tuple-element.88), channel_id=1, source_target_pairs={{0,8},{4,12},{8,0},{12,4},{16,24},{20,28},{24,16},{28,20},{1,9},{5... | collective-permute-start | bytes 393224 | tf_op jit(solution)/shard_map/ppermute | solution.py:29
  201.0 12.7 %collective-permute-start.25 = (bf16[64,1024]{1,0:T(8,128)(2,1)S(1)}, bf16[64,1024]{1,0:T(8,128)(2,1)S(1)}, u32[]{:S(2)}, u32[]{:S(2)}) collective-permute-start(bf16[64,1024]{1,0:T(8,128)(2,1)S(1)} %get-tuple-element.88), channel_id=1, source_target_pairs={{0,16},{4,20},{8,24},{12,28},{16,0},{20,4},{24,8},{28,12},{1,17},{... | collective-permute-start | bytes 393224 | tf_op jit(solution)/shard_map/ppermute | solution.py:29
  204.0 10.4 %collective-permute-start.26 = (bf16[64,1024]{1,0:T(8,128)(2,1)S(1)}, bf16[64,1024]{1,0:T(8,128)(2,1)S(1)}, u32[]{:S(2)}, u32[]{:S(2)}) collective-permute-start(bf16[64,1024]{1,0:T(8,128)(2,1)S(1)} %get-tuple-element.88), channel_id=1, source_target_pairs={{0,24},{4,28},{8,16},{12,20},{16,8},{20,12},{24,0},{28,4},{1,25},{... | collective-permute-start | bytes 393224 | tf_op jit(solution)/shard_map/ppermute | solution.py:29
  216.1 9.6 %collective-permute-start.29 = (bf16[128,1024]{1,0:T(8,128)(2,1)S(1)}, bf16[128,1024]{1,0:T(8,128)(2,1)S(1)}, u32[]{:S(2)}, u32[]{:S(2)}) collective-permute-start(bf16[128,1024]{1,0:T(8,128)(2,1)S(1)} %bitcast.141), channel_id=1, source_target_pairs={{0,4},{4,0},{8,12},{12,8},{16,20},{20,16},{24,28},{28,24},{1,5},{5... | collective-permute-start | bytes 786440 | tf_op jit(solution)/shard_map/ppermute | solution.py:29
  217.7 36.2 %collective-permute-start.27 = (bf16[128,1024]{1,0:T(8,128)(2,1)S(1)}, bf16[128,1024]{1,0:T(8,128)(2,1)S(1)}, u32[]{:S(2)}, u32[]{:S(2)}) collective-permute-start(bf16[128,1024]{1,0:T(8,128)(2,1)S(1)} %bitcast.139), channel_id=1, source_target_pairs={{0,2},{1,3},{2,0},{3,1},{4,6},{5,7},{6,4},{7,5},{8,10},{9,11},{10,... | collective-permute-start | bytes 786440 | tf_op jit(solution)/shard_map/ppermute | solution.py:29
  222.0 13.2 %collective-permute-start.3 = (bf16[192,1024]{1,0:T(8,128)(2,1)S(1)}, bf16[192,1024]{1,0:T(8,128)(2,1)S(1)}, u32[]{:S(2)}, u32[]{:S(2)}) collective-permute-start(bf16[192,1024]{1,0:T(8,128)(2,1)S(1)} %dynamic-slice_convert_fusion.3), channel_id=1, source_target_pairs={{0,2},{1,3},{2,0},{3,1},{4,6},{5,7},{6,4},{7,5},{8,10},{9,11},{10,... | collective-permute-start | bytes 1179656 | tf_op jit(solution)/shard_map/ppermute | solution.py:29
  225.1 11.0 %collective-permute-start.1 = (bf16[208,1024]{1,0:T(8,128)(2,1)S(1)}, bf16[208,1024]{1,0:T(8,128)(2,1)S(1)}, u32[]{:S(2)}, u32[]{:S(2)}) collective-permute-start(bf16[208,1024]{1,0:T(8,128)(2,1)S(1)} %pad_maximum_fusion.9), channel_id=1, source_target_pairs={{0,4},{4,0},{8,12},{12,8},{16,20},{20,16},{24,28},{28,24},{1,5},{5... | collective-permute-start | bytes 1277960 | tf_op jit(solution)/shard_map/ppermute | solution.py:29
  225.9 34.9 %collective-permute-start.30 = (bf16[256,1024]{1,0:T(8,128)(2,1)S(1)}, bf16[256,1024]{1,0:T(8,128)(2,1)S(1)}, u32[]{:S(2)}, u32[]{:S(2)}) collective-permute-start(bf16[256,1024]{1,0:T(8,128)(2,1)S(1)} %maximum_select_fusion.7), channel_id=1, source_target_pairs={{0,2},{1,3},{2,0},{3,1},{4,6},{5,7},{6,4},{7,5},{8,10},{9,11},{10,... | collective-permute-start | bytes 1572872 | tf_op jit(solution)/shard_map/ppermute | solution.py:29
  235.4 5.7 %collective-permute-start.4 = (bf16[96,1024]{1,0:T(8,128)(2,1)S(1)}, bf16[96,1024]{1,0:T(8,128)(2,1)S(1)}, u32[]{:S(2)}, u32[]{:S(2)}) collective-permute-start(bf16[96,1024]{1,0:T(8,128)(2,1)S(1)} %dynamic-slice_convert_fusion.7), channel_id=1, source_target_pairs={{0,4},{4,0},{8,12},{12,8},{16,20},{20,16},{24,28},{28,24},{1,5},{5... | collective-permute-start | bytes 589832 | tf_op jit(solution)/shard_map/ppermute | solution.py:29
  237.0 15.6 %copy-start.7 = (bf16[1024,1024]{0,1:T(8,128)(2,1)S(1)}, bf16[1024,1024]{0,1:T(8,128)(2,1)}, u32[]{:S(2)}) copy-start(bf16[1024,1024]{0,1:T(8,128)(2,1)} %copy-done.6) | copy-start | bytes 6291460
  237.0 15.6 %copy-start.30 = (bf16[512,1024]{1,0:T(8,128)(2,1)S(1)}, bf16[512,1024]{1,0:T(8,128)(2,1)}, u32[]{:S(2)}) copy-start(bf16[512,1024]{1,0:T(8,128)(2,1)} %param.20) | copy-start | bytes 3145732
  237.1 10.8 %collective-permute-start.2 = (bf16[112,1024]{1,0:T(8,128)(2,1)S(1)}, bf16[112,1024]{1,0:T(8,128)(2,1)S(1)}, u32[]{:S(2)}, u32[]{:S(2)}) collective-permute-start(bf16[112,1024]{1,0:T(8,128)(2,1)S(1)} %pad_maximum_fusion.23), channel_id=1, source_target_pairs={{0,2},{1,3},{2,0},{3,1},{4,6},{5,7},{6,4},{7,5},{8,10},{9,11},{10,... | collective-permute-start | bytes 688136 | tf_op jit(solution)/shard_map/ppermute | solution.py:29
  248.2 7.9 %collective-permute-start.7 = (bf16[64,1024]{1,0:T(8,128)(2,1)S(1)}, bf16[64,1024]{1,0:T(8,128)(2,1)S(1)}, u32[]{:S(2)}, u32[]{:S(2)}) collective-permute-start(bf16[64,1024]{1,0:T(8,128)(2,1)S(1)} %get-tuple-element.131), channel_id=1, source_target_pairs={{0,24},{4,28},{8,16},{12,20},{16,8},{20,12},{24,0},{28,4},{1,25},{... | collective-permute-start | bytes 393224 | tf_op jit(solution)/shard_map/ppermute | solution.py:29
  249.1 11.4 %collective-permute-start.6 = (bf16[64,1024]{1,0:T(8,128)(2,1)S(1)}, bf16[64,1024]{1,0:T(8,128)(2,1)S(1)}, u32[]{:S(2)}, u32[]{:S(2)}) collective-permute-start(bf16[64,1024]{1,0:T(8,128)(2,1)S(1)} %get-tuple-element.130), channel_id=1, source_target_pairs={{0,16},{4,20},{8,24},{12,28},{16,0},{20,4},{24,8},{28,12},{1,17},{... | collective-permute-start | bytes 393224 | tf_op jit(solution)/shard_map/ppermute | solution.py:29
  251.7 8.9 %collective-permute-start.5 = (bf16[64,1024]{1,0:T(8,128)(2,1)S(1)}, bf16[64,1024]{1,0:T(8,128)(2,1)S(1)}, u32[]{:S(2)}, u32[]{:S(2)}) collective-permute-start(bf16[64,1024]{1,0:T(8,128)(2,1)S(1)} %get-tuple-element.129), channel_id=1, source_target_pairs={{0,8},{4,12},{8,0},{12,4},{16,24},{20,28},{24,16},{28,20},{1,9},{5... | collective-permute-start | bytes 393224 | tf_op jit(solution)/shard_map/ppermute | solution.py:29
  254.0 19.2 %collective-permute-start.28 = (bf16[256,1024]{1,0:T(8,128)(2,1)S(1)}, bf16[256,1024]{1,0:T(8,128)(2,1)S(1)}, u32[]{:S(2)}, u32[]{:S(2)}) collective-permute-start(bf16[256,1024]{1,0:T(8,128)(2,1)S(1)} %maximum_select_fusion.6), channel_id=1, source_target_pairs={{0,4},{4,0},{8,12},{12,8},{16,20},{20,16},{24,28},{28,24},{1,5},{5... | collective-permute-start | bytes 1572872 | tf_op jit(solution)/shard_map/ppermute | solution.py:29
  260.6 10.9 %copy-start.16 = (bf16[64,1024]{1,0:T(8,128)(2,1)}, bf16[64,1024]{1,0:T(8,128)(2,1)S(1)}, u32[]{:S(2)}) copy-start(bf16[64,1024]{1,0:T(8,128)(2,1)S(1)} %collective-permute-done.5) | copy-start | bytes 393220
  260.7 5.4 %collective-permute-start.8 = (bf16[48,1024]{1,0:T(8,128)(2,1)S(1)}, bf16[48,1024]{1,0:T(8,128)(2,1)S(1)}, u32[]{:S(2)}, u32[]{:S(2)}) collective-permute-start(bf16[48,1024]{1,0:T(8,128)(2,1)S(1)} %get-tuple-element.100), channel_id=1, source_target_pairs={{0,8},{4,12},{8,0},{12,4},{16,24},{20,28},{24,16},{28,20},{1,9},{5... | collective-permute-start | bytes 294920 | tf_op jit(solution)/shard_map/ppermute | solution.py:29
  261.7 9.7 %collective-permute-start.9 = (bf16[48,1024]{1,0:T(8,128)(2,1)S(1)}, bf16[48,1024]{1,0:T(8,128)(2,1)S(1)}, u32[]{:S(2)}, u32[]{:S(2)}) collective-permute-start(bf16[48,1024]{1,0:T(8,128)(2,1)S(1)} %get-tuple-element.100), channel_id=1, source_target_pairs={{0,16},{4,20},{8,24},{12,28},{16,0},{20,4},{24,8},{28,12},{1,17},{... | collective-permute-start | bytes 294920 | tf_op jit(solution)/shard_map/ppermute | solution.py:29
  263.1 8.4 %collective-permute-start.10 = (bf16[48,1024]{1,0:T(8,128)(2,1)S(1)}, bf16[48,1024]{1,0:T(8,128)(2,1)S(1)}, u32[]{:S(2)}, u32[]{:S(2)}) collective-permute-start(bf16[48,1024]{1,0:T(8,128)(2,1)S(1)} %get-tuple-element.100), channel_id=1, source_target_pairs={{0,24},{4,28},{8,16},{12,20},{16,8},{20,12},{24,0},{28,4},{1,25},{... | collective-permute-start | bytes 294920 | tf_op jit(solution)/shard_map/ppermute | solution.py:29
  271.5 5.7 %collective-permute-start.13 = (bf16[96,1024]{1,0:T(8,128)(2,1)S(1)}, bf16[96,1024]{1,0:T(8,128)(2,1)S(1)}, u32[]{:S(2)}, u32[]{:S(2)}) collective-permute-start(bf16[96,1024]{1,0:T(8,128)(2,1)S(1)} %bitcast.145), channel_id=1, source_target_pairs={{0,4},{4,0},{8,12},{12,8},{16,20},{20,16},{24,28},{28,24},{1,5},{5... | collective-permute-start | bytes 589832 | tf_op jit(solution)/shard_map/ppermute | solution.py:29
  273.7 7.5 %copy-start.25 = (pred[1024]{0:T(1024)(128)(4,1)S(1)}, pred[1024]{0:T(1024)(128)(4,1)}, u32[]{:S(2)}) copy-start(pred[1024]{0:T(1024)(128)(4,1)} %copy-done.23) | copy-start | bytes 3076
  273.7 5.7 %collective-permute-start.11 = (bf16[96,1024]{1,0:T(8,128)(2,1)S(1)}, bf16[96,1024]{1,0:T(8,128)(2,1)S(1)}, u32[]{:S(2)}, u32[]{:S(2)}) collective-permute-start(bf16[96,1024]{1,0:T(8,128)(2,1)S(1)} %bitcast.143), channel_id=1, source_target_pairs={{0,2},{1,3},{2,0},{3,1},{4,6},{5,7},{6,4},{7,5},{8,10},{9,11},{10,... | collective-permute-start | bytes 589832 | tf_op jit(solution)/shard_map/ppermute | solution.py:29
  276.6 20.5 %collective-permute-start.31 = (bf16[1024,1024]{1,0:T(8,128)(2,1)}, bf16[1024,1024]{1,0:T(8,128)(2,1)}, u32[]{:S(2)}, u32[]{:S(2)}) collective-permute-start(bf16[1024,1024]{1,0:T(8,128)(2,1)} %pad_maximum_fusion.3), channel_id=1, source_target_pairs={{0,1},{1,0},{2,3},{3,2},{4,5},{5,4},{6,7},{7,6},{8,9},{9,8},{10,11... | collective-permute-start | bytes 6291464 | tf_op jit(solution)/shard_map/ppermute | solution.py:29
  277.3 12.7 %collective-permute-start.14 = (bf16[192,1024]{1,0:T(8,128)(2,1)S(1)}, bf16[192,1024]{1,0:T(8,128)(2,1)}, u32[]{:S(2)}, u32[]{:S(2)}) collective-permute-start(bf16[192,1024]{1,0:T(8,128)(2,1)S(1)} %maximum_select_fusion.9), channel_id=1, source_target_pairs={{0,2},{1,3},{2,0},{3,1},{4,6},{5,7},{6,4},{7,5},{8,10},{9,11},{10,... | collective-permute-start | bytes 1179656 | tf_op jit(solution)/shard_map/ppermute | solution.py:29
  280.3 11.3 %collective-permute-start.12 = (bf16[192,1024]{1,0:T(8,128)(2,1)}, bf16[192,1024]{1,0:T(8,128)(2,1)}, u32[]{:S(2)}, u32[]{:S(2)}) collective-permute-start(bf16[192,1024]{1,0:T(8,128)(2,1)} %maximum_select_fusion.8), channel_id=1, source_target_pairs={{0,4},{4,0},{8,12},{12,8},{16,20},{20,16},{24,28},{28,24},{1,5},{5... | collective-permute-start | bytes 1179656 | tf_op jit(solution)/shard_map/ppermute | solution.py:29
  290.0 6.5 %copy-start.19 = (f32[1,1024]{1,0:T(1,128)S(1)}, f32[1,1024]{1,0:T(1,128)}, u32[]{:S(2)}) copy-start(f32[1,1024]{1,0:T(1,128)} %get-tuple-element.108) | copy-start | bytes 12292
  290.0 6.5 %copy-start.20 = (f32[1,1024]{1,0:T(1,128)S(1)}, f32[1,1024]{1,0:T(1,128)}, u32[]{:S(2)}) copy-start(f32[1,1024]{1,0:T(1,128)} %get-tuple-element.105) | copy-start | bytes 12292
  290.0 7.1 %copy-start.3 = (bf16[512,1024]{1,0:T(8,128)(2,1)S(1)}, bf16[512,1024]{1,0:T(8,128)(2,1)}, u32[]{:S(2)}) copy-start(bf16[512,1024]{1,0:T(8,128)(2,1)} %copy-done.2) | copy-start | bytes 3145732
  293.4 9.7 %collective-permute-start.15 = (bf16[768,1024]{1,0:T(8,128)(2,1)S(1)}, bf16[768,1024]{1,0:T(8,128)(2,1)S(1)}, u32[]{:S(2)}, u32[]{:S(2)}) collective-permute-start(bf16[768,1024]{1,0:T(8,128)(2,1)S(1)} %pad_maximum_fusion.5), channel_id=1, source_target_pairs={{0,1},{1,0},{2,3},{3,2},{4,5},{5,4},{6,7},{7,6},{8,9},{9,8},{10,11... | collective-permute-start | bytes 4718600 | tf_op jit(solution)/shard_map/ppermute | solution.py:29
  (29 other events, 115.7 us)

commit v2 on v0

v2 whole, which is shorter than its diff:
```python
import functools

import jax
import jax.numpy as jnp
from jax import lax
from jax.experimental import pallas as pl
from jax.experimental.pallas import tpu as pltpu
from jax.sharding import PartitionSpec as P

F32 = jnp.float32
BF16 = jnp.bfloat16
LANES = 128
BLOCK = 256
MEGA = 1024 * 1024
MARK = 64.0
PLACES = 16
BIAS_ROWS = 16
ROWS_ROWS = (((0,), (0,)), ((), ()))
COLS_COLS = (((1,), (1,)), ((), ()))
VMEM = pl.BlockSpec(memory_space=pltpu.VMEM)
SMEM = pl.BlockSpec(memory_space=pltpu.SMEM)
ANY = pl.BlockSpec(memory_space=pl.ANY)


COST = pl.CostEstimate(flops=0, bytes_accessed=0, transcendentals=0)


def dot(left, right):
    return jnp.dot(left, right, preferred_element_type=F32)


def contract_rows(left, right):
    return lax.dot_general(left, right, ROWS_ROWS, preferred_element_type=F32)


def contract_cols(left, right):
    return lax.dot_general(left, right, COLS_COLS, preferred_element_type=F32)


def whole(*shape):
    return pl.BlockSpec(shape, lambda *_: (0,) * len(shape), pipeline_mode=pl.Buffered(1))


def shape(dims, dtype):
    return jax.ShapeDtypeStruct(dims, dtype)


def call(kernel, outs, in_specs, out_specs, scratch, tokens=(), moved=0, **more):
    count, extra = len(in_specs), len(tokens)

    def run(*refs):
        return kernel(*refs[:count], *refs[count + extra :])

    built = pl.pallas_call(
        run,
        out_shape=outs,
        in_specs=list(in_specs) + [ANY] * extra,
        out_specs=out_specs,
        scratch_shapes=list(scratch),
        compiler_params=pltpu.CompilerParams(vmem_limit_bytes=60 * MEGA),
        cost_estimate=pl.CostEstimate(flops=0, bytes_accessed=moved * MEGA, transcendentals=0),
    )
    return lambda *operands: built(*operands, *tokens)


class Copies:
    def __init__(self, arrived):
        self.arrived = arrived
        self.used = 0

    def start(self, source, target):
        copy = pltpu.make_async_copy(source, target, self.arrived.at[self.used])
        self.used += 1
        copy.start()
        return copy

    def by_blocks(self, source, target, start=True):
        first, count = self.used, source.shape[0] // BLOCK
        self.used += count

        def block(step):
            here = rows_of(step)
            return pltpu.make_async_copy(
                source.at[here], target.at[here], self.arrived.at[first + step]
            )

        if start:
            each_block(count, lambda step: block(step).start())
        return block


def rows_of(step):
    return pl.ds(pl.multiple_of(step * BLOCK, BLOCK), BLOCK)


def each_block(count, body):
    def run(step, _):
        body(step)
        return 0

    lax.fori_loop(0, count, run, 0)


def sigmoid(value):
    return 0.5 * jnp.tanh(0.5 * value) + 0.5


def add_up(low):
    rows, width = low.shape
    return jnp.sum(low.astype(F32).reshape(rows // 8, 8, width), axis=0)


def outgoing_kernel(send, board, features_hbm, out, features, arrived):
    got = pltpu.make_async_copy(features_hbm, features, arrived.at[0])
    got.start()
    rows, width = features.shape
    size = min(512, out.shape[0])
    for step in range(out.shape[0] // size):
        here = slice(step * size, step * size + size)
        names = jnp.broadcast_to(send[:, here], (LANES, size)).T
        lane = lax.broadcasted_iota(jnp.int32, (size, LANES), 1)
        match = [names == lane + first for first in range(0, rows, LANES)]
        hot = jnp.concatenate([jnp.where(m, 1.0, 0.0) for m in match], axis=1)
        kinds = jnp.sum(hot * board[...].astype(F32), axis=1, keepdims=True)
        if step == 0:
            got.wait()
        picked = dot(hot.astype(BF16), features[...])
        last = width - LANES
        out[here, :last] = picked[:, :last].astype(BF16)
        marked = (kinds > 0.5) & (lane == LANES - 1)
        out[here, last:] = jnp.where(marked, MARK, picked[:, last:]).astype(BF16)


def local_kernel(
    names, weights, kinds, q_bias, w_bias, features_hbm, proj_hbm, q_hbm, w_hbm,
    near_hbm, far_hbm, hidden_hbm, slope_hbm, agg_hbm, base_hbm, lowered_hbm, boards,
    features, proj, q_weight, w_top, near, far, hidden, active, slope, agg, base, masked, arrived,
):
    copies = Copies(arrived)
    rows, width = features.shape
    lowered = proj.shape[0]
    got = [
        copies.start(features_hbm, features),
        copies.start(proj_hbm, proj),
        copies.start(q_hbm, q_weight),
    ]
    got_w = copies.start(w_hbm.at[:width], w_top)
    slots = names.shape[1]
    near_heights = near.shape[1] // LANES
    heights = near_heights + far.shape[1] // LANES

    def eight(group):
        name = names[pl.ds(group, 1), :]
        lane = lax.broadcasted_iota(jnp.int32, (LANES, slots), 0)
        hot = jnp.where(lane == (name & (LANES - 1)), 1.0, 0.0).astype(BF16)
        node = lax.broadcasted_iota(jnp.int32, (1, slots), 1) // (slots // 8)
        key = (name >> 7) * 8 + node
        row = lax.broadcasted_iota(jnp.int32, (8 * heights, slots), 0)
        held = jnp.where(row == key, weights[pl.ds(group, 1), :], 0.0)
        return contract_cols(held.astype(BF16), hot)

    def pair(step, _):
        first, second = eight(2 * step), eight(2 * step + 1)
        place = pl.ds(pl.multiple_of(16 * step, 16), 16)
        for h in range(heights):
            both = jnp.concatenate([first[8 * h : 8 * h + 8], second[8 * h : 8 * h + 8]], axis=0)
            if h < near_heights:
                near[place, h * LANES : (h + 1) * LANES] = both.astype(BF16)
            else:
                at = h - near_heights
                far[place, at * LANES : (at + 1) * LANES] = both.astype(BF16)
        return 0

    lax.fori_loop(0, names.shape[0] // 2, pair, 0, unroll=4)
    out = [copies.start(near, near_hbm), copies.start(far, far_hbm)]
    for copy in got:
        copy.wait()
    count = rows // BLOCK

    def front(step):
        here = rows_of(step)
        own = features[here]
        low = own[:, :lowered]
        is_board = kinds[here] == 1
        boards[here] = jnp.where(is_board, jnp.ones((BLOCK, LANES), F32), 0.0)
        masked[here] = jnp.where(is_board, low, jnp.zeros_like(low))
        left = jnp.where(is_board, dot(low, proj[...]), own.astype(F32)).astype(BF16)
        hidden[here] = left
        pre = dot(left, q_weight[...]) + q_bias[...]
        sigma = sigmoid(pre)
        active[here] = (pre * sigma).astype(BF16)
        slope[here] = sigma + pre * sigma * (1.0 - sigma)

    each_block(count, front)
    out += [copies.start(hidden, hidden_hbm), copies.start(slope, slope_hbm)]
    out += [copies.start(masked, lowered_hbm)]
    got_w.wait()
    agg_out = copies.by_blocks(agg, agg_hbm, start=False)
    base_out = copies.by_blocks(base, base_hbm, start=False)

    def local(step):
        here = rows_of(step)
        agg[here] = dot(near[here], active[...])
        agg_out(step).start()
        base[here] = dot(hidden[here], w_top[...]) + w_bias[...]
        base_out(step).start()

    each_block(count, local)
    for copy in out:
        copy.wait()
    each_block(count, lambda step: agg_out(step).wait())
    each_block(count, lambda step: base_out(step).wait())


def combine_kernel(
    live, bits, weight, q_bias, far_hbm, incoming_hbm, proj_hbm, q_hbm, agg_hbm, base_hbm, w_hbm,
    cotangent_hbm, hidden_hbm,
    embedding_hbm, dpre2_hbm, dagg_hbm, to_peers_hbm, w_sent_hbm, w_kept_hbm, far_hidden_hbm,
    far_dpre_hbm, far_lowered_hbm, far_slope_hbm, bias,
    far, incoming, proj, q_weight, agg, base, w_low, cotangent, hidden, mean, dpre2, dagg, to_peers,
    w_sent, w_kept, far_hidden, far_slope, far_lowered, arrived,
):
    copies = Copies(arrived)
    rows, width = agg.shape
    count = rows // BLOCK
    got_front = [copies.start(incoming_hbm, incoming), copies.start(proj_hbm, proj)]
    got_front += [copies.start(q_hbm, q_weight)]
    got = [copies.start(far_hbm, far), copies.start(w_hbm.at[width:], w_low)]
    got_agg = copies.by_blocks(agg_hbm, agg)
    got_base = copies.by_blocks(base_hbm, base)
    got_cotangent = copies.by_blocks(cotangent_hbm, cotangent)
    got_hidden = copies.start(hidden_hbm, hidden)
    embedding = agg
    embedding_out = copies.by_blocks(embedding, embedding_hbm, start=False)
    dpre2_out = copies.by_blocks(dpre2, dpre2_hbm, start=False)
    dagg_out = copies.by_blocks(dagg, dagg_hbm, start=False)
    outs = [embedding_out, dpre2_out, dagg_out]
    bias[...] = jnp.zeros(bias.shape, F32)
    for copy in got_front:
        copy.wait()
    lowered = proj.shape[0]
    active = incoming
    held = far_hidden.shape[0] == far.shape[1]

    def move(*pairs):
        for i, (source, target) in enumerate(pairs):
            copy = pltpu.make_async_copy(source, target, arrived.at[arrived.shape[0] - 1 - i])
            copy.start()
            copy.wait()

    def front(step):
        here = rows_of(step)
        spot = here if held else pl.ds(0, BLOCK)
        own = incoming[here]
        is_board = own[:, width - 1 :].astype(F32) > MARK / 2
        low = own[:, :lowered]
        far_lowered[spot] = jnp.where(is_board, low, jnp.zeros_like(low))
        left = jnp.where(is_board, dot(low, proj[...]), own.astype(F32)).astype(BF16)
        far_hidden[spot] = left
        pre = dot(left, q_weight[...]) + q_bias[...]
        sigma = sigmoid(pre)
        active[here] = (pre * sigma).astype(BF16)
        far_slope[spot] = sigma + pre * sigma * (1.0 - sigma)
        if not held:
            move(
                (far_lowered, far_lowered_hbm.at[here]),
                (far_hidden, far_hidden_hbm.at[here]),
                (far_slope, far_slope_hbm.at[here]),
            )

    each_block(far.shape[1] // BLOCK, front)
    far_out = []
    if held:
        far_out += [copies.start(far_hidden, far_hidden_hbm)]
        far_out += [copies.start(far_lowered, far_lowered_hbm)]
    for copy in got:
        copy.wait()

    def node_block(step):
        here = rows_of(step)
        got_agg(step).wait()
        average = ((agg[here] + dot(far[here], active[...])) * weight[here]).astype(BF16)
        mean[here] = average
        got_base(step).wait()
        pre = base[here] + dot(average, w_low[...])
        got_cotangent(step).wait()
        sigma = sigmoid(pre)
        post = pre * sigma
        scale = lax.rsqrt(jnp.sum(post * post, axis=1, keepdims=True) + 1e-06)
        row = lax.broadcasted_iota(jnp.int32, (BLOCK, 1), 0) + step * BLOCK
        scale = jnp.where(row < live[0], scale, 0.0)
        embedding[here] = post * scale
        grad = cotangent[here].astype(F32)
        lean = scale * scale * scale * jnp.sum(post * grad, axis=1, keepdims=True)
        dpost = scale * grad - post * lean
        low = (dpost * (sigma + post * (1.0 - sigma))).astype(BF16)
        dpre2[here] = low
        bias[...] += add_up(low)
        dagg[here] = (contract_cols(low, w_low[...]) * weight[here]).astype(BF16)
        for out in outs:
            out(step).start()

    each_block(count, node_block)
    got_hidden.wait()

    stride = width // PLACES

    @pl.when(bits[0] == 1)
    def _():
        write_pieces(bits[2], [(hidden, 0, dpre2)], width, w_sent, stride, 0)
        write_pieces(bits[1], [(mean, 0, dpre2)], width, w_kept, stride, 0)

    @pl.when(bits[0] == 0)
    def _():
        write_pieces(bits[2], [(mean, 0, dpre2)], width, w_sent, stride, 0)
        write_pieces(bits[1], [(hidden, 0, dpre2)], width, w_kept, stride, 0)

    far_out += [copies.start(w_sent, w_sent_hbm), copies.start(w_kept, w_kept_hbm)]
    far_dpre = far_hidden
    if held:
        far_out.pop(0).wait()

    def peer_block(step):
        here = rows_of(step)
        spot = here if held else pl.ds(0, BLOCK)
        if not held:
            move((far_slope_hbm.at[here], far_slope))
        table = contract_rows(far[:, here], dagg[...])
        to_peers[spot] = table.astype(BF16)
        far_dpre[spot] = (table * far_slope[spot]).astype(BF16)
        if not held:
            move((to_peers, to_peers_hbm.at[here]), (far_dpre, far_dpre_hbm.at[here]))

    each_block(far.shape[1] // BLOCK, peer_block)
    if held:
        far_out += [copies.start(to_peers, to_peers_hbm), copies.start(far_dpre, far_dpre_hbm)]
    for copy in far_out:
        copy.wait()
    for out in outs:
        each_block(count, lambda step, out=out: out(step).wait())


def write_pieces(mark, pairs, depth, out, stride, at, plus=None):
    piece = depth // PLACES
    size = min(BLOCK, depth)

    def block(step):
        product = 0.0
        for left, first, right in pairs:
            here = pl.ds(pl.multiple_of(first + step * size, size), size)
            product += contract_rows(left[:, here], right[...])
        write_block(mark, product, step * (size // piece), out, stride, at, piece, plus)

    each_block(depth // size, block)


def write_block(mark, product, first, out, stride, at, piece, plus=None):
    for j in range(product.shape[0] // piece):
        place = (first + j) ^ mark
        here = pl.ds(pl.multiple_of(place * stride + at, 16), piece)
        part = product[j * piece : (j + 1) * piece]
        if plus is not None:
            part += plus[here].astype(F32)
        out[here] = part.astype(out.dtype)


def gradients_kernel(
    bits, w_bias, near_hbm, dagg_hbm, slope_hbm, dpre2_hbm, w_hbm, hidden_hbm,
    far_hidden_hbm, far_dpre_hbm, lowered_hbm, far_lowered_hbm, q_hbm,
    dtable_hbm, djoined_hbm, sent_hbm, kept_hbm,
    near, dagg, slope, dpre2, w_top, hidden, far_hidden, far_dpre, lowered, far_lowered,
    q_weight, dtable, djoined, dpre, sent, kept, bias, arrived,
):
    copies = Copies(arrived)
    rows, width = dpre.shape
    depth = lowered.shape[1]
    half = width // 2
    count = rows // BLOCK
    got_table = [copies.start(dagg_hbm, dagg), copies.start(near_hbm, near)]
    got_slope = copies.by_blocks(slope_hbm, slope)
    got_q = [copies.start(hidden_hbm, hidden), copies.start(far_hidden_hbm, far_hidden)]
    got_q += [copies.start(far_dpre_hbm, far_dpre)]
    got_joined = [copies.start(w_hbm.at[:width], w_top), copies.start(dpre2_hbm, dpre2)]
    got_p = [copies.start(lowered_hbm, lowered), copies.start(far_lowered_hbm, far_lowered)]
    got_p += [copies.start(q_hbm, q_weight)]
    bias[...] = jnp.zeros(bias.shape, F32)
    for copy in got_table:
        copy.wait()

    def table_block(step):
        here = rows_of(step)
        table = contract_rows(near[:, here], dagg[...])
        dtable[here] = table.astype(BF16)
        got_slope(step).wait()
        low = (table * slope[here]).astype(BF16)
        dpre[here] = low
        bias[...] += add_up(low)

    each_block(count, table_block)
    out = [copies.start(dtable, dtable_hbm)]
    for copy in got_q:
        copy.wait()

    def far_block(step):
        bias[...] += add_up(far_dpre[rows_of(step)])

    each_block(far_dpre.shape[0] // BLOCK, far_block)
    stride = (half + depth // 2) // PLACES
    sides = ((sent, 1 - bits[0], bits[2]), (kept, bits[0], bits[1]))
    for target, side, mark in sides:
        first = side * half
        pairs = [(hidden, first, dpre), (far_hidden, first, far_dpre)]
        write_pieces(mark, pairs, half, target, stride, 0)
    for copy in got_joined:
        copy.wait()

    def joined_block(step):
        here = rows_of(step)
        djoined[here] = contract_cols(dpre2[here], w_top[...]).astype(BF16)

    each_block(count, joined_block)
    out += [copies.start(djoined, djoined_hbm)]
    for copy in got_p:
        copy.wait()
    for target, side, mark in sides:
        here = pl.ds(pl.multiple_of(side * (depth // 2), depth // 2), depth // 2)
        part = lowered[:, here]
        through = contract_rows(part, dpre[...]) + contract_rows(far_lowered[:, here], far_dpre[...])
        product = contract_cols(through.astype(BF16), q_weight[...])
        product += contract_rows(part, djoined[...])
        write_block(mark, product, 0, target, stride, half // PLACES, depth // 2 // PLACES)
    row = lax.broadcasted_iota(jnp.int32, (BIAS_ROWS, 1), 0)
    block = jnp.zeros((BIAS_ROWS, width), F32)
    for i, part in enumerate((bias, w_bias)):
        total = jnp.sum(part[...], axis=0, keepdims=True)
        high = total.astype(BF16).astype(F32)
        block = jnp.where(row == i, high, jnp.where(row == i + 2, total - high, block))
    sent[sent.shape[0] - BIAS_ROWS :] = block.astype(BF16)
    out += [copies.start(sent, sent_hbm), copies.start(kept, kept_hbm)]
    for copy in out:
        copy.wait()


def grad_features_kernel(
    send, boards, returned_hbm, dtable_hbm, slope_hbm, q_hbm, djoined_hbm, proj_hbm, grad_hbm,
    returned, dtable, slope, q_weight, djoined, proj, arrived,
):
    copies = Copies(arrived)
    rows = dtable.shape[0]
    lowered = proj.shape[0]
    count = rows // BLOCK
    got = [copies.start(returned_hbm, returned), copies.start(dtable_hbm, dtable)]
    got += [copies.start(q_hbm, q_weight)]
    got_slope = copies.by_blocks(slope_hbm, slope)
    got += [copies.start(djoined_hbm, djoined), copies.start(proj_hbm, proj)]
    grad_out = copies.by_blocks(slope, grad_hbm, start=False)
    for copy in got:
        copy.wait()

    def block(step):
        here = rows_of(step)
        row = lax.broadcasted_iota(jnp.int32, (BLOCK, send.shape[1]), 0) + step * BLOCK
        hot = jnp.where(row == send[...], 1.0, 0.0).astype(BF16)
        owned = dtable[here].astype(F32) + dot(hot, returned[...])
        got_slope(step).wait()
        dpre = (owned * slope[here]).astype(BF16)
        low = (contract_cols(dpre, q_weight[...]) + djoined[here].astype(F32)).astype(BF16)
        product = contract_cols(low, proj[...])
        is_board = boards[here, :1] > 0.5
        own = low.astype(F32)
        slope[here, :lowered] = jnp.where(is_board, product, own[:, :lowered])
        slope[here, lowered:] = jnp.where(is_board, 0.0, own[:, lowered:])
        grad_out(step).start()

    each_block(count, block)
    each_block(count, lambda step: grad_out(step).wait())


def ordered_kernel(bits, held, *refs, count, other):
    outs = refs[-count:]
    mark = bits[2 if other else 1] % 4
    stride = held.shape[0] // 4
    first = 0
    for out in outs:
        piece = out.shape[0] // 4
        for j in range(4):
            here = pl.ds(pl.multiple_of((j ^ mark) * stride + first, 16), piece)
            out[j * piece : (j + 1) * piece] = held[here].astype(F32)
        first += piece


def ordered(bits, held, sizes, other, into=None):
    columns = held.shape[1]
    steps = PLACES // 4
    into = list(into or ())
    mark = 2 if other else 1

    def target(i, b):
        return ((1 - b[0] if other else b[0]) * steps + i, 0)

    return pl.pallas_call(
        functools.partial(ordered_kernel, count=len(sizes), other=other),
        out_shape=[shape((2 * PLACES * size, columns), F32) for size in sizes],
        grid_spec=pltpu.PrefetchScalarGridSpec(
            num_scalar_prefetch=1,
            grid=(steps,),
            in_specs=[pl.BlockSpec((4 * sum(sizes), columns), lambda i, b: (i ^ (b[mark] // 4), 0))]
            + [ANY] * len(into),
            out_specs=[pl.BlockSpec((4 * size, columns), target) for size in sizes],
        ),
        input_output_aliases={2 + i: i for i in range(len(into))},
        compiler_params=pltpu.CompilerParams(vmem_limit_bytes=24 * MEGA),
        cost_estimate=pl.CostEstimate(
            flops=0, bytes_accessed=200 * MEGA, transcendentals=0
        ),
    )(bits, held, *into)


def swap(value, axis, mask):
    size = lax.axis_size(axis)
    return lax.ppermute(value, axis, [(s, s ^ mask) for s in range(size)])


WAYS = (
    (("dom", 1), ("rep", 2)),
    (("rep", 2), ("dom", 1)),
    (("dom", 2), ("dom", 4)),
    (("dom", 4), ("dom", 2)),
)
FAR_WAYS = WAYS[3], WAYS[2], (("dom", 6), ("dom", 6))


def cross(value, ways):
    doms, reps = lax.axis_size("dom"), lax.axis_size("rep")
    pairs = []
    for d in range(doms):
        for r in range(reps):
            axis, mask = ways[r % 2]
            to = (d ^ mask, r) if axis == "dom" else (d, r ^ mask)
            pairs.append((d * reps + r, to[0] * reps + to[1]))
    return lax.ppermute(value, ("dom", "rep"), pairs)


class Order:
    def __init__(self):
        self.last = ()

    def __call__(self, step, *operands):
        held, _ = lax.optimization_barrier((operands, self.last))
        result = step(*held)
        self.last = jax.tree.leaves(result)[:1]
        return result


def pack(bias):
    high = lax.reduce_precision(bias, 8, 7)
    rest = jnp.zeros((BIAS_ROWS - 4, bias.shape[1]), F32)
    return jnp.concatenate([high, bias - high, rest]).astype(BF16)


def unpack(rows):
    rows = rows[-BIAS_ROWS:].astype(F32)
    return rows[:2] + rows[2:4]


class PieceSum:
    def __init__(self, sent, with_bias):
        self.got = swap(sent, "rep", 1)
        self.bias = unpack(sent) if with_bias else None
        self.stage = 0

    def first(self, order, kept):
        self.split(order, kept, self.got)

    def reduce(self, order):
        self.stage += 1
        self.split(order, self.held, self.back)

    def split(self, order, held, back):
        half = held.shape[0] // 2

        def step(held, back, bias):
            stay = held[:half].astype(F32) + back[:half].astype(F32)
            away = (held[half:].astype(F32) + back[half : 2 * half].astype(F32)).astype(BF16)
            if bias is not None:
                bias = bias + unpack(back)
                away = jnp.concatenate([away, pack(bias)])
                bias = unpack(away)
            return away, stay, bias

        away, self.held, self.bias = order(step, held, back, self.bias)
        self.back = cross(away, WAYS[self.stage])

    def reduce_far(self, order):
        part = self.held.shape[0] // 4

        def step(held, back, bias):
            stay = held[:part] + back[:part].astype(F32)
            if bias is not None:
                bias = bias + unpack(back)
                packed = pack(bias)
                bias = unpack(packed)
            aways = []
            for i in (1, 2, 3):
                here = slice(i * part, (i + 1) * part)
                away = (held[here] + back[here].astype(F32)).astype(BF16)
                aways.append(away if bias is None else jnp.concatenate([away, packed]))
            return aways, stay, bias

        aways, self.held, self.bias = order(step, self.held, self.back, self.bias)
        self.back = [cross(away, way) for away, way in zip(aways, FAR_WAYS)]

    def turn_far(self, order):
        rows = self.held.shape[0]

        def step(held, back, bias):
            total = held + sum(b[:rows].astype(F32) for b in back)
            if bias is not None:
                got = [unpack(b) for b in back]
                bias = (bias + got[0]) + (got[1] + got[2])
            return total.astype(BF16), bias

        total, self.bias = order(step, self.held, self.back, self.bias)
        self.held = self.beyond(total)
        self.back = [cross(self.held, way) for way in FAR_WAYS]

    def gather_far(self, order):
        self.held = order(lambda h, b: jnp.concatenate([h] + list(b)), self.held, self.back)
        self.back = cross(self.held, WAYS[self.stage])

    def beyond(self, total):
        mask = 8
        while mask < lax.axis_size("dom"):
            total = (total.astype(F32) + swap(total, "dom", mask).astype(F32)).astype(BF16)
            if self.bias is not None:
                self.bias = self.bias + swap(self.bias, "dom", mask)
            mask *= 2
        return total

    def turn(self, order):
        rows = self.held.shape[0]

        def step(held, back, bias):
            total = (held + back[:rows].astype(F32)).astype(BF16)
            return total, None if bias is None else bias + unpack(back)

        total, self.bias = order(step, self.held, self.back, self.bias)
        self.held = self.beyond(total)
        self.back = cross(self.held, WAYS[self.stage])

    def gather(self, order):
        self.held = order(lambda *parts: jnp.concatenate(parts), self.held, self.back)
        self.stage -= 1
        self.back = cross(self.held, WAYS[self.stage])

    def last(self, order):
        extra = [] if self.bias is None else [pack(self.bias)]
        self.mine = order(lambda *parts: jnp.concatenate(parts), self.held, self.back, *extra)
        self.other = swap(self.mine, "rep", 1)


def per_device(
    features,
    node_type,
    neighbours,
    importance,
    send_rows,
    live_rows,
    proj_board,
    q_weight,
    q_bias,
    w_weight,
    w_bias,
    cotangent,
):
    rows, width = features.shape
    lowered = proj_board.shape[0]
    halo = send_rows.shape[0]
    slots = importance.shape[1]
    dom = lax.axis_index("dom")
    rep = lax.axis_index("rep")
    core, y, x, z = rep % 2, rep // 2 % 2, dom % 2, dom // 2 % 4
    low_z, high_z = z % 2, z // 2
    marks = x * 8 + y * 4 + low_z * 2 + high_z, y * 8 + x * 4 + high_z * 2 + low_z
    own, sibling = jnp.where(core == 0, marks[0], marks[1]), jnp.where(core == 0, marks[1], marks[0])
    bits = jnp.stack([core, own, sibling]).astype(jnp.int32)
    send_row = send_rows.reshape(1, halo)
    board_row = node_type.reshape(1, rows)
    kinds = node_type.reshape(rows, 1)
    q_bias_row = q_bias.reshape(1, width)
    w_bias_row = w_bias.reshape(1, width)
    low = (rows, width)
    half = width // 2

    def buffers(*dims):
        return [pltpu.VMEM(d, kind) for d, kind in dims]

    def semaphores(count):
        return [pltpu.SemaphoreType.DMA((count,))]

    outgoing = call(
        outgoing_kernel,
        shape((halo, width), BF16),
        [whole(1, halo), whole(1, rows), ANY],
        whole(halo, width),
        buffers((low, BF16)) + semaphores(1),
    )(send_row, board_row, features)
    incoming = lax.all_to_all(outgoing, "dom", split_axis=0, concat_axis=0, tiled=True)

    wide = -(-slots // 64) * 64
    pad = ((0, 0), (0, wide - slots))
    names = jnp.pad(neighbours, pad, constant_values=-1).reshape(rows // 8, 8 * wide)
    weights = jnp.pad(importance, pad).reshape(rows // 8, 8 * wide)
    narrow = (rows, lowered)
    near, far, hidden, slope, agg, base, own_lowered, boards = call(
        local_kernel,
        (shape((rows, rows), BF16), shape((rows, halo), BF16), shape(low, BF16))
        + (shape(low, F32),) * 3
        + (shape(narrow, BF16), shape((rows, LANES), F32)),
        [whole(rows // 8, 8 * wide)] * 2 + [whole(rows, 1)] + [whole(1, width)] * 2 + [ANY] * 4,
        (ANY,) * 7 + (whole(rows, LANES),),
        buffers((low, BF16), ((lowered, width), BF16), ((width, width), BF16))
        + buffers(((width, width), BF16), ((rows, rows), BF16), ((rows, halo), BF16))
        + buffers((low, BF16), (low, BF16), (low, F32), (low, F32), (low, F32), (narrow, BF16))
        + semaphores(9 + 2 * (rows // BLOCK)),
        tokens=(outgoing,),
    )(names, weights, kinds, q_bias_row, w_bias_row, features, proj_board, q_weight, w_weight)

    weight = (1.0 / jnp.sum(importance, axis=1)).reshape(rows, 1)
    w_dims = (width, width)
    far_low, far_narrow = (halo, width), (halo, lowered)
    spot = halo if halo <= rows else BLOCK
    (
        embedding, dpre2, dagg, to_peers, w_sent, w_kept, far_hidden, far_dpre, far_lowered, _,
        w_bias_part,
    ) = call(
        combine_kernel,
        (shape(low, F32), shape(low, BF16), shape(low, BF16))
        + (shape(far_low, BF16), shape(w_dims, BF16), shape(w_dims, BF16))
        + (shape(far_low, BF16), shape(far_low, BF16), shape(far_narrow, BF16))
        + (shape(far_low if spot < halo else (8, LANES), F32), shape((8, width), F32)),
        [SMEM, SMEM, whole(rows, 1), whole(1, width)] + [ANY] * 9,
        (ANY,) * 10 + (whole(8, width),),
        buffers(((rows, halo), BF16), (far_low, BF16), ((lowered, width), BF16))
        + buffers(((width, width), BF16), (low, F32), (low, F32), ((width, width), BF16))
        + buffers((low, BF16), (low, BF16), (low, BF16), (low, BF16), (low, BF16))
        + buffers(((spot, width), BF16), (w_dims, BF16), (w_dims, BF16), ((spot, width), BF16))
        + buffers(((spot, width), F32), ((spot, lowered), BF16))
        + semaphores(15 + 6 * (rows // BLOCK)),
    )(
        live_rows, bits, weight, q_bias_row, far, incoming, proj_board, q_weight, agg, base, w_weight,
        cotangent, hidden,
    )
    returned = lax.all_to_all(to_peers, "dom", split_axis=0, concat_axis=0, tiled=True)

    order = Order()
    w_sum = PieceSum(w_sent, False)
    late_rows = (width + lowered) // 2
    sent_dims, kept_dims = (late_rows + BIAS_ROWS, width), (late_rows, width)
    w_sum.first(order, w_kept)
    dtable, djoined, late_sent, late_kept = order(
        call(
            gradients_kernel,
            (shape(low, BF16), shape(low, BF16))
            + (shape(sent_dims, BF16), shape(kept_dims, BF16)),
            [SMEM, whole(8, width)] + [ANY] * 11,
            (ANY,) * 4,
            buffers(((rows, rows), BF16), (low, BF16), (low, F32), (low, BF16))
            + buffers(((width, width), BF16), (low, BF16), (far_low, BF16))
            + buffers((far_low, BF16), (narrow, BF16), (far_narrow, BF16), ((width, width), BF16))
            + buffers((low, BF16), (low, BF16), (low, BF16), (sent_dims, BF16))
            + buffers((kept_dims, BF16), ((8, width), F32))
            + semaphores(16 + rows // BLOCK),
            moved=200,
        ),
        bits, w_bias_part, near, dagg, slope, dpre2, w_weight, hidden, far_hidden, far_dpre,
        own_lowered, far_lowered, q_weight,
    )
    w_sum.reduce(order)
    late_sum = PieceSum(order(lambda sent: sent, late_sent), True)
    returned = order(lambda value: value, returned)
    late_sum.first(order, late_kept)
    grad_features = order(
        call(
            grad_features_kernel,
            shape(low, F32),
            [whole(1, halo), whole(rows, LANES)] + [ANY] * 6,
            ANY,
            buffers((far_low, BF16), (low, BF16), (low, F32), ((width, width), BF16))
            + buffers((low, BF16), ((lowered, width), BF16))
            + semaphores(5 + 2 * (rows // BLOCK)),
            moved=200,
        ),
        send_row, boards, returned, dtable, slope, q_weight, djoined, proj_board,
    )
    w_sum.reduce(order)
    late_sum.reduce(order)
    w_sum.reduce(order)
    late_sum.reduce(order)
    w_sum.turn(order)
    late_sum.reduce(order)
    w_sum.gather(order)
    late_sum.turn(order)
    w_sum.gather(order)
    late_sum.gather(order)
    w_sum.gather(order)
    late_sum.gather(order)
    late_sum.gather(order)
    w_sum.last(order)
    w_sizes, late_sizes = [width // 16], [width // 32, lowered // 32]
    grad_w = order(lambda b, m: ordered(b, m, w_sizes, False), bits, w_sum.mine)
    (grad_w,) = order(lambda b, m, o: ordered(b, m, w_sizes, True, o), bits, w_sum.other, grad_w)
    late_sum.last(order)
    both = order(lambda b, m: ordered(b, m, late_sizes, False), bits, late_sum.mine)
    grad_q, grad_proj = order(
        lambda b, m, o: ordered(b, m, late_sizes, True, o), bits, late_sum.other, both
    )
    biases = unpack(jnp.where(core == 0, late_sum.mine[late_rows:], late_sum.other[late_rows:]))
    return (embedding, grad_features, grad_proj, grad_q, biases[0], grad_w, biases[1])


def solution(mesh):
    placed = (
        P(("dom", "rep"), None),
        P(("dom", "rep")),
        P(("dom", "rep"), None),
        P(("dom", "rep"), None),
        P(("dom", "rep")),
        P(("dom", "rep")),
        P(),
        P(),
        P(),
        P(),
        P(),
        P(("dom", "rep"), None),
    )
    return jax.shard_map(
        per_device,
        mesh=mesh,
        in_specs=placed,
        out_specs=(P(("dom", "rep"), None), P(("dom", "rep"), None), P(), P(), P(), P(), P()),
        check_vma=False,
    )
```

time: 497 us -> 213 us (0.43)
  waiting for transfers between devices: 216 us -> 64.9 us
  matrix products: 109 us -> 0 us
  Pallas kernels: 0 us -> 94.6 us
  other arithmetic: 55.7 us -> 13.7 us
  blocking collectives: 39.7 us -> 0 us
  local copies, waits for them, and re-layouts: 42.7 us -> 6.46 us
  starting transfers between devices: 13.5 us -> 31.1 us
  between operations: 15.5 us -> 1.86 us
    psum x1 -> x0, waiting for transfers between devices: 203 us -> none  [per_device(): lax.psum((grad_proj, grad_q, grad_q_bias, grad_w, grad_w_bias), ('dom', '...]
    dot_general x15 -> x0, matrix products: 109 us -> none  [the longest x1 41.2 us: per_device(): lax.dot_general(adjacency, dagg, (((0,), (0,)), ((), ())), precision=lax....]
    pallas_call x0 -> x9, Pallas kernels: none -> 94.6 us  [the longest x5 83.3 us: call(): return lambda *operands: built(*operands, *tokens)]
    ppermute x0 -> x20, waiting for transfers between devices: none -> 62.1 us  [the longest x16 56.9 us: cross(): return lax.ppermute(value, ('dom', 'rep'), pairs)]
    reduce_sum x6 -> x1, other arithmetic: 49.9 us -> 0.02 us  [per_device(): weight = (1.0 / jnp.sum(importance, axis=1)).reshape(rows, 1)]
    psum x1 -> x0, blocking collectives: 39.7 us -> none  [per_device(): lax.psum((grad_proj, grad_q, grad_q_bias, grad_w, grad_w_bias), ('dom', '...]
    unnamed x61 -> x25, local copies, waits for them, and re-layouts: 28.7 us -> 1.73 us
    ppermute x0 -> x20, starting transfers between devices: none -> 19.1 us  [the longest x16 18.4 us: cross(): return lax.ppermute(value, ('dom', 'rep'), pairs)]
  transfers between devices with their start and end apart: 3 -> 22, of which waited for: 2 -> 15; matrix products, arithmetic and copies ran while one was open for 16% -> 7% of each run, Pallas kernels for 0% -> 29%
where the time goes in v2:
time: 213 us
  Pallas kernels  94.6 us (44%)
  waiting for transfers between devices  64.9 us (30%)
  starting transfers between devices  31.1 us (15%)
  other arithmetic  13.7 us (6%)
  local copies, waits for them, and re-layouts  6.46 us (3%)
    pallas_call x5, Pallas kernels, call(): return lambda *operands: built(*operands, *tokens)  83.3 us
    ppermute x16, waiting for transfers between devices, cross(): return lax.ppermute(value, ('dom', 'rep'), pairs)  56.9 us
    ppermute x16, starting transfers between devices, cross(): return lax.ppermute(value, ('dom', 'rep'), pairs)  18.4 us
    pallas_call x4, Pallas kernels, ordered(): pl.pallas_call(functools.partial(ordered_kernel, count=len(sizes), other=...  11.3 us
    add x5, other arithmetic, step(): stay = held[:half].astype(F32) + back[:half].astype(F32)  9.77 us
    all_to_all x1, starting transfers between devices, per_device(): lax.all_to_all(outgoing, 'dom', split_axis=0, concat_axis=0, tiled=True)  7.4 us
    ppermute x4, waiting for transfers between devices, swap(): return lax.ppermute(value, axis, [(s, s ^ mask) for s in range(size)])  5.14 us
    all_to_all x1, starting transfers between devices, per_device(): lax.all_to_all(to_peers, 'dom', split_axis=0, concat_axis=0, tiled=True)  4.53 us
  transfers between devices with their start and end apart: 22, of which 15 were waited for; matrix products, arithmetic and copies ran while one was open for 7% of the time, Pallas kernels for 29%

profile of v2, /device:TPU:0, one launch (start us, length us, event | category | flops | bytes accessed | tf_op | source)
XLA Modules:
  0.0 212.6 jit_solution(760183536088984879)
XLA Ops:
  0.6 4.6 %shard_map.171.refs_9_ = bf16[512,1024]{1,0:T(8,128)(2,1)} custom-call(s32[1,512]{1,0:T(1,128)} %bitcast.24, s32[1,1024]{1,0:T(1,128)} %bitcast.21, bf16[1024,1024]{1,0:T(8,128)(2,1)} %refs_5_.1), custom_call_target="tpu_custom_call" | custom-call | tf_op jit(solution)/shard_map/pallas_call | solution.py:63
  5.2 7.4 %all-to-all-start = ((bf16[8,64,1024]{2,1,0:T(8,128)(2,1)}), bf16[8,64,1024]{2,1,0:T(8,128)(2,1)S(1)}, u32[]{:S(2)}, u32[]{:S(2)}) async-start(bf16[8,64,1024]{2,1,0:T(8,128)(2,1)} %bitcast.15), calls=%async_computation | async-start | bytes 2097152 | tf_op jit(solution)/shard_map/all_to_all | solution.py:708
  12.9 0.9 reshape.50.refs_0_
  14.1 0.9 reshape.51.refs_1_
  15.0 1.0 copy.26.refs_2_
  16.0 1.1 copy.27.refs_2_
  17.7 20.7 %shard_map.172 = (bf16[1024,1024]{1,0:T(8,128)(2,1)}, bf16[1024,512]{1,0:T(8,128)(2,1)}, bf16[1024,1024]{1,0:T(8,128)(2,1)}, f32[1024,1024]{1,0:T(8,128)}, f32[1...) custom-call(s32[128,512]{1,0:T(8,128)} %reshape.50.refs_0_, ...), custom_call_target="tpu_custom_call" | custom-call | tf_op jit(solution)/shard_map/pallas_call | solution.py:63
  39.1 1.0 copy-done.1
  40.0 25.5 %shard_map.173 = (f32[1024,1024]{1,0:T(8,128)}, bf16[1024,1024]{1,0:T(8,128)(2,1)}, bf16[1024,1024]{1,0:T(8,128)(2,1)}, bf16[512,1024]{1,0:T(8,128)(2,1)}, bf16[...) custom-call(s32[1]{0:T(128)S(6)} %copy.42.refs_0_, ...), custom_call_target="tpu_custom_call" | custom-call | tf_op jit(solution)/shard_map/pallas_call | solution.py:63
  65.6 4.4 %collective-permute-done = bf16[1024,1024]{1,0:T(8,128)(2,1)S(1)} collective-permute-done((bf16[1024,1024]{1,0:T(8,128)(2,1)}, bf16[1024,1024]{1,0:T(8,128)(2,1)S(1)}, u32[]{:S(2)}, u32[]{:S(2)}) %collective-permute-start) | collective-permute-done | bytes 2097184 | tf_op jit(solution)/shard_map/ppermute | solution.py:521
  70.0 3.4 %convert_add_fusion = (f32[512,1024]{1,0:T(8,128)S(1)}, bf16[512,1024]{1,0:T(8,128)(2,1)}) fusion(bf16[1024,1024]{1,0:T(8,128)(2,1)S(1)} %collective-permute-done, bf16[1024,1024]{1,0:T(8,128)(2,1)} %get-tuple-element.127), kind=kLoop, calls=%fused_computation | loop fusion | flops 3670016 | bytes 7340032 | tf_op jit(solution)/shard_map/add | solution.py:583
  73.4 2.0 collective-permute-start.1
  75.5 4.5 %all-to-all-start.1 = ((bf16[8,64,1024]{2,1,0:T(8,128)(2,1)}), bf16[8,64,1024]{2,1,0:T(8,128)(2,1)S(1)}, u32[]{:S(2)}, u32[]{:S(2)}) async-start(bf16[8,64,1024]{2,1,0:T(8,128)(2,1)} %bitcast.18), calls=%async_computation.1 | async-start | bytes 2097152 | tf_op jit(solution)/shard_map/all_to_all | solution.py:754
  80.0 19.7 %shard_map.174 = (bf16[1024,1024]{1,0:T(8,128)(2,1)}, bf16[1024,1024]{1,0:T(8,128)(2,1)}, bf16[784,1024]{1,0:T(8,128)(2,1)}, bf16[768,1024]{1,0:T(8,128)(2,1)}) custom-call(s32[3]{0:T(128)} %pad_add_fusion.refs_1_.refs_0_.bits, f32[8,1024]{1,0:T(8,128)} %get-tuple-element.130.refs_1_, bf16[1024,1024]{1,0:T(8,128)(2,1)} %get-tuple-element.131.refs_2_, ...), custom_call_target="tpu_custom_call" | custom-call | bytes 209715200 | tf_op jit(solution)/shard_map/pallas_call | solution.py:63
  99.7 2.7 %convert_add_fusion.2 = (f32[256,1024]{1,0:T(8,128)}, bf16[256,1024]{1,0:T(8,128)(2,1)}) fusion(f32[512,1024]{1,0:T(8,128)S(1)} %get-tuple-element.144, bf16[512,1024]{1,0:T(8,128)(2,1)} %collective-permute-done.1), kind=kLoop, calls=%fused_computation.4 | loop fusion | flops 1310720 | bytes 4718592 | tf_op jit(solution)/shard_map/add | solution.py:583
  102.9 1.0 collective-permute-start.4
  103.9 2.8 %all-to-all-done.1 = bf16[8,64,1024]{2,1,0:T(8,128)(2,1)S(1)} async-done(((bf16[8,64,1024]{2,1,0:T(8,128)(2,1)}), bf16[8,64,1024]{2,1,0:T(8,128)(2,1)S(1)}, u32[]{:S(2)}, u32[]{:S(2)}) %all-to-all-start.1) | async-done | bytes 1048608 | tf_op jit(solution)/shard_map/all_to_all | solution.py:754
  106.7 0.8 slice_convert_fusion.5
  107.5 0.8 slice_convert_fusion.4
  108.3 2.5 %convert_add_fusion.1 = (f32[384,1024]{1,0:T(8,128)S(1)}, bf16[384,1024]{1,0:T(8,128)(2,1)S(1)}) fusion(bf16[784,1024]{1,0:T(8,128)(2,1)} %collective-permute-done.2, bf16[768,1024]{1,0:T(8,128)(2,1)} %get-tuple-element.150), kind=kLoop, calls=%fused_computation.2 | loop fusion | flops 2752512 | bytes 5505024 | tf_op jit(solution)/shard_map/add | solution.py:583
  110.8 1.0 pad_maximum_fusion
  111.8 1.5 collective-permute-start.3
  113.3 12.8 %shard_map.175 = f32[1024,1024]{1,0:T(8,128)} custom-call(s32[1,512]{1,0:T(1,128)} %bitcast.25, f32[1024,128]{1,0:T(8,128)} %get-tuple-element.154.refs_1_, bf16[512,1024]{1,0:T(8,128)(2,1)} %bitcast.17, bf16[1024,1024]{1,0:T(8,128)(2,1)} %get-tuple-element.156.refs_3_, f32[1024,1024]{1,0:T(8,128)} %get-tuple-element.157.refs_4_, ...), custom_call_target="tpu_custom_call" | custom-call | bytes 209715200 | tf_op jit(solution)/shard_map/pallas_call | solution.py:63
  126.1 1.2 convert_add_fusion.4
  128.3 1.6 collective-permute-start.5
  129.9 5.3 %collective-permute-done.6 = bf16[128,1024]{1,0:T(8,128)(2,1)S(1)} collective-permute-done((bf16[128,1024]{1,0:T(8,128)(2,1)S(1)}, bf16[128,1024]{1,0:T(8,128)(2,1)S(1)}, u32[]{:S(2)}, u32[]{:S(2)}) %collective-permute-start.6) | collective-permute-done | bytes 262176 | tf_op jit(solution)/shard_map/ppermute | solution.py:541
  135.3 1.8 collective-permute-start.8
  137.4 2.5 %collective-permute-start.7 = (bf16[112,1024]{1,0:T(8,128)(2,1)S(1)}, bf16[112,1024]{1,0:T(8,128)(2,1)S(1)}, u32[]{:S(2)}, u32[]{:S(2)}) collective-permute-start(bf16[112,1024]{1,0:T(8,128)(2,1)S(1)} %pad_maximum_fusion.2), channel_id=1, source_target_pairs={{0,8},{1,17},{2,10},{3,19},{4,12},{5,21},{6,14},{7,23},{8,0},{9,25... | collective-permute-start | bytes 688136 | tf_op jit(solution)/shard_map/ppermute | solution.py:541
  139.9 6.3 %collective-permute-done.8 = bf16[64,1024]{1,0:T(8,128)(2,1)S(1)} collective-permute-done((bf16[64,1024]{1,0:T(8,128)(2,1)S(1)}, bf16[64,1024]{1,0:T(8,128)(2,1)S(1)}, u32[]{:S(2)}, u32[]{:S(2)}) %collective-permute-start.8) | collective-permute-done | bytes 131104 | tf_op jit(solution)/shard_map/ppermute | solution.py:541
  146.3 1.5 collective-permute-done.7
  147.9 1.6 collective-permute-start.9
  149.6 9.1 %collective-permute-done.10 = bf16[64,1024]{1,0:T(8,128)(2,1)S(1)} collective-permute-done((bf16[64,1024]{1,0:T(8,128)(2,1)S(1)}, bf16[64,1024]{1,0:T(8,128)(2,1)S(1)}, u32[]{:S(2)}, u32[]{:S(2)}) %collective-permute-start.10) | collective-permute-done | bytes 131104 | tf_op jit(solution)/shard_map/ppermute | solution.py:541
  158.8 2.7 %collective-permute-done.9 = bf16[64,1024]{1,0:T(8,128)(2,1)S(1)} collective-permute-done((bf16[64,1024]{1,0:T(8,128)(2,1)S(1)}, bf16[64,1024]{1,0:T(8,128)(2,1)S(1)}, u32[]{:S(2)}, u32[]{:S(2)}) %collective-permute-start.9) | collective-permute-done | bytes 131104 | tf_op jit(solution)/shard_map/ppermute | solution.py:541
  161.6 4.1 %collective-permute-done.12 = bf16[128,1024]{1,0:T(8,128)(2,1)S(1)} collective-permute-done((bf16[128,1024]{1,0:T(8,128)(2,1)S(1)}, bf16[128,1024]{1,0:T(8,128)(2,1)S(1)}, u32[]{:S(2)}, u32[]{:S(2)}) %collective-permute-start.12) | collective-permute-done | bytes 262176 | tf_op jit(solution)/shard_map/ppermute | solution.py:541
  165.8 2.2 %collective-permute-start.11 = (bf16[48,1024]{1,0:T(8,128)(2,1)S(1)}, bf16[48,1024]{1,0:T(8,128)(2,1)S(1)}, u32[]{:S(2)}, u32[]{:S(2)}) collective-permute-start(bf16[48,1024]{1,0:T(8,128)(2,1)S(1)} %add_convert_fusion.8), channel_id=1, source_target_pairs={{0,16},{1,9},{2,18},{3,11},{4,20},{5,13},{6,22},{7,15},{8,24},{9,1... | collective-permute-start | bytes 294920 | tf_op jit(solution)/shard_map/ppermute | solution.py:541
  168.0 6.4 %collective-permute-done.11 = bf16[48,1024]{1,0:T(8,128)(2,1)S(1)} collective-permute-done((bf16[48,1024]{1,0:T(8,128)(2,1)S(1)}, bf16[48,1024]{1,0:T(8,128)(2,1)S(1)}, u32[]{:S(2)}, u32[]{:S(2)}) %collective-permute-start.11) | collective-permute-done | bytes 98336 | tf_op jit(solution)/shard_map/ppermute | solution.py:541
  174.5 2.4 %collective-permute-done.14 = bf16[256,1024]{1,0:T(8,128)(2,1)S(1)} collective-permute-done((bf16[256,1024]{1,0:T(8,128)(2,1)S(1)}, bf16[256,1024]{1,0:T(8,128)(2,1)S(1)}, u32[]{:S(2)}, u32[]{:S(2)}) %collective-permute-start.14) | collective-permute-done | bytes 524320 | tf_op jit(solution)/shard_map/ppermute | solution.py:541
  177.1 3.1 %collective-permute-done.13 = bf16[96,1024]{1,0:T(8,128)(2,1)S(1)} collective-permute-done((bf16[96,1024]{1,0:T(8,128)(2,1)S(1)}, bf16[96,1024]{1,0:T(8,128)(2,1)S(1)}, u32[]{:S(2)}, u32[]{:S(2)}) %collective-permute-start.13) | collective-permute-done | bytes 196640 | tf_op jit(solution)/shard_map/ppermute | solution.py:541
  180.2 1.7 collective-permute-start.15
  182.0 8.5 %collective-permute-done.15 = bf16[192,1024]{1,0:T(8,128)(2,1)S(1)} collective-permute-done((bf16[192,1024]{1,0:T(8,128)(2,1)S(1)}, bf16[192,1024]{1,0:T(8,128)(2,1)S(1)}, u32[]{:S(2)}, u32[]{:S(2)}) %collective-permute-start.15) | collective-permute-done | bytes 393248 | tf_op jit(solution)/shard_map/ppermute | solution.py:541
  190.5 2.9 %collective-permute-done.17 = bf16[512,1024]{1,0:T(8,128)(2,1)S(1)} collective-permute-done((bf16[512,1024]{1,0:T(8,128)(2,1)S(1)}, bf16[512,1024]{1,0:T(8,128)(2,1)S(1)}, u32[]{:S(2)}, u32[]{:S(2)}) %collective-permute-start.17) | collective-permute-done | bytes 1048608 | tf_op jit(solution)/shard_map/ppermute | solution.py:541
  193.6 1.3 collective-permute-start.16
  195.0 3.0 %shard_map.176.refs_0_ = f32[2048,1024]{1,0:T(8,128)} custom-call(s32[3]{0:T(128)S(1)} %copy-done, bf16[1024,1024]{1,0:T(8,128)(2,1)S(1)} %constant_dynamic-update-slice_fusion.12.held), custom_call_target="tpu_custom_call" | custom-call | bytes 209715200 | tf_op jit(solution)/shard_map/pallas_call | solution.py:501
  198.0 3.0 %shard_map.177 = f32[2048,1024]{1,0:T(8,128)} custom-call(s32[3]{0:T(128)S(1)} %copy-done, bf16[1024,1024]{1,0:T(8,128)(2,1)S(1)} %collective-permute-done.18.held, f32[2048,1024]{1,0:T(8,128)} %shard_map.176.refs_0_), custom_call_target="tpu_custom_call", output_to_operand_aliasing={{}: (2, {})} | custom-call | bytes 209715200 | tf_op jit(solution)/shard_map/pallas_call | solution.py:501
  201.0 4.7 %collective-permute-done.16 = bf16[384,1024]{1,0:T(8,128)(2,1)S(1)} collective-permute-done((bf16[384,1024]{1,0:T(8,128)(2,1)S(1)}, bf16[384,1024]{1,0:T(8,128)(2,1)S(1)}, u32[]{:S(2)}, u32[]{:S(2)}) %collective-permute-start.16) | collective-permute-done | bytes 786464 | tf_op jit(solution)/shard_map/ppermute | solution.py:541
  205.9 2.7 %shard_map.178 = (f32[1024,1024]{1,0:T(8,128)}, f32[512,1024]{1,0:T(8,128)}) custom-call(s32[3]{0:T(128)S(1)} %copy-done, bf16[784,1024]{1,0:T(8,128)(2,1)S(1)} %constant_dynamic-update-slice_fusion.14.held), custom_call_target="tpu_custom_call" | custom-call | bytes 209715200 | tf_op jit(solution)/shard_map/pallas_call | solution.py:501
  208.5 0.8 collective-permute-done.19.held
  210.0 2.7 %shard_map.179 = (f32[1024,1024]{1,0:T(8,128)}, f32[512,1024]{1,0:T(8,128)}) custom-call(s32[3]{0:T(128)S(1)} %copy-done, bf16[784,1024]{1,0:T(8,128)(2,1)S(1)} %collective-permute-done.19.held, f32[1024,1024]{1,0:T(8,128)} %get-tuple-element.207.refs_0_, f32[512,1024]{1,0:T(8,128)} %get-tuple-element.208.refs_1_), custom_call_target="tpu_custom_call", output_to_operand_aliasing={{0}: (2, {}), {1}: (3, {})} | custom-call | bytes 209715200 | tf_op jit(solution)/shard_map/pallas_call | solution.py:501
  (91 shorter events, 4.9 us)
Async XLA Ops:
  0.6 12.0 %copy-start.5 = (s32[1024,50]{0,1:T(8,128)S(1)}, s32[1024,50]{0,1:T(8,128)}, u32[]{:S(2)}) copy-start(s32[1024,50]{0,1:T(8,128)} %param.14) | copy-start | bytes 614404
  5.2 8.6 %copy-start.4 = (f32[1024,50]{0,1:T(8,128)S(1)}, f32[1024,50]{0,1:T(8,128)}, u32[]{:S(2)}) copy-start(f32[1024,50]{0,1:T(8,128)} %param.15) | copy-start | bytes 614404
  5.2 33.8 %all-to-all-start = ((bf16[8,64,1024]{2,1,0:T(8,128)(2,1)}), bf16[8,64,1024]{2,1,0:T(8,128)(2,1)S(1)}, u32[]{:S(2)}, u32[]{:S(2)}) async-start(bf16[8,64,1024]{2,1,0:T(8,128)(2,1)} %bitcast.15), calls=%async_computation | async-start | bytes 2097152 | tf_op jit(solution)/shard_map/all_to_all | solution.py:708
  12.9 2.1 copy-start.6
  39.1 1.0 copy-start.1
  65.6 4.4 %collective-permute-start = (bf16[1024,1024]{1,0:T(8,128)(2,1)}, bf16[1024,1024]{1,0:T(8,128)(2,1)S(1)}, u32[]{:S(2)}, u32[]{:S(2)}) collective-permute-start(bf16[1024,1024]{1,0:T(8,128)(2,1)} %get-tuple-element.126), channel_id=1, source_target_pairs={{0,1},{1,0},{2,3},{3,2},{4,5},{5,4},{6,7},{7,6},{8,9},{9,8},{10,11... | collective-permute-start | bytes 6291464 | tf_op jit(solution)/shard_map/ppermute | solution.py:521
  73.4 26.3 %collective-permute-start.1 = (bf16[512,1024]{1,0:T(8,128)(2,1)}, bf16[512,1024]{1,0:T(8,128)(2,1)}, u32[]{:S(2)}, u32[]{:S(2)}) collective-permute-start(bf16[512,1024]{1,0:T(8,128)(2,1)} %get-tuple-element.222), channel_id=1, source_target_pairs={{0,4},{1,3},{2,6},{3,1},{4,0},{5,7},{6,2},{7,5},{8,12},{9,11},{10,... | collective-permute-start | bytes 3145736 | tf_op jit(solution)/shard_map/ppermute | solution.py:541
  75.5 31.3 %all-to-all-start.1 = ((bf16[8,64,1024]{2,1,0:T(8,128)(2,1)}), bf16[8,64,1024]{2,1,0:T(8,128)(2,1)S(1)}, u32[]{:S(2)}, u32[]{:S(2)}) async-start(bf16[8,64,1024]{2,1,0:T(8,128)(2,1)} %bitcast.18), calls=%async_computation.1 | async-start | bytes 2097152 | tf_op jit(solution)/shard_map/all_to_all | solution.py:754
  102.4 5.1 %collective-permute-start.2 = (bf16[784,1024]{1,0:T(8,128)(2,1)}, bf16[784,1024]{1,0:T(8,128)(2,1)}, u32[]{:S(2)}, u32[]{:S(2)}) collective-permute-start(bf16[784,1024]{1,0:T(8,128)(2,1)} %get-tuple-element.146), channel_id=1, source_target_pairs={{0,1},{1,0},{2,3},{3,2},{4,5},{5,4},{6,7},{7,6},{8,9},{9,8},{10,11... | collective-permute-start | bytes 4816904 | tf_op jit(solution)/shard_map/ppermute | solution.py:521
  102.9 23.2 %collective-permute-start.4 = (bf16[256,1024]{1,0:T(8,128)(2,1)}, bf16[256,1024]{1,0:T(8,128)(2,1)}, u32[]{:S(2)}, u32[]{:S(2)}) collective-permute-start(bf16[256,1024]{1,0:T(8,128)(2,1)} %get-tuple-element.226), channel_id=1, source_target_pairs={{0,2},{1,5},{2,0},{3,7},{4,6},{5,1},{6,4},{7,3},{8,10},{9,13},{10,... | collective-permute-start | bytes 1572872 | tf_op jit(solution)/shard_map/ppermute | solution.py:541
  106.7 4.0 %copy-start.2 = (bf16[8,64,1024]{2,1,0:T(8,128)(2,1)}, bf16[8,64,1024]{2,1,0:T(8,128)(2,1)S(1)}, u32[]{:S(2)}) copy-start(bf16[8,64,1024]{2,1,0:T(8,128)(2,1)S(1)} %all-to-all-done.1) | copy-start | bytes 3145732
  111.8 16.2 %collective-permute-start.3 = (bf16[400,1024]{1,0:T(8,128)(2,1)}, bf16[400,1024]{1,0:T(8,128)(2,1)S(1)}, u32[]{:S(2)}, u32[]{:S(2)}) collective-permute-start(bf16[400,1024]{1,0:T(8,128)(2,1)} %pad_maximum_fusion), channel_id=1, source_target_pairs={{0,4},{1,3},{2,6},{3,1},{4,0},{5,7},{6,2},{7,5},{8,12},{9,11},{10,... | collective-permute-start | bytes 2457608 | tf_op jit(solution)/shard_map/ppermute | solution.py:541
  113.3 12.8 %copy-start.3 = (f32[256,1024]{1,0:T(8,128)S(1)}, f32[256,1024]{1,0:T(8,128)}, u32[]{:S(2)}) copy-start(f32[256,1024]{1,0:T(8,128)} %get-tuple-element.161) | copy-start | bytes 3145732
  127.3 8.0 %collective-permute-start.6 = (bf16[128,1024]{1,0:T(8,128)(2,1)S(1)}, bf16[128,1024]{1,0:T(8,128)(2,1)S(1)}, u32[]{:S(2)}, u32[]{:S(2)}) collective-permute-start(bf16[128,1024]{1,0:T(8,128)(2,1)S(1)} %get-tuple-element.230), channel_id=1, source_target_pairs={{0,8},{1,17},{2,10},{3,19},{4,12},{5,21},{6,14},{7,23},{8,0},{9,25... | collective-permute-start | bytes 786440 | tf_op jit(solution)/shard_map/ppermute | solution.py:541
  128.3 8.9 %collective-permute-start.5 = (bf16[208,1024]{1,0:T(8,128)(2,1)S(1)}, bf16[208,1024]{1,0:T(8,128)(2,1)S(1)}, u32[]{:S(2)}, u32[]{:S(2)}) collective-permute-start(bf16[208,1024]{1,0:T(8,128)(2,1)S(1)} %pad_maximum_fusion.1), channel_id=1, source_target_pairs={{0,2},{1,5},{2,0},{3,7},{4,6},{5,1},{6,4},{7,3},{8,10},{9,13},{10,... | collective-permute-start | bytes 1277960 | tf_op jit(solution)/shard_map/ppermute | solution.py:541
  135.3 10.8 %collective-permute-start.8 = (bf16[64,1024]{1,0:T(8,128)(2,1)S(1)}, bf16[64,1024]{1,0:T(8,128)(2,1)S(1)}, u32[]{:S(2)}, u32[]{:S(2)}) collective-permute-start(bf16[64,1024]{1,0:T(8,128)(2,1)S(1)} %get-tuple-element.234), channel_id=1, source_target_pairs={{0,16},{1,9},{2,18},{3,11},{4,20},{5,13},{6,22},{7,15},{8,24},{9,1... | collective-permute-start | bytes 393224 | tf_op jit(solution)/shard_map/ppermute | solution.py:541
  137.4 10.4 %collective-permute-start.7 = (bf16[112,1024]{1,0:T(8,128)(2,1)S(1)}, bf16[112,1024]{1,0:T(8,128)(2,1)S(1)}, u32[]{:S(2)}, u32[]{:S(2)}) collective-permute-start(bf16[112,1024]{1,0:T(8,128)(2,1)S(1)} %pad_maximum_fusion.2), channel_id=1, source_target_pairs={{0,8},{1,17},{2,10},{3,19},{4,12},{5,21},{6,14},{7,23},{8,0},{9,25... | collective-permute-start | bytes 688136 | tf_op jit(solution)/shard_map/ppermute | solution.py:541
  146.2 12.5 %collective-permute-start.10 = (bf16[64,1024]{1,0:T(8,128)(2,1)S(1)}, bf16[64,1024]{1,0:T(8,128)(2,1)S(1)}, u32[]{:S(2)}, u32[]{:S(2)}) collective-permute-start(bf16[64,1024]{1,0:T(8,128)(2,1)S(1)} %add_convert_fusion.6), channel_id=1, source_target_pairs={{0,16},{1,9},{2,18},{3,11},{4,20},{5,13},{6,22},{7,15},{8,24},{9,1... | collective-permute-start | bytes 393224 | tf_op jit(solution)/shard_map/ppermute | solution.py:541
  147.9 13.6 %collective-permute-start.9 = (bf16[64,1024]{1,0:T(8,128)(2,1)S(1)}, bf16[64,1024]{1,0:T(8,128)(2,1)S(1)}, u32[]{:S(2)}, u32[]{:S(2)}) collective-permute-start(bf16[64,1024]{1,0:T(8,128)(2,1)S(1)} %pad_maximum_fusion.3), channel_id=1, source_target_pairs={{0,16},{1,9},{2,18},{3,11},{4,20},{5,13},{6,22},{7,15},{8,24},{9,1... | collective-permute-start | bytes 393224 | tf_op jit(solution)/shard_map/ppermute | solution.py:541
  158.8 6.9 %collective-permute-start.12 = (bf16[128,1024]{1,0:T(8,128)(2,1)S(1)}, bf16[128,1024]{1,0:T(8,128)(2,1)S(1)}, u32[]{:S(2)}, u32[]{:S(2)}) collective-permute-start(bf16[128,1024]{1,0:T(8,128)(2,1)S(1)} %constant_dynamic-update-slice_fusion), channel_id=1, source_target_pairs={{0,8},{1,17},{2,10},{3,19},{4,12},{5,21},{6,14},{7,23},{8,0},{9,25... | collective-permute-start | bytes 786440 | tf_op jit(solution)/shard_map/ppermute | solution.py:541
  165.8 11.2 %collective-permute-start.14 = (bf16[256,1024]{1,0:T(8,128)(2,1)S(1)}, bf16[256,1024]{1,0:T(8,128)(2,1)S(1)}, u32[]{:S(2)}, u32[]{:S(2)}) collective-permute-start(bf16[256,1024]{1,0:T(8,128)(2,1)S(1)} %constant_dynamic-update-slice_fusion.2), channel_id=1, source_target_pairs={{0,2},{1,5},{2,0},{3,7},{4,6},{5,1},{6,4},{7,3},{8,10},{9,13},{10,... | collective-permute-start | bytes 1572872 | tf_op jit(solution)/shard_map/ppermute | solution.py:541
  165.8 8.6 %collective-permute-start.11 = (bf16[48,1024]{1,0:T(8,128)(2,1)S(1)}, bf16[48,1024]{1,0:T(8,128)(2,1)S(1)}, u32[]{:S(2)}, u32[]{:S(2)}) collective-permute-start(bf16[48,1024]{1,0:T(8,128)(2,1)S(1)} %add_convert_fusion.8), channel_id=1, source_target_pairs={{0,16},{1,9},{2,18},{3,11},{4,20},{5,13},{6,22},{7,15},{8,24},{9,1... | collective-permute-start | bytes 294920 | tf_op jit(solution)/shard_map/ppermute | solution.py:541
  174.4 5.7 %collective-permute-start.13 = (bf16[96,1024]{1,0:T(8,128)(2,1)S(1)}, bf16[96,1024]{1,0:T(8,128)(2,1)S(1)}, u32[]{:S(2)}, u32[]{:S(2)}) collective-permute-start(bf16[96,1024]{1,0:T(8,128)(2,1)S(1)} %constant_dynamic-update-slice_fusion.4), channel_id=1, source_target_pairs={{0,8},{1,17},{2,10},{3,19},{4,12},{5,21},{6,14},{7,23},{8,0},{9,25... | collective-permute-start | bytes 589832 | tf_op jit(solution)/shard_map/ppermute | solution.py:541
  177.0 16.4 %collective-permute-start.17 = (bf16[512,1024]{1,0:T(8,128)(2,1)S(1)}, bf16[512,1024]{1,0:T(8,128)(2,1)S(1)}, u32[]{:S(2)}, u32[]{:S(2)}) collective-permute-start(bf16[512,1024]{1,0:T(8,128)(2,1)S(1)} %constant_dynamic-update-slice_fusion.6), channel_id=1, source_target_pairs={{0,4},{1,3},{2,6},{3,1},{4,0},{5,7},{6,2},{7,5},{8,12},{9,11},{10,... | collective-permute-start | bytes 3145736 | tf_op jit(solution)/shard_map/ppermute | solution.py:541
  180.2 10.2 %collective-permute-start.15 = (bf16[192,1024]{1,0:T(8,128)(2,1)S(1)}, bf16[192,1024]{1,0:T(8,128)(2,1)S(1)}, u32[]{:S(2)}, u32[]{:S(2)}) collective-permute-start(bf16[192,1024]{1,0:T(8,128)(2,1)S(1)} %constant_dynamic-update-slice_fusion.8), channel_id=1, source_target_pairs={{0,2},{1,5},{2,0},{3,7},{4,6},{5,1},{6,4},{7,3},{8,10},{9,13},{10,... | collective-permute-start | bytes 1179656 | tf_op jit(solution)/shard_map/ppermute | solution.py:541
  190.5 4.5 %copy-start = (s32[3]{0:T(128)S(1)}, s32[3]{0:T(128)}, u32[]{:S(2)}) copy-start(s32[3]{0:T(128)} %pad_add_fusion.refs_1_.refs_0_.bits) | copy-start | bytes 40
  193.5 4.5 %collective-permute-start.18 = (bf16[1024,1024]{1,0:T(8,128)(2,1)S(1)}, bf16[1024,1024]{1,0:T(8,128)(2,1)S(1)}, u32[]{:S(2)}, u32[]{:S(2)}) collective-permute-start(bf16[1024,1024]{1,0:T(8,128)(2,1)S(1)} %constant_dynamic-update-slice_fusion.12.held), channel_id=1, source_target_pairs={{0,1},{1,0},{2,3},{3,2},{4,5},{5,4},{6,7},{7,6},{8,9},{9,8},{10,11... | collective-permute-start | bytes 6291464 | tf_op jit(solution)/shard_map/ppermute | solution.py:521
  193.6 12.1 %collective-permute-start.16 = (bf16[384,1024]{1,0:T(8,128)(2,1)S(1)}, bf16[384,1024]{1,0:T(8,128)(2,1)S(1)}, u32[]{:S(2)}, u32[]{:S(2)}) collective-permute-start(bf16[384,1024]{1,0:T(8,128)(2,1)S(1)} %constant_dynamic-update-slice_fusion.10), channel_id=1, source_target_pairs={{0,4},{1,3},{2,6},{3,1},{4,0},{5,7},{6,2},{7,5},{8,12},{9,11},{10,... | collective-permute-start | bytes 2359304 | tf_op jit(solution)/shard_map/ppermute | solution.py:541
  205.8 3.5 %collective-permute-start.19 = (bf16[784,1024]{1,0:T(8,128)(2,1)S(1)}, bf16[784,1024]{1,0:T(8,128)(2,1)S(1)}, u32[]{:S(2)}, u32[]{:S(2)}) collective-permute-start(bf16[784,1024]{1,0:T(8,128)(2,1)S(1)} %constant_dynamic-update-slice_fusion.14.held), channel_id=1, source_target_pairs={{0,1},{1,0},{2,3},{3,2},{4,5},{5,4},{6,7},{7,6},{8,9},{9,8},{10,11... | collective-permute-start | bytes 4816904 | tf_op jit(solution)/shard_map/ppermute | solution.py:521

commit v3 on v2

--- a/solution.py
+++ b/solution.py
@@ -10,7 +10,7 @@
 F32 = jnp.float32
 BF16 = jnp.bfloat16
 LANES = 128
-BLOCK = 256
+BLOCK = 512
 MEGA = 1024 * 1024
 MARK = 64.0
 PLACES = 16
@@ -200,7 +200,7 @@
 
     def local(step):
         here = rows_of(step)
-        agg[here] = dot(near[here], active[...])
+        agg[here] = dot(near[here], active[...]).astype(BF16)
         agg_out(step).start()
         base[here] = dot(hidden[here], w_top[...]) + w_bias[...]
         base_out(step).start()
@@ -230,7 +230,7 @@
     got_base = copies.by_blocks(base_hbm, base)
     got_cotangent = copies.by_blocks(cotangent_hbm, cotangent)
     got_hidden = copies.start(hidden_hbm, hidden)
-    embedding = agg
+    embedding = base
     embedding_out = copies.by_blocks(embedding, embedding_hbm, start=False)
     dpre2_out = copies.by_blocks(dpre2, dpre2_hbm, start=False)
     dagg_out = copies.by_blocks(dagg, dagg_hbm, start=False)
@@ -279,7 +279,8 @@
     def node_block(step):
         here = rows_of(step)
         got_agg(step).wait()
-        average = ((agg[here] + dot(far[here], active[...])) * weight[here]).astype(BF16)
+        total = agg[here].astype(F32) + dot(far[here], active[...])
+        average = (total * weight[here]).astype(BF16)
         mean[here] = average
         got_base(step).wait()
         pre = base[here] + dot(average, w_low[...])
@@ -301,21 +302,6 @@
             out(step).start()
 
     each_block(count, node_block)
-    got_hidden.wait()
-
-    stride = width // PLACES
-
-    @pl.when(bits[0] == 1)
-    def _():
-        write_pieces(bits[2], [(hidden, 0, dpre2)], width, w_sent, stride, 0)
-        write_pieces(bits[1], [(mean, 0, dpre2)], width, w_kept, stride, 0)
-
-    @pl.when(bits[0] == 0)
-    def _():
-        write_pieces(bits[2], [(mean, 0, dpre2)], width, w_sent, stride, 0)
-        write_pieces(bits[1], [(hidden, 0, dpre2)], width, w_kept, stride, 0)
-
-    far_out += [copies.start(w_sent, w_sent_hbm), copies.start(w_kept, w_kept_hbm)]
     far_dpre = far_hidden
     if held:
         far_out.pop(0).wait()
@@ -334,6 +320,19 @@
     each_block(far.shape[1] // BLOCK, peer_block)
     if held:
         far_out += [copies.start(to_peers, to_peers_hbm), copies.start(far_dpre, far_dpre_hbm)]
+    got_hidden.wait()
+    stride = width // PLACES
+    for target, target_hbm, mark, low in ((w_sent, w_sent_hbm, 2, 1), (w_kept, w_kept_hbm, 1, 0)):
+
+        @pl.when(bits[0] == low)
+        def _():
+            write_pieces(bits[mark], [(hidden, 0, dpre2)], width, target, stride, 0)
+
+        @pl.when(bits[0] != low)
+        def _():
+            write_pieces(bits[mark], [(mean, 0, dpre2)], width, target, stride, 0)
+
+        far_out += [copies.start(target, target_hbm)]
     for copy in far_out:
         copy.wait()
     for out in outs:
@@ -406,29 +405,34 @@
 
     each_block(far_dpre.shape[0] // BLOCK, far_block)
     stride = (half + depth // 2) // PLACES
-    sides = ((sent, 1 - bits[0], bits[2]), (kept, bits[0], bits[1]))
-    for target, side, mark in sides:
+    sides = ((sent, sent_hbm, 1 - bits[0], bits[2]), (kept, kept_hbm, bits[0], bits[1]))
+
+    def write_q(target, side, mark):
         first = side * half
         pairs = [(hidden, first, dpre), (far_hidden, first, far_dpre)]
         write_pieces(mark, pairs, half, target, stride, 0)
-    for copy in got_joined:
-        copy.wait()
-
-    def joined_block(step):
-        here = rows_of(step)
-        djoined[here] = contract_cols(dpre2[here], w_top[...]).astype(BF16)
-
-    each_block(count, joined_block)
-    out += [copies.start(djoined, djoined_hbm)]
-    for copy in got_p:
-        copy.wait()
-    for target, side, mark in sides:
+
+    def write_p(target, side, mark):
         here = pl.ds(pl.multiple_of(side * (depth // 2), depth // 2), depth // 2)
         part = lowered[:, here]
         through = contract_rows(part, dpre[...]) + contract_rows(far_lowered[:, here], far_dpre[...])
         product = contract_cols(through.astype(BF16), q_weight[...])
         product += contract_rows(part, djoined[...])
         write_block(mark, product, 0, target, stride, half // PLACES, depth // 2 // PLACES)
+
+    write_q(sent, *sides[0][2:])
+    for copy in got_joined:
+        copy.wait()
+
+    def joined_block(step):
+        here = rows_of(step)
+        djoined[here] = contract_cols(dpre2[here], w_top[...]).astype(BF16)
+
+    each_block(count, joined_block)
+    out += [copies.start(djoined, djoined_hbm)]
+    for copy in got_p:
+        copy.wait()
+    write_p(sent, *sides[0][2:])
     row = lax.broadcasted_iota(jnp.int32, (BIAS_ROWS, 1), 0)
     block = jnp.zeros((BIAS_ROWS, width), F32)
     for i, part in enumerate((bias, w_bias)):
@@ -436,7 +440,10 @@
         high = total.astype(BF16).astype(F32)
         block = jnp.where(row == i, high, jnp.where(row == i + 2, total - high, block))
     sent[sent.shape[0] - BIAS_ROWS :] = block.astype(BF16)
-    out += [copies.start(sent, sent_hbm), copies.start(kept, kept_hbm)]
+    out += [copies.start(sent, sent_hbm)]
+    write_q(kept, *sides[1][2:])
+    write_p(kept, *sides[1][2:])
+    out += [copies.start(kept, kept_hbm)]
     for copy in out:
         copy.wait()
 
@@ -450,21 +457,29 @@
     lowered = proj.shape[0]
     count = rows // BLOCK
     got = [copies.start(returned_hbm, returned), copies.start(dtable_hbm, dtable)]
-    got += [copies.start(q_hbm, q_weight)]
+    for copy in got:
+        copy.wait()
     got_slope = copies.by_blocks(slope_hbm, slope)
-    got += [copies.start(djoined_hbm, djoined), copies.start(proj_hbm, proj)]
+    got = [copies.start(q_hbm, q_weight), copies.start(djoined_hbm, djoined)]
+    got += [copies.start(proj_hbm, proj)]
     grad_out = copies.by_blocks(slope, grad_hbm, start=False)
-    for copy in got:
-        copy.wait()
-
-    def block(step):
+
+    def own_block(step):
         here = rows_of(step)
         row = lax.broadcasted_iota(jnp.int32, (BLOCK, send.shape[1]), 0) + step * BLOCK
         hot = jnp.where(row == send[...], 1.0, 0.0).astype(BF16)
         owned = dtable[here].astype(F32) + dot(hot, returned[...])
         got_slope(step).wait()
-        dpre = (owned * slope[here]).astype(BF16)
-        low = (contract_cols(dpre, q_weight[...]) + djoined[here].astype(F32)).astype(BF16)
+        dtable[here] = (owned * slope[here]).astype(BF16)
+
+    each_block(count, own_block)
+    for copy in got:
+        copy.wait()
+
+    def block(step):
+        here = rows_of(step)
+        low = contract_cols(dtable[here], q_weight[...]) + djoined[here].astype(F32)
+        low = low.astype(BF16)
         product = contract_cols(low, proj[...])
         is_board = boards[here, :1] > 0.5
         own = low.astype(F32)
@@ -489,30 +504,29 @@
         first += piece
 
 
-def ordered(bits, held, sizes, other, into=None):
+def ordered(bits, held, sizes, other, into=None, part=0, parts=1):
     columns = held.shape[1]
     steps = PLACES // 4
     into = list(into or ())
     mark = 2 if other else 1
 
     def target(i, b):
-        return ((1 - b[0] if other else b[0]) * steps + i, 0)
+        block = (part * (steps // parts) + i) ^ (b[mark] // 4)
+        return ((1 - b[0] if other else b[0]) * steps + block, 0)
 
     return pl.pallas_call(
         functools.partial(ordered_kernel, count=len(sizes), other=other),
         out_shape=[shape((2 * PLACES * size, columns), F32) for size in sizes],
         grid_spec=pltpu.PrefetchScalarGridSpec(
             num_scalar_prefetch=1,
-            grid=(steps,),
-            in_specs=[pl.BlockSpec((4 * sum(sizes), columns), lambda i, b: (i ^ (b[mark] // 4), 0))]
+            grid=(steps // parts,),
+            in_specs=[pl.BlockSpec((4 * sum(sizes), columns), lambda i, b: (i, 0))]
             + [ANY] * len(into),
             out_specs=[pl.BlockSpec((4 * size, columns), target) for size in sizes],
         ),
         input_output_aliases={2 + i: i for i in range(len(into))},
         compiler_params=pltpu.CompilerParams(vmem_limit_bytes=24 * MEGA),
-        cost_estimate=pl.CostEstimate(
-            flops=0, bytes_accessed=200 * MEGA, transcendentals=0
-        ),
+        cost_estimate=COST,
     )(bits, held, *into)
 
 
@@ -563,14 +577,55 @@
     return rows[:2] + rows[2:4]
 
 
+def split_kernel(*refs, with_bias):
+    held, back = refs[:2]
+    away, stay = refs[-2:]
+    half = stay.shape[0]
+    size = 64
+
+    def block(step):
+        here = pl.ds(pl.multiple_of(step * size, size), size)
+        there = pl.ds(pl.multiple_of(half + step * size, size), size)
+        stay[here] = held[here].astype(F32) + back[here].astype(F32)
+        away[here] = (held[there].astype(F32) + back[there].astype(F32)).astype(BF16)
+
+    each_block(half // size, block)
+    if with_bias:
+        mine = refs[2][...].astype(F32)
+        other = back[2 * half :].astype(F32)
+        total = mine[0:2] + mine[2:4] + (other[0:2] + other[2:4])
+        total = jnp.concatenate([total, total] + [jnp.zeros((12, total.shape[1]), F32)])
+        high = total.astype(BF16).astype(F32)
+        row = lax.broadcasted_iota(jnp.int32, total.shape, 0)
+        rest = jnp.where(row < 4, total - high, 0.0)
+        away[half:] = jnp.where(row < 2, high, rest).astype(BF16)
+
+
+def split(held, back, *mine):
+    half, width = held.shape[0] // 2, held.shape[1]
+    return pl.pallas_call(
+        functools.partial(split_kernel, with_bias=bool(mine)),
+        out_shape=(
+            shape((half + len(mine) * BIAS_ROWS, width), BF16), shape((half, width), F32)
+        ),
+        in_specs=[VMEM] * (2 + len(mine)),
+        out_specs=(VMEM, VMEM),
+        compiler_params=pltpu.CompilerParams(vmem_limit_bytes=16 * MEGA),
+        cost_estimate=COST,
+    )(held, back, *mine)
+
+
 class PieceSum:
     def __init__(self, sent, with_bias):
         self.got = swap(sent, "rep", 1)
-        self.bias = unpack(sent) if with_bias else None
+        self.bias = None
+        self.mine = (sent[-BIAS_ROWS:],) if with_bias else ()
         self.stage = 0
 
     def first(self, order, kept):
-        self.split(order, kept, self.got)
+        away, self.held = order(split, kept, self.got, *self.mine)
+        self.bias = unpack(away) if self.mine else None
+        self.back = cross(away, WAYS[0])
 
     def reduce(self, order):
         self.stage += 1
@@ -654,9 +709,20 @@
         self.back = cross(self.held, WAYS[self.stage])
 
     def last(self, order):
+        self.mine = order(lambda *parts: jnp.concatenate(parts), self.held, self.back)
+        self.other = swap(self.mine, "rep", 1)
+
+    def gather_last(self, order):
         extra = [] if self.bias is None else [pack(self.bias)]
+        rows = self.held.shape[0] + self.back.shape[0]
         self.mine = order(lambda *parts: jnp.concatenate(parts), self.held, self.back, *extra)
+        self.stage -= 1
+        self.back = cross(self.mine[:rows], WAYS[self.stage])
         self.other = swap(self.mine, "rep", 1)
+
+    def last_half(self, order):
+        self.back = order(lambda value: value, self.back)
+        self.other_back = swap(self.back, "rep", 1)
 
 
 def per_device(
@@ -715,13 +781,13 @@
     near, far, hidden, slope, agg, base, own_lowered, boards = call(
         local_kernel,
         (shape((rows, rows), BF16), shape((rows, halo), BF16), shape(low, BF16))
-        + (shape(low, F32),) * 3
+        + (shape(low, F32), shape(low, BF16), shape(low, F32))
         + (shape(narrow, BF16), shape((rows, LANES), F32)),
         [whole(rows // 8, 8 * wide)] * 2 + [whole(rows, 1)] + [whole(1, width)] * 2 + [ANY] * 4,
         (ANY,) * 7 + (whole(rows, LANES),),
         buffers((low, BF16), ((lowered, width), BF16), ((width, width), BF16))
         + buffers(((width, width), BF16), ((rows, rows), BF16), ((rows, halo), BF16))
-        + buffers((low, BF16), (low, BF16), (low, F32), (low, F32), (low, F32), (narrow, BF16))
+        + buffers((low, BF16), (low, BF16), (low, F32), (low, BF16), (low, F32), (narrow, BF16))
         + semaphores(9 + 2 * (rows // BLOCK)),
         tokens=(outgoing,),
     )(names, weights, kinds, q_bias_row, w_bias_row, features, proj_board, q_weight, w_weight)
@@ -742,7 +808,7 @@
         [SMEM, SMEM, whole(rows, 1), whole(1, width)] + [ANY] * 9,
         (ANY,) * 10 + (whole(8, width),),
         buffers(((rows, halo), BF16), (far_low, BF16), ((lowered, width), BF16))
-        + buffers(((width, width), BF16), (low, F32), (low, F32), ((width, width), BF16))
+        + buffers(((width, width), BF16), (low, BF16), (low, F32), ((width, width), BF16))
         + buffers((low, BF16), (low, BF16), (low, BF16), (low, BF16), (low, BF16))
         + buffers(((spot, width), BF16), (w_dims, BF16), (w_dims, BF16), ((spot, width), BF16))
         + buffers(((spot, width), F32), ((spot, lowered), BF16))
@@ -780,6 +846,7 @@
     late_sum = PieceSum(order(lambda sent: sent, late_sent), True)
     returned = order(lambda value: value, returned)
     late_sum.first(order, late_kept)
+    w_sizes, late_sizes = [width // 16], [width // 32, lowered // 32]
     grad_features = order(
         call(
             grad_features_kernel,
@@ -797,25 +864,32 @@
     late_sum.reduce(order)
     w_sum.reduce(order)
     late_sum.reduce(order)
+    late_sum.reduce(order)
     w_sum.turn(order)
-    late_sum.reduce(order)
-    w_sum.gather(order)
     late_sum.turn(order)
     w_sum.gather(order)
     late_sum.gather(order)
     w_sum.gather(order)
     late_sum.gather(order)
-    late_sum.gather(order)
+    w_sum.gather(order)
+    late_sum.gather_last(order)
     w_sum.last(order)
-    w_sizes, late_sizes = [width // 16], [width // 32, lowered // 32]
     grad_w = order(lambda b, m: ordered(b, m, w_sizes, False), bits, w_sum.mine)
     (grad_w,) = order(lambda b, m, o: ordered(b, m, w_sizes, True, o), bits, w_sum.other, grad_w)
-    late_sum.last(order)
-    both = order(lambda b, m: ordered(b, m, late_sizes, False), bits, late_sum.mine)
+    both = order(
+        lambda b, m: ordered(b, m, late_sizes, False, None, 0, 2), bits, late_sum.mine
+    )
+    both = order(
+        lambda b, m, o: ordered(b, m, late_sizes, True, o, 0, 2), bits, late_sum.other, both
+    )
+    late_sum.last_half(order)
+    both = order(
+        lambda b, m, o: ordered(b, m, late_sizes, False, o, 1, 2), bits, late_sum.back, both
+    )
     grad_q, grad_proj = order(
-        lambda b, m, o: ordered(b, m, late_sizes, True, o), bits, late_sum.other, both
+        lambda b, m, o: ordered(b, m, late_sizes, True, o, 1, 2), bits, late_sum.other_back, both
     )
-    biases = unpack(jnp.where(core == 0, late_sum.mine[late_rows:], late_sum.other[late_rows:]))
+    biases = unpack(jnp.where(core == 0, late_sum.mine[-BIAS_ROWS:], late_sum.other[-BIAS_ROWS:]))
     return (embedding, grad_features, grad_proj, grad_q, biases[0], grad_w, biases[1])
 
 

time: 213 us -> 201 us (0.944)
  waiting for transfers between devices: 64.9 us -> 52.6 us
  other arithmetic: 13.7 us -> 6.01 us
  starting transfers between devices: 31.1 us -> 37.1 us
  local copies, waits for them, and re-layouts: 6.46 us -> 10.1 us
    ppermute x16, waiting for transfers between devices: 56.9 us -> 44.4 us  [cross(): return lax.ppermute(value, ('dom', 'rep'), pairs)]
    add x5 -> x3, other arithmetic: 9.77 us -> 3.71 us  [step(): stay = held[:half].astype(F32) + back[:half].astype(F32)]
    ppermute x16, starting transfers between devices: 18.4 us -> 24 us  [cross(): return lax.ppermute(value, ('dom', 'rep'), pairs)]
    pallas_call x5, Pallas kernels: 83.3 us -> 77.8 us  [call(): return lambda *operands: built(*operands, *tokens)]
    unnamed x25 -> x26, local copies, waits for them, and re-layouts: 1.73 us -> 4.65 us
    pallas_call x4 -> x6, Pallas kernels: 11.3 us -> 13 us  [ordered(): pl.pallas_call(functools.partial(ordered_kernel, count=len(sizes), other=...]
    ppermute x4 -> x5, waiting for transfers between devices: 5.14 us -> 4.37 us  [swap(): return lax.ppermute(value, axis, [(s, s ^ mask) for s in range(size)])]
  transfers between devices with their start and end apart: 22 -> 23, of which waited for: 15 -> 14; matrix products, arithmetic and copies ran while one was open for 7% -> 6% of each run, Pallas kernels for 29% -> 31%
where the time goes in v3:
time: 201 us; the launch traced here: 200 us
  Pallas kernels  92.6 us (46%)
  waiting for transfers between devices  52.6 us (26%)
  starting transfers between devices  37.1 us (18%)
  local copies, waits for them, and re-layouts  10.1 us (5%)
  other arithmetic  6.01 us (3%)
    pallas_call x5, Pallas kernels, call(): return lambda *operands: built(*operands, *tokens)  77.8 us
    ppermute x16, waiting for transfers between devices, cross(): return lax.ppermute(value, ('dom', 'rep'), pairs)  44.4 us
    ppermute x16, starting transfers between devices, cross(): return lax.ppermute(value, ('dom', 'rep'), pairs)  24 us
    pallas_call x6, Pallas kernels, ordered(): pl.pallas_call(functools.partial(ordered_kernel, count=len(sizes), other=...  13 us
    all_to_all x1, starting transfers between devices, per_device(): lax.all_to_all(outgoing, 'dom', split_axis=0, concat_axis=0, tiled=True)  7.4 us
    unnamed x26, local copies, waits for them, and re-layouts  4.65 us
    all_to_all x1, starting transfers between devices, per_device(): lax.all_to_all(to_peers, 'dom', split_axis=0, concat_axis=0, tiled=True)  4.54 us
    ppermute x5, waiting for transfers between devices, swap(): return lax.ppermute(value, axis, [(s, s ^ mask) for s in range(size)])  4.37 us
  transfers between devices with their start and end apart: 23, of which 14 were waited for; matrix products, arithmetic and copies ran while one was open for 6% of the time, Pallas kernels for 31%

profile of v3, /device:TPU:0, one launch (start us, length us, event | category | flops | bytes accessed | tf_op | source)
XLA Modules:
  0.0 200.2 jit_solution(16124396745753454495)
XLA Ops:
  0.6 4.6 %shard_map.171.refs_9_ = bf16[512,1024]{1,0:T(8,128)(2,1)} custom-call(s32[1,512]{1,0:T(1,128)} %bitcast.23, s32[1,1024]{1,0:T(1,128)} %bitcast.18, bf16[1024,1024]{1,0:T(8,128)(2,1)} %refs_5_.1), custom_call_target="tpu_custom_call" | custom-call | tf_op jit(solution)/shard_map/pallas_call | solution.py:63
  5.2 7.4 %all-to-all-start = ((bf16[8,64,1024]{2,1,0:T(8,128)(2,1)}), bf16[8,64,1024]{2,1,0:T(8,128)(2,1)S(1)}, u32[]{:S(2)}, u32[]{:S(2)}) async-start(bf16[8,64,1024]{2,1,0:T(8,128)(2,1)} %bitcast.15), calls=%async_computation | async-start | bytes 2097152 | tf_op jit(solution)/shard_map/all_to_all | solution.py:774
  12.9 0.9 reshape.50.refs_0_
  14.1 0.9 reshape.51.refs_1_
  15.0 1.0 copy.30.refs_2_
  16.0 1.1 copy.31.refs_2_
  17.7 20.3 %shard_map.172 = (bf16[1024,1024]{1,0:T(8,128)(2,1)}, bf16[1024,512]{1,0:T(8,128)(2,1)}, bf16[1024,1024]{1,0:T(8,128)(2,1)}, f32[1024,1024]{1,0:T(8,128)}, bf16[...) custom-call(s32[128,512]{1,0:T(8,128)} %reshape.50.refs_0_, ...), custom_call_target="tpu_custom_call" | custom-call | tf_op jit(solution)/shard_map/pallas_call | solution.py:63
  38.8 1.0 copy-done.3
  39.7 22.8 %shard_map.173 = (f32[1024,1024]{1,0:T(8,128)}, bf16[1024,1024]{1,0:T(8,128)(2,1)}, bf16[1024,1024]{1,0:T(8,128)(2,1)}, bf16[512,1024]{1,0:T(8,128)(2,1)}, bf16[...) custom-call(s32[1]{0:T(128)S(6)} %copy.49.refs_0_, ...), custom_call_target="tpu_custom_call" | custom-call | tf_op jit(solution)/shard_map/pallas_call | solution.py:63
  62.7 4.4 %collective-permute-done.refs_1_ = bf16[1024,1024]{1,0:T(8,128)(2,1)S(1)} collective-permute-done((bf16[1024,1024]{1,0:T(8,128)(2,1)}, bf16[1024,1024]{1,0:T(8,128)(2,1)S(1)}, u32[]{:S(2)}, u32[]{:S(2)}) %collective-permute-start) | collective-permute-done | bytes 2097184 | tf_op jit(solution)/shard_map/ppermute | solution.py:535
  67.0 1.6 copy-done
  69.1 2.1 %collective-permute-start.1 = (bf16[512,1024]{1,0:T(8,128)(2,1)S(1)}, bf16[512,1024]{1,0:T(8,128)(2,1)}, u32[]{:S(2)}, u32[]{:S(2)}) collective-permute-start(bf16[512,1024]{1,0:T(8,128)(2,1)S(1)} %get-tuple-element.144), channel_id=1, source_target_pairs={{0,4},{1,3},{2,6},{3,1},{4,0},{5,7},{6,2},{7,5},{8,12},{9,11},{10,... | collective-permute-start | bytes 3145736 | tf_op jit(solution)/shard_map/ppermute | solution.py:555
  71.2 4.5 %all-to-all-start.1 = ((bf16[8,64,1024]{2,1,0:T(8,128)(2,1)}), bf16[8,64,1024]{2,1,0:T(8,128)(2,1)}, u32[]{:S(2)}, u32[]{:S(2)}) async-start(bf16[8,64,1024]{2,1,0:T(8,128)(2,1)} %bitcast.17), calls=%async_computation.1 | async-start | bytes 2097152 | tf_op jit(solution)/shard_map/all_to_all | solution.py:820
  75.7 18.2 %shard_map.175 = (bf16[1024,1024]{1,0:T(8,128)(2,1)}, bf16[1024,1024]{1,0:T(8,128)(2,1)}, bf16[784,1024]{1,0:T(8,128)(2,1)}, bf16[768,1024]{1,0:T(8,128)(2,1)}) custom-call(s32[3]{0:T(128)} %pad_add_fusion.refs_1_.refs_0_.bits, f32[8,1024]{1,0:T(8,128)} %get-tuple-element.146.refs_1_, bf16[1024,1024]{1,0:T(8,128)(2,1)} %get-tuple-element.147.refs_2_, ...), custom_call_target="tpu_custom_call" | custom-call | bytes 209715200 | tf_op jit(solution)/shard_map/pallas_call | solution.py:63
  93.9 2.5 %convert_add_fusion = (f32[256,1024]{1,0:T(8,128)}, bf16[256,1024]{1,0:T(8,128)(2,1)S(1)}) fusion(f32[512,1024]{1,0:T(8,128)S(1)} %get-tuple-element.161, bf16[512,1024]{1,0:T(8,128)(2,1)} %collective-permute-done.1), kind=kLoop, calls=%fused_computation | loop fusion | flops 1310720 | bytes 4718592 | tf_op jit(solution)/shard_map/add | solution.py:638
  97.0 1.0 collective-permute-start.4
  98.0 0.8 slice.160.refs_2_
  98.7 3.9 %all-to-all-done.1 = bf16[8,64,1024]{2,1,0:T(8,128)(2,1)} async-done(((bf16[8,64,1024]{2,1,0:T(8,128)(2,1)}), bf16[8,64,1024]{2,1,0:T(8,128)(2,1)}, u32[]{:S(2)}, u32[]{:S(2)}) %all-to-all-start.1) | async-done | bytes 1048608 | tf_op jit(solution)/shard_map/all_to_all | solution.py:820
  102.6 1.4 copy-done.1
  104.0 1.3 shard_map.176
  105.3 1.5 collective-permute-start.3
  106.8 11.8 %shard_map.177 = f32[1024,1024]{1,0:T(8,128)} custom-call(s32[1,512]{1,0:T(1,128)} %bitcast.24, f32[1024,128]{1,0:T(8,128)} %get-tuple-element.172.refs_1_, bf16[512,1024]{1,0:T(8,128)(2,1)} %bitcast.12.refs_2_, bf16[1024,1024]{1,0:T(8,128)(2,1)} %get-tuple-element.174.refs_3_, f32[1024,1024]{1,0:T(8,128)} %get-tuple-element.175.refs_4_, ...), custom_call_target="tpu_custom_call" | custom-call | bytes 209715200 | tf_op jit(solution)/shard_map/pallas_call | solution.py:63
  118.6 1.1 convert_add_fusion.2
  119.9 0.8 slice_convert_fusion.4
  121.0 1.1 collective-permute-start.5
  122.1 6.3 %collective-permute-done.6 = bf16[128,1024]{1,0:T(8,128)(2,1)S(1)} collective-permute-done((bf16[128,1024]{1,0:T(8,128)(2,1)S(1)}, bf16[128,1024]{1,0:T(8,128)(2,1)S(1)}, u32[]{:S(2)}, u32[]{:S(2)}) %collective-permute-start.6) | collective-permute-done | bytes 262176 | tf_op jit(solution)/shard_map/ppermute | solution.py:555
  129.4 2.1 %collective-permute-start.7 = (bf16[112,1024]{1,0:T(8,128)(2,1)S(1)}, bf16[112,1024]{1,0:T(8,128)(2,1)S(1)}, u32[]{:S(2)}, u32[]{:S(2)}) collective-permute-start(bf16[112,1024]{1,0:T(8,128)(2,1)S(1)} %pad_maximum_fusion.2), channel_id=1, source_target_pairs={{0,8},{1,17},{2,10},{3,19},{4,12},{5,21},{6,14},{7,23},{8,0},{9,25... | collective-permute-start | bytes 688136 | tf_op jit(solution)/shard_map/ppermute | solution.py:555
  131.5 4.5 %collective-permute-done.7 = bf16[112,1024]{1,0:T(8,128)(2,1)S(1)} collective-permute-done((bf16[112,1024]{1,0:T(8,128)(2,1)S(1)}, bf16[112,1024]{1,0:T(8,128)(2,1)S(1)}, u32[]{:S(2)}, u32[]{:S(2)}) %collective-permute-start.7) | collective-permute-done | bytes 229408 | tf_op jit(solution)/shard_map/ppermute | solution.py:555
  136.1 3.5 %collective-permute-start.8 = (bf16[64,1024]{1,0:T(8,128)(2,1)S(1)}, bf16[64,1024]{1,0:T(8,128)(2,1)S(1)}, u32[]{:S(2)}, u32[]{:S(2)}) collective-permute-start(bf16[64,1024]{1,0:T(8,128)(2,1)S(1)} %pad_maximum_fusion.3), channel_id=1, source_target_pairs={{0,16},{1,9},{2,18},{3,11},{4,20},{5,13},{6,22},{7,15},{8,24},{9,1... | collective-permute-start | bytes 393224 | tf_op jit(solution)/shard_map/ppermute | solution.py:555
  139.8 3.6 %collective-permute-done.8 = bf16[64,1024]{1,0:T(8,128)(2,1)S(1)} collective-permute-done((bf16[64,1024]{1,0:T(8,128)(2,1)S(1)}, bf16[64,1024]{1,0:T(8,128)(2,1)S(1)}, u32[]{:S(2)}, u32[]{:S(2)}) %collective-permute-start.8) | collective-permute-done | bytes 131104 | tf_op jit(solution)/shard_map/ppermute | solution.py:555
  143.5 3.4 %collective-permute-start.10 = (bf16[48,1024]{1,0:T(8,128)(2,1)S(1)}, bf16[48,1024]{1,0:T(8,128)(2,1)S(1)}, u32[]{:S(2)}, u32[]{:S(2)}) collective-permute-start(bf16[48,1024]{1,0:T(8,128)(2,1)S(1)} %add_convert_fusion.6), channel_id=1, source_target_pairs={{0,16},{1,9},{2,18},{3,11},{4,20},{5,13},{6,22},{7,15},{8,24},{9,1... | collective-permute-start | bytes 294920 | tf_op jit(solution)/shard_map/ppermute | solution.py:555
  147.1 1.8 collective-permute-start.13
  149.5 5.2 %collective-permute-done.13 = bf16[128,1024]{1,0:T(8,128)(2,1)S(1)} collective-permute-done((bf16[128,1024]{1,0:T(8,128)(2,1)S(1)}, bf16[128,1024]{1,0:T(8,128)(2,1)S(1)}, u32[]{:S(2)}, u32[]{:S(2)}) %collective-permute-start.13) | collective-permute-done | bytes 262176 | tf_op jit(solution)/shard_map/ppermute | solution.py:555
  154.8 1.1 collective-permute-start.15
  155.9 2.5 %collective-permute-start.12 = (bf16[96,1024]{1,0:T(8,128)(2,1)S(1)}, bf16[96,1024]{1,0:T(8,128)(2,1)S(1)}, u32[]{:S(2)}, u32[]{:S(2)}) collective-permute-start(bf16[96,1024]{1,0:T(8,128)(2,1)S(1)} %constant_dynamic-update-slice_fusion.2), channel_id=1, source_target_pairs={{0,8},{1,17},{2,10},{3,19},{4,12},{5,21},{6,14},{7,23},{8,0},{9,25... | collective-permute-start | bytes 589832 | tf_op jit(solution)/shard_map/ppermute | solution.py:555
  158.3 4.5 %collective-permute-done.12 = bf16[96,1024]{1,0:T(8,128)(2,1)S(1)} collective-permute-done((bf16[96,1024]{1,0:T(8,128)(2,1)S(1)}, bf16[96,1024]{1,0:T(8,128)(2,1)S(1)}, u32[]{:S(2)}, u32[]{:S(2)}) %collective-permute-start.12) | collective-permute-done | bytes 196640 | tf_op jit(solution)/shard_map/ppermute | solution.py:555
  162.8 1.2 collective-permute-done.15
  164.1 1.6 collective-permute-start.18
  166.3 11.4 %collective-permute-done.14 = bf16[192,1024]{1,0:T(8,128)(2,1)S(1)} collective-permute-done((bf16[192,1024]{1,0:T(8,128)(2,1)S(1)}, bf16[192,1024]{1,0:T(8,128)(2,1)S(1)}, u32[]{:S(2)}, u32[]{:S(2)}) %collective-permute-start.14) | collective-permute-done | bytes 393248 | tf_op jit(solution)/shard_map/ppermute | solution.py:555
  177.8 5.4 %collective-permute-done.18 = bf16[512,1024]{1,0:T(8,128)(2,1)S(1)} collective-permute-done((bf16[512,1024]{1,0:T(8,128)(2,1)S(1)}, bf16[512,1024]{1,0:T(8,128)(2,1)S(1)}, u32[]{:S(2)}, u32[]{:S(2)}) %collective-permute-start.18) | collective-permute-done | bytes 1048608 | tf_op jit(solution)/shard_map/ppermute | solution.py:555
  184.0 1.5 collective-permute-start.16
  185.5 3.0 %shard_map.178.refs_0_ = f32[2048,1024]{1,0:T(8,128)} custom-call(s32[3]{0:T(128)S(1)} %copy-done.2, bf16[1024,1024]{1,0:T(8,128)(2,1)S(1)} %constant_dynamic-update-slice_fusion.13.held), custom_call_target="tpu_custom_call" | custom-call | tf_op jit(solution)/shard_map/pallas_call | solution.py:517
  188.5 3.0 %shard_map.179 = f32[2048,1024]{1,0:T(8,128)} custom-call(s32[3]{0:T(128)S(1)} %copy-done.2, bf16[1024,1024]{1,0:T(8,128)(2,1)S(1)} %collective-permute-done.19.held, f32[2048,1024]{1,0:T(8,128)} %shard_map.178.refs_0_), custom_call_target="tpu_custom_call", output_to_operand_aliasing={{}: (2, {})} | custom-call | tf_op jit(solution)/shard_map/pallas_call | solution.py:517
  191.5 1.8 shard_map.180
  193.2 1.8 shard_map.181
  195.0 1.0 collective-permute-done.16.held
  196.6 1.8 shard_map.182
  198.4 1.8 shard_map.183
  (91 shorter events, 7.1 us)
Async XLA Ops:
  0.6 12.0 %copy-start.6 = (s32[1024,50]{0,1:T(8,128)S(1)}, s32[1024,50]{0,1:T(8,128)}, u32[]{:S(2)}) copy-start(s32[1024,50]{0,1:T(8,128)} %param.14) | copy-start | bytes 614404
  5.2 8.6 %copy-start.5 = (f32[1024,50]{0,1:T(8,128)S(1)}, f32[1024,50]{0,1:T(8,128)}, u32[]{:S(2)}) copy-start(f32[1024,50]{0,1:T(8,128)} %param.15) | copy-start | bytes 614404
  5.2 33.5 %all-to-all-start = ((bf16[8,64,1024]{2,1,0:T(8,128)(2,1)}), bf16[8,64,1024]{2,1,0:T(8,128)(2,1)S(1)}, u32[]{:S(2)}, u32[]{:S(2)}) async-start(bf16[8,64,1024]{2,1,0:T(8,128)(2,1)} %bitcast.15), calls=%async_computation | async-start | bytes 2097152 | tf_op jit(solution)/shard_map/all_to_all | solution.py:774
  12.9 2.1 %copy-start.7 = (s32[1024]{0:T(1024)S(1)}, s32[1024]{0:T(1024)}, u32[]{:S(2)}) copy-start(s32[1024]{0:T(1024)} %param.13) | copy-start | bytes 12292
  38.8 1.0 copy-start.3
  62.6 4.4 %collective-permute-start = (bf16[1024,1024]{1,0:T(8,128)(2,1)}, bf16[1024,1024]{1,0:T(8,128)(2,1)S(1)}, u32[]{:S(2)}, u32[]{:S(2)}) collective-permute-start(bf16[1024,1024]{1,0:T(8,128)(2,1)} %get-tuple-element.141), channel_id=1, source_target_pairs={{0,1},{1,0},{2,3},{3,2},{4,5},{5,4},{6,7},{7,6},{8,9},{9,8},{10,11... | collective-permute-start | bytes 6291464 | tf_op jit(solution)/shard_map/ppermute | solution.py:535
  67.0 1.6 copy-start
  69.1 24.8 %collective-permute-start.1 = (bf16[512,1024]{1,0:T(8,128)(2,1)S(1)}, bf16[512,1024]{1,0:T(8,128)(2,1)}, u32[]{:S(2)}, u32[]{:S(2)}) collective-permute-start(bf16[512,1024]{1,0:T(8,128)(2,1)S(1)} %get-tuple-element.144), channel_id=1, source_target_pairs={{0,4},{1,3},{2,6},{3,1},{4,0},{5,7},{6,2},{7,5},{8,12},{9,11},{10,... | collective-permute-start | bytes 3145736 | tf_op jit(solution)/shard_map/ppermute | solution.py:555
  71.2 31.4 %all-to-all-start.1 = ((bf16[8,64,1024]{2,1,0:T(8,128)(2,1)}), bf16[8,64,1024]{2,1,0:T(8,128)(2,1)}, u32[]{:S(2)}, u32[]{:S(2)}) async-start(bf16[8,64,1024]{2,1,0:T(8,128)(2,1)} %bitcast.17), calls=%async_computation.1 | async-start | bytes 2097152 | tf_op jit(solution)/shard_map/all_to_all | solution.py:820
  96.4 6.2 %collective-permute-start.2 = (bf16[784,1024]{1,0:T(8,128)(2,1)}, bf16[784,1024]{1,0:T(8,128)(2,1)S(1)}, u32[]{:S(2)}, u32[]{:S(2)}) collective-permute-start(bf16[784,1024]{1,0:T(8,128)(2,1)} %get-tuple-element.163), channel_id=1, source_target_pairs={{0,1},{1,0},{2,3},{3,2},{4,5},{5,4},{6,7},{7,6},{8,9},{9,8},{10,11... | collective-permute-start | bytes 4816904 | tf_op jit(solution)/shard_map/ppermute | solution.py:535
  97.0 21.7 %collective-permute-start.4 = (bf16[256,1024]{1,0:T(8,128)(2,1)S(1)}, bf16[256,1024]{1,0:T(8,128)(2,1)}, u32[]{:S(2)}, u32[]{:S(2)}) collective-permute-start(bf16[256,1024]{1,0:T(8,128)(2,1)S(1)} %get-tuple-element.250), channel_id=1, source_target_pairs={{0,2},{1,5},{2,0},{3,7},{4,6},{5,1},{6,4},{7,3},{8,10},{9,13},{10,... | collective-permute-start | bytes 1572872 | tf_op jit(solution)/shard_map/ppermute | solution.py:555
  102.6 1.4 copy-start.1
  105.3 15.4 %collective-permute-start.3 = (bf16[400,1024]{1,0:T(8,128)(2,1)}, bf16[400,1024]{1,0:T(8,128)(2,1)S(1)}, u32[]{:S(2)}, u32[]{:S(2)}) collective-permute-start(bf16[400,1024]{1,0:T(8,128)(2,1)} %get-tuple-element.170), channel_id=1, source_target_pairs={{0,4},{1,3},{2,6},{3,1},{4,0},{5,7},{6,2},{7,5},{8,12},{9,11},{10,... | collective-permute-start | bytes 2457608 | tf_op jit(solution)/shard_map/ppermute | solution.py:555
  106.8 11.9 %copy-start.4 = (f32[256,1024]{1,0:T(8,128)S(1)}, f32[256,1024]{1,0:T(8,128)}, u32[]{:S(2)}) copy-start(f32[256,1024]{1,0:T(8,128)} %get-tuple-element.180) | copy-start | bytes 3145732
  119.8 8.5 %collective-permute-start.6 = (bf16[128,1024]{1,0:T(8,128)(2,1)S(1)}, bf16[128,1024]{1,0:T(8,128)(2,1)S(1)}, u32[]{:S(2)}, u32[]{:S(2)}) collective-permute-start(bf16[128,1024]{1,0:T(8,128)(2,1)S(1)} %get-tuple-element.254), channel_id=1, source_target_pairs={{0,8},{1,17},{2,10},{3,19},{4,12},{5,21},{6,14},{7,23},{8,0},{9,25... | collective-permute-start | bytes 786440 | tf_op jit(solution)/shard_map/ppermute | solution.py:555
  121.0 8.2 %collective-permute-start.5 = (bf16[208,1024]{1,0:T(8,128)(2,1)S(1)}, bf16[208,1024]{1,0:T(8,128)(2,1)S(1)}, u32[]{:S(2)}, u32[]{:S(2)}) collective-permute-start(bf16[208,1024]{1,0:T(8,128)(2,1)S(1)} %pad_maximum_fusion.1), channel_id=1, source_target_pairs={{0,2},{1,5},{2,0},{3,7},{4,6},{5,1},{6,4},{7,3},{8,10},{9,13},{10,... | collective-permute-start | bytes 1277960 | tf_op jit(solution)/shard_map/ppermute | solution.py:555
  128.4 11.2 %collective-permute-start.9 = (bf16[64,1024]{1,0:T(8,128)(2,1)S(1)}, bf16[64,1024]{1,0:T(8,128)(2,1)S(1)}, u32[]{:S(2)}, u32[]{:S(2)}) collective-permute-start(bf16[64,1024]{1,0:T(8,128)(2,1)S(1)} %get-tuple-element.258), channel_id=1, source_target_pairs={{0,16},{1,9},{2,18},{3,11},{4,20},{5,13},{6,22},{7,15},{8,24},{9,1... | collective-permute-start | bytes 393224 | tf_op jit(solution)/shard_map/ppermute | solution.py:555
  129.4 6.6 %collective-permute-start.7 = (bf16[112,1024]{1,0:T(8,128)(2,1)S(1)}, bf16[112,1024]{1,0:T(8,128)(2,1)S(1)}, u32[]{:S(2)}, u32[]{:S(2)}) collective-permute-start(bf16[112,1024]{1,0:T(8,128)(2,1)S(1)} %pad_maximum_fusion.2), channel_id=1, source_target_pairs={{0,8},{1,17},{2,10},{3,19},{4,12},{5,21},{6,14},{7,23},{8,0},{9,25... | collective-permute-start | bytes 688136 | tf_op jit(solution)/shard_map/ppermute | solution.py:555
  136.1 7.3 %collective-permute-start.8 = (bf16[64,1024]{1,0:T(8,128)(2,1)S(1)}, bf16[64,1024]{1,0:T(8,128)(2,1)S(1)}, u32[]{:S(2)}, u32[]{:S(2)}) collective-permute-start(bf16[64,1024]{1,0:T(8,128)(2,1)S(1)} %pad_maximum_fusion.3), channel_id=1, source_target_pairs={{0,16},{1,9},{2,18},{3,11},{4,20},{5,13},{6,22},{7,15},{8,24},{9,1... | collective-permute-start | bytes 393224 | tf_op jit(solution)/shard_map/ppermute | solution.py:555
  139.7 7.3 %collective-permute-start.11 = (bf16[64,1024]{1,0:T(8,128)(2,1)S(1)}, bf16[64,1024]{1,0:T(8,128)(2,1)S(1)}, u32[]{:S(2)}, u32[]{:S(2)}) collective-permute-start(bf16[64,1024]{1,0:T(8,128)(2,1)S(1)} %add_convert_fusion.4), channel_id=1, source_target_pairs={{0,16},{1,9},{2,18},{3,11},{4,20},{5,13},{6,22},{7,15},{8,24},{9,1... | collective-permute-start | bytes 393224 | tf_op jit(solution)/shard_map/ppermute | solution.py:555
  143.5 6.0 %collective-permute-start.10 = (bf16[48,1024]{1,0:T(8,128)(2,1)S(1)}, bf16[48,1024]{1,0:T(8,128)(2,1)S(1)}, u32[]{:S(2)}, u32[]{:S(2)}) collective-permute-start(bf16[48,1024]{1,0:T(8,128)(2,1)S(1)} %add_convert_fusion.6), channel_id=1, source_target_pairs={{0,16},{1,9},{2,18},{3,11},{4,20},{5,13},{6,22},{7,15},{8,24},{9,1... | collective-permute-start | bytes 294920 | tf_op jit(solution)/shard_map/ppermute | solution.py:555
  147.1 7.7 %collective-permute-start.13 = (bf16[128,1024]{1,0:T(8,128)(2,1)S(1)}, bf16[128,1024]{1,0:T(8,128)(2,1)S(1)}, u32[]{:S(2)}, u32[]{:S(2)}) collective-permute-start(bf16[128,1024]{1,0:T(8,128)(2,1)S(1)} %constant_dynamic-update-slice_fusion), channel_id=1, source_target_pairs={{0,8},{1,17},{2,10},{3,19},{4,12},{5,21},{6,14},{7,23},{8,0},{9,25... | collective-permute-start | bytes 786440 | tf_op jit(solution)/shard_map/ppermute | solution.py:555
  154.8 9.2 %collective-permute-start.15 = (bf16[256,1024]{1,0:T(8,128)(2,1)S(1)}, bf16[256,1024]{1,0:T(8,128)(2,1)S(1)}, u32[]{:S(2)}, u32[]{:S(2)}) collective-permute-start(bf16[256,1024]{1,0:T(8,128)(2,1)S(1)} %constant_dynamic-update-slice_fusion.4), channel_id=1, source_target_pairs={{0,2},{1,5},{2,0},{3,7},{4,6},{5,1},{6,4},{7,3},{8,10},{9,13},{10,... | collective-permute-start | bytes 1572872 | tf_op jit(solution)/shard_map/ppermute | solution.py:555
  155.9 6.9 %collective-permute-start.12 = (bf16[96,1024]{1,0:T(8,128)(2,1)S(1)}, bf16[96,1024]{1,0:T(8,128)(2,1)S(1)}, u32[]{:S(2)}, u32[]{:S(2)}) collective-permute-start(bf16[96,1024]{1,0:T(8,128)(2,1)S(1)} %constant_dynamic-update-slice_fusion.2), channel_id=1, source_target_pairs={{0,8},{1,17},{2,10},{3,19},{4,12},{5,21},{6,14},{7,23},{8,0},{9,25... | collective-permute-start | bytes 589832 | tf_op jit(solution)/shard_map/ppermute | solution.py:555
  164.1 19.1 %collective-permute-start.18 = (bf16[512,1024]{1,0:T(8,128)(2,1)S(1)}, bf16[512,1024]{1,0:T(8,128)(2,1)S(1)}, u32[]{:S(2)}, u32[]{:S(2)}) collective-permute-start(bf16[512,1024]{1,0:T(8,128)(2,1)S(1)} %constant_dynamic-update-slice_fusion.8), channel_id=1, source_target_pairs={{0,4},{1,3},{2,6},{3,1},{4,0},{5,7},{6,2},{7,5},{8,12},{9,11},{10,... | collective-permute-start | bytes 3145736 | tf_op jit(solution)/shard_map/ppermute | solution.py:555
  165.7 12.1 %collective-permute-start.14 = (bf16[192,1024]{1,0:T(8,128)(2,1)S(1)}, bf16[192,1024]{1,0:T(8,128)(2,1)S(1)}, u32[]{:S(2)}, u32[]{:S(2)}) collective-permute-start(bf16[192,1024]{1,0:T(8,128)(2,1)S(1)} %constant_dynamic-update-slice_fusion.6), channel_id=1, source_target_pairs={{0,2},{1,5},{2,0},{3,7},{4,6},{5,1},{6,4},{7,3},{8,10},{9,13},{10,... | collective-permute-start | bytes 1179656 | tf_op jit(solution)/shard_map/ppermute | solution.py:555
  183.2 2.2 %copy-start.2 = (s32[3]{0:T(128)S(1)}, s32[3]{0:T(128)}, u32[]{:S(2)}) copy-start(s32[3]{0:T(128)} %pad_add_fusion.refs_1_.refs_0_.bits) | copy-start | bytes 40
  183.3 5.2 %collective-permute-start.19 = (bf16[1024,1024]{1,0:T(8,128)(2,1)S(1)}, bf16[1024,1024]{1,0:T(8,128)(2,1)S(1)}, u32[]{:S(2)}, u32[]{:S(2)}) collective-permute-start(bf16[1024,1024]{1,0:T(8,128)(2,1)S(1)} %constant_dynamic-update-slice_fusion.13.held), channel_id=1, source_target_pairs={{0,1},{1,0},{2,3},{3,2},{4,5},{5,4},{6,7},{7,6},{8,9},{9,8},{10,11... | collective-permute-start | bytes 6291464 | tf_op jit(solution)/shard_map/ppermute | solution.py:535
  183.4 9.8 %collective-permute-start.17 = (bf16[400,1024]{1,0:T(8,128)(2,1)S(1)}, bf16[400,1024]{1,0:T(8,128)(2,1)S(1)}, u32[]{:S(2)}, u32[]{:S(2)}) collective-permute-start(bf16[400,1024]{1,0:T(8,128)(2,1)S(1)} %constant_dynamic-update-slice_fusion.10.held), channel_id=1, source_target_pairs={{0,1},{1,0},{2,3},{3,2},{4,5},{5,4},{6,7},{7,6},{8,9},{9,8},{10,11... | collective-permute-start | bytes 2457608 | tf_op jit(solution)/shard_map/ppermute | solution.py:535
  184.0 12.1 %collective-permute-start.16 = (bf16[384,1024]{1,0:T(8,128)(2,1)S(1)}, bf16[384,1024]{1,0:T(8,128)(2,1)S(1)}, u32[]{:S(2)}, u32[]{:S(2)}) collective-permute-start(bf16[384,1024]{1,0:T(8,128)(2,1)S(1)} %pad_maximum_fusion), channel_id=1, source_target_pairs={{0,4},{1,3},{2,6},{3,1},{4,0},{5,7},{6,2},{7,5},{8,12},{9,11},{10,... | collective-permute-start | bytes 2359304 | tf_op jit(solution)/shard_map/ppermute | solution.py:555
  196.0 2.4 %collective-permute-start.20 = (bf16[384,1024]{1,0:T(8,128)(2,1)S(1)}, bf16[384,1024]{1,0:T(8,128)(2,1)S(1)}, u32[]{:S(2)}, u32[]{:S(2)}) collective-permute-start(bf16[384,1024]{1,0:T(8,128)(2,1)S(1)} %collective-permute-done.16.held), channel_id=1, source_target_pairs={{0,1},{1,0},{2,3},{3,2},{4,5},{5,4},{6,7},{7,6},{8,9},{9,8},{10,11... | collective-permute-start | bytes 2359304 | tf_op jit(solution)/shard_map/ppermute | solution.py:535

commit v4 on v3

--- a/solution.py
+++ b/solution.py
@@ -564,6 +564,21 @@
         result = step(*held)
         self.last = jax.tree.leaves(result)[:1]
         return result
+
+    def tick(self):
+        def nothing(_, out):
+            out[...] = jnp.zeros(out.shape, F32)
+
+        self.last = [
+            pl.pallas_call(
+                nothing,
+                out_shape=shape((8, LANES), F32),
+                in_specs=[ANY],
+                out_specs=VMEM,
+                compiler_params=pltpu.CompilerParams(vmem_limit_bytes=MEGA),
+                cost_estimate=COST,
+            )(*self.last)
+        ]
 
 
 def pack(bias):
@@ -847,6 +862,18 @@
     returned = order(lambda value: value, returned)
     late_sum.first(order, late_kept)
     w_sizes, late_sizes = [width // 16], [width // 32, lowered // 32]
+    w_sum.reduce(order)
+    late_sum.reduce(order)
+    w_sum.reduce(order)
+    late_sum.reduce(order)
+    w_sum.turn(order)
+    w_sum.gather(order)
+    late_sum.reduce(order)
+    late_sum.turn(order)
+    w_sum.gather(order)
+    late_sum.gather(order)
+    late_sum.gather(order)
+    w_sum.gather(order)
     grad_features = order(
         call(
             grad_features_kernel,
@@ -860,28 +887,16 @@
         ),
         send_row, boards, returned, dtable, slope, q_weight, djoined, proj_board,
     )
-    w_sum.reduce(order)
-    late_sum.reduce(order)
-    w_sum.reduce(order)
-    late_sum.reduce(order)
-    late_sum.reduce(order)
-    w_sum.turn(order)
-    late_sum.turn(order)
-    w_sum.gather(order)
-    late_sum.gather(order)
-    w_sum.gather(order)
-    late_sum.gather(order)
-    w_sum.gather(order)
     late_sum.gather_last(order)
-    w_sum.last(order)
-    grad_w = order(lambda b, m: ordered(b, m, w_sizes, False), bits, w_sum.mine)
-    (grad_w,) = order(lambda b, m, o: ordered(b, m, w_sizes, True, o), bits, w_sum.other, grad_w)
     both = order(
         lambda b, m: ordered(b, m, late_sizes, False, None, 0, 2), bits, late_sum.mine
     )
+    w_sum.last(order)
     both = order(
         lambda b, m, o: ordered(b, m, late_sizes, True, o, 0, 2), bits, late_sum.other, both
     )
+    grad_w = order(lambda b, m: ordered(b, m, w_sizes, False), bits, w_sum.mine)
+    (grad_w,) = order(lambda b, m, o: ordered(b, m, w_sizes, True, o), bits, w_sum.other, grad_w)
     late_sum.last_half(order)
     both = order(
         lambda b, m, o: ordered(b, m, late_sizes, False, o, 1, 2), bits, late_sum.back, both

time: 201 us -> 194 us (0.965)
  waiting for transfers between devices: 52.6 us -> 40.4 us
  starting transfers between devices: 37.1 us -> 43.9 us
    ppermute x16, waiting for transfers between devices: 44.4 us -> 28.8 us  [cross(): return lax.ppermute(value, ('dom', 'rep'), pairs)]
    ppermute x16, starting transfers between devices: 24 us -> 30.7 us  [cross(): return lax.ppermute(value, ('dom', 'rep'), pairs)]
    ppermute x5, waiting for transfers between devices: 4.37 us -> 7.6 us  [swap(): return lax.ppermute(value, axis, [(s, s ^ mask) for s in range(size)])]
    unnamed x26 -> x24, local copies, waits for them, and re-layouts: 4.65 us -> 4.64 us
  transfers between devices with their start and end apart: 23 -> 23, of which waited for: 14 -> 11; matrix products, arithmetic and copies ran while one was open for 6% -> 6% of each run, Pallas kernels for 31% -> 32%
where the time goes in v4:
time: 194 us; the launch traced here: 193 us
  Pallas kernels  91.7 us (47%)
  starting transfers between devices  43.9 us (23%)
  waiting for transfers between devices  40.4 us (21%)
  local copies, waits for them, and re-layouts  10.1 us (5%)
  other arithmetic  5.08 us (3%)
    pallas_call x5, Pallas kernels, call(): return lambda *operands: built(*operands, *tokens)  77.7 us
    ppermute x16, starting transfers between devices, cross(): return lax.ppermute(value, ('dom', 'rep'), pairs)  30.7 us
    ppermute x16, waiting for transfers between devices, cross(): return lax.ppermute(value, ('dom', 'rep'), pairs)  28.8 us
    pallas_call x6, Pallas kernels, ordered(): pl.pallas_call(functools.partial(ordered_kernel, count=len(sizes), other=...  13 us
    ppermute x5, waiting for transfers between devices, swap(): return lax.ppermute(value, axis, [(s, s ^ mask) for s in range(size)])  7.6 us
    all_to_all x1, starting transfers between devices, per_device(): lax.all_to_all(outgoing, 'dom', split_axis=0, concat_axis=0, tiled=True)  7.4 us
    unnamed x24, local copies, waits for them, and re-layouts  4.64 us
    all_to_all x1, starting transfers between devices, per_device(): lax.all_to_all(to_peers, 'dom', split_axis=0, concat_axis=0, tiled=True)  4.54 us
  transfers between devices with their start and end apart: 23, of which 11 were waited for; matrix products, arithmetic and copies ran while one was open for 6% of the time, Pallas kernels for 32%

profile of v4, /device:TPU:0, one launch (start us, length us, event | category | flops | bytes accessed | tf_op | source)
XLA Modules:
  0.0 192.9 jit_solution(12210743367478399085)
XLA Ops:
  0.6 4.6 %shard_map.171.refs_9_ = bf16[512,1024]{1,0:T(8,128)(2,1)} custom-call(s32[1,512]{1,0:T(1,128)} %bitcast.23, s32[1,1024]{1,0:T(1,128)} %bitcast.18, bf16[1024,1024]{1,0:T(8,128)(2,1)} %refs_5_.1), custom_call_target="tpu_custom_call" | custom-call | tf_op jit(solution)/shard_map/pallas_call | solution.py:63
  5.2 7.4 %all-to-all-start = ((bf16[8,64,1024]{2,1,0:T(8,128)(2,1)}), bf16[8,64,1024]{2,1,0:T(8,128)(2,1)S(1)}, u32[]{:S(2)}, u32[]{:S(2)}) async-start(bf16[8,64,1024]{2,1,0:T(8,128)(2,1)} %bitcast.15), calls=%async_computation | async-start | bytes 2097152 | tf_op jit(solution)/shard_map/all_to_all | solution.py:789
  12.9 0.9 reshape.50.refs_0_
  14.1 0.9 reshape.51.refs_1_
  15.0 1.0 copy.30.refs_2_
  16.0 1.1 copy.31.refs_2_
  17.7 20.4 %shard_map.172 = (bf16[1024,1024]{1,0:T(8,128)(2,1)}, bf16[1024,512]{1,0:T(8,128)(2,1)}, bf16[1024,1024]{1,0:T(8,128)(2,1)}, f32[1024,1024]{1,0:T(8,128)}, bf16[...) custom-call(s32[128,512]{1,0:T(8,128)} %reshape.50.refs_0_, ...), custom_call_target="tpu_custom_call" | custom-call | tf_op jit(solution)/shard_map/pallas_call | solution.py:63
  38.1 0.6 pad_add_fusion.refs_1_.refs_0_.bits
  38.7 1.0 copy-done.3
  39.7 22.8 %shard_map.173 = (f32[1024,1024]{1,0:T(8,128)}, bf16[1024,1024]{1,0:T(8,128)(2,1)}, bf16[1024,1024]{1,0:T(8,128)(2,1)}, bf16[512,1024]{1,0:T(8,128)(2,1)}, bf16[...) custom-call(s32[1]{0:T(128)S(6)} %copy.49.refs_0_, ...), custom_call_target="tpu_custom_call" | custom-call | tf_op jit(solution)/shard_map/pallas_call | solution.py:63
  62.6 4.4 %collective-permute-done.refs_1_ = bf16[1024,1024]{1,0:T(8,128)(2,1)S(1)} collective-permute-done((bf16[1024,1024]{1,0:T(8,128)(2,1)}, bf16[1024,1024]{1,0:T(8,128)(2,1)S(1)}, u32[]{:S(2)}, u32[]{:S(2)}) %collective-permute-start) | collective-permute-done | bytes 2097184 | tf_op jit(solution)/shard_map/ppermute | solution.py:535
  67.0 1.6 copy-done
  69.0 2.1 %collective-permute-start.1 = (bf16[512,1024]{1,0:T(8,128)(2,1)S(1)}, bf16[512,1024]{1,0:T(8,128)(2,1)}, u32[]{:S(2)}, u32[]{:S(2)}) collective-permute-start(bf16[512,1024]{1,0:T(8,128)(2,1)S(1)} %get-tuple-element.144), channel_id=1, source_target_pairs={{0,4},{1,3},{2,6},{3,1},{4,0},{5,7},{6,2},{7,5},{8,12},{9,11},{10,... | collective-permute-start | bytes 3145736 | tf_op jit(solution)/shard_map/ppermute | solution.py:555
  71.1 4.5 %all-to-all-start.1 = ((bf16[8,64,1024]{2,1,0:T(8,128)(2,1)}), bf16[8,64,1024]{2,1,0:T(8,128)(2,1)}, u32[]{:S(2)}, u32[]{:S(2)}) async-start(bf16[8,64,1024]{2,1,0:T(8,128)(2,1)} %bitcast.17), calls=%async_computation.1 | async-start | bytes 2097152 | tf_op jit(solution)/shard_map/all_to_all | solution.py:835
  75.6 18.2 %shard_map.175 = (bf16[1024,1024]{1,0:T(8,128)(2,1)}, bf16[1024,1024]{1,0:T(8,128)(2,1)}, bf16[784,1024]{1,0:T(8,128)(2,1)}, bf16[768,1024]{1,0:T(8,128)(2,1)}) custom-call(s32[3]{0:T(128)} %pad_add_fusion.refs_1_.refs_0_.bits, f32[8,1024]{1,0:T(8,128)} %get-tuple-element.146.refs_1_, bf16[1024,1024]{1,0:T(8,128)(2,1)} %get-tuple-element.147.refs_2_, ...), custom_call_target="tpu_custom_call" | custom-call | bytes 209715200 | tf_op jit(solution)/shard_map/pallas_call | solution.py:63
  93.9 2.4 %convert_add_fusion = (f32[256,1024]{1,0:T(8,128)S(1)}, bf16[256,1024]{1,0:T(8,128)(2,1)}) fusion(f32[512,1024]{1,0:T(8,128)S(1)} %get-tuple-element.161, bf16[512,1024]{1,0:T(8,128)(2,1)} %collective-permute-done.1), kind=kLoop, calls=%fused_computation | loop fusion | flops 1310720 | bytes 4718592 | tf_op jit(solution)/shard_map/add | solution.py:653
  96.8 1.0 collective-permute-start.2
  97.8 0.8 slice.162.refs_2_
  98.5 4.0 %all-to-all-done.1 = bf16[8,64,1024]{2,1,0:T(8,128)(2,1)} async-done(((bf16[8,64,1024]{2,1,0:T(8,128)(2,1)}), bf16[8,64,1024]{2,1,0:T(8,128)(2,1)}, u32[]{:S(2)}, u32[]{:S(2)}) %all-to-all-start.1) | async-done | bytes 1048608 | tf_op jit(solution)/shard_map/all_to_all | solution.py:835
  102.5 1.4 copy-done.1
  104.4 1.6 collective-permute-start.5
  106.3 1.2 add_convert_fusion.2
  107.4 3.0 %collective-permute-start.4 = (bf16[128,1024]{1,0:T(8,128)(2,1)S(1)}, bf16[128,1024]{1,0:T(8,128)(2,1)S(1)}, u32[]{:S(2)}, u32[]{:S(2)}) collective-permute-start(bf16[128,1024]{1,0:T(8,128)(2,1)S(1)} %get-tuple-element.253), channel_id=1, source_target_pairs={{0,8},{1,17},{2,10},{3,19},{4,12},{5,21},{6,14},{7,23},{8,0},{9,25... | collective-permute-start | bytes 786440 | tf_op jit(solution)/shard_map/ppermute | solution.py:555
  110.4 6.4 %collective-permute-done.5 = bf16[400,1024]{1,0:T(8,128)(2,1)S(1)} collective-permute-done((bf16[400,1024]{1,0:T(8,128)(2,1)S(1)}, bf16[400,1024]{1,0:T(8,128)(2,1)S(1)}, u32[]{:S(2)}, u32[]{:S(2)}) %collective-permute-start.5) | collective-permute-done | bytes 819232 | tf_op jit(solution)/shard_map/ppermute | solution.py:555
  117.8 1.4 collective-permute-start.6
  119.2 6.1 %collective-permute-done.7 = bf16[208,1024]{1,0:T(8,128)(2,1)S(1)} collective-permute-done((bf16[208,1024]{1,0:T(8,128)(2,1)S(1)}, bf16[208,1024]{1,0:T(8,128)(2,1)S(1)}, u32[]{:S(2)}, u32[]{:S(2)}) %collective-permute-start.7) | collective-permute-done | bytes 426016 | tf_op jit(solution)/shard_map/ppermute | solution.py:555
  125.7 2.9 %collective-permute-start.8 = (bf16[64,1024]{1,0:T(8,128)(2,1)S(1)}, bf16[64,1024]{1,0:T(8,128)(2,1)S(1)}, u32[]{:S(2)}, u32[]{:S(2)}) collective-permute-start(bf16[64,1024]{1,0:T(8,128)(2,1)S(1)} %add_convert_fusion.4), channel_id=1, source_target_pairs={{0,16},{1,9},{2,18},{3,11},{4,20},{5,13},{6,22},{7,15},{8,24},{9,1... | collective-permute-start | bytes 393224 | tf_op jit(solution)/shard_map/ppermute | solution.py:555
  128.6 5.0 %collective-permute-done.8 = bf16[64,1024]{1,0:T(8,128)(2,1)S(1)} collective-permute-done((bf16[64,1024]{1,0:T(8,128)(2,1)S(1)}, bf16[64,1024]{1,0:T(8,128)(2,1)S(1)}, u32[]{:S(2)}, u32[]{:S(2)}) %collective-permute-start.8) | collective-permute-done | bytes 131104 | tf_op jit(solution)/shard_map/ppermute | solution.py:555
  133.6 2.5 %collective-permute-start.9 = (bf16[128,1024]{1,0:T(8,128)(2,1)S(1)}, bf16[128,1024]{1,0:T(8,128)(2,1)S(1)}, u32[]{:S(2)}, u32[]{:S(2)}) collective-permute-start(bf16[128,1024]{1,0:T(8,128)(2,1)S(1)} %constant_dynamic-update-slice_fusion), channel_id=1, source_target_pairs={{0,8},{1,17},{2,10},{3,19},{4,12},{5,21},{6,14},{7,23},{8,0},{9,25... | collective-permute-start | bytes 786440 | tf_op jit(solution)/shard_map/ppermute | solution.py:555
  136.3 1.1 collective-permute-start.11
  137.4 6.0 %collective-permute-done.11 = bf16[64,1024]{1,0:T(8,128)(2,1)S(1)} collective-permute-done((bf16[64,1024]{1,0:T(8,128)(2,1)S(1)}, bf16[64,1024]{1,0:T(8,128)(2,1)S(1)}, u32[]{:S(2)}, u32[]{:S(2)}) %collective-permute-start.11) | collective-permute-done | bytes 131104 | tf_op jit(solution)/shard_map/ppermute | solution.py:555
  143.5 3.1 %collective-permute-start.13 = (bf16[48,1024]{1,0:T(8,128)(2,1)S(1)}, bf16[48,1024]{1,0:T(8,128)(2,1)S(1)}, u32[]{:S(2)}, u32[]{:S(2)}) collective-permute-start(bf16[48,1024]{1,0:T(8,128)(2,1)S(1)} %add_convert_fusion.6), channel_id=1, source_target_pairs={{0,16},{1,9},{2,18},{3,11},{4,20},{5,13},{6,22},{7,15},{8,24},{9,1... | collective-permute-start | bytes 294920 | tf_op jit(solution)/shard_map/ppermute | solution.py:555
  146.6 1.6 collective-permute-start.12
  148.2 0.9 collective-permute-done.13
  149.2 4.8 %collective-permute-start.14 = (bf16[96,1024]{1,0:T(8,128)(2,1)S(1)}, bf16[96,1024]{1,0:T(8,128)(2,1)S(1)}, u32[]{:S(2)}, u32[]{:S(2)}) collective-permute-start(bf16[96,1024]{1,0:T(8,128)(2,1)S(1)} %constant_dynamic-update-slice_fusion.4), channel_id=1, source_target_pairs={{0,8},{1,17},{2,10},{3,19},{4,12},{5,21},{6,14},{7,23},{8,0},{9,25... | collective-permute-start | bytes 589832 | tf_op jit(solution)/shard_map/ppermute | solution.py:555
  154.0 3.6 %collective-permute-done.14 = bf16[96,1024]{1,0:T(8,128)(2,1)S(1)} collective-permute-done((bf16[96,1024]{1,0:T(8,128)(2,1)S(1)}, bf16[96,1024]{1,0:T(8,128)(2,1)S(1)}, u32[]{:S(2)}, u32[]{:S(2)}) %collective-permute-start.14) | collective-permute-done | bytes 196640 | tf_op jit(solution)/shard_map/ppermute | solution.py:555
  157.8 1.6 collective-permute-start.17
  159.4 1.8 collective-permute-start.15
  161.3 11.8 %shard_map.177 = f32[1024,1024]{1,0:T(8,128)} custom-call(s32[1,512]{1,0:T(1,128)} %bitcast.24, f32[1024,128]{1,0:T(8,128)} %get-tuple-element.200.refs_1_, bf16[512,1024]{1,0:T(8,128)(2,1)} %bitcast.12.refs_2_, bf16[1024,1024]{1,0:T(8,128)(2,1)} %get-tuple-element.202.refs_3_, f32[1024,1024]{1,0:T(8,128)} %get-tuple-element.203.refs_4_, ...), custom_call_target="tpu_custom_call" | custom-call | bytes 209715200 | tf_op jit(solution)/shard_map/pallas_call | solution.py:63
  173.2 1.8 shard_map.178
  176.1 1.5 collective-permute-start.16
  177.6 3.2 %collective-permute-done.19.held = bf16[400,1024]{1,0:T(8,128)(2,1)S(1)} collective-permute-done((bf16[400,1024]{1,0:T(8,128)(2,1)S(1)}, bf16[400,1024]{1,0:T(8,128)(2,1)S(1)}, u32[]{:S(2)}, u32[]{:S(2)}) %collective-permute-start.19) | collective-permute-done | bytes 819232 | tf_op jit(solution)/shard_map/ppermute | solution.py:535
  180.8 1.8 shard_map.179
  182.6 3.0 %shard_map.180.refs_0_ = f32[2048,1024]{1,0:T(8,128)} custom-call(s32[3]{0:T(128)S(1)} %copy-done.2, bf16[1024,1024]{1,0:T(8,128)(2,1)S(1)} %constant_dynamic-update-slice_fusion.13.held), custom_call_target="tpu_custom_call" | custom-call | tf_op jit(solution)/shard_map/pallas_call | solution.py:517
  185.6 3.0 %shard_map.181 = f32[2048,1024]{1,0:T(8,128)} custom-call(s32[3]{0:T(128)S(1)} %copy-done.2, bf16[1024,1024]{1,0:T(8,128)(2,1)S(1)} %collective-permute-done.18.held, f32[2048,1024]{1,0:T(8,128)} %shard_map.180.refs_0_), custom_call_target="tpu_custom_call", output_to_operand_aliasing={{}: (2, {})} | custom-call | tf_op jit(solution)/shard_map/pallas_call | solution.py:517
  188.8 0.6 fusion.16
  189.4 1.8 shard_map.182
  191.1 1.8 shard_map.183
  (89 shorter events, 5.5 us)
Async XLA Ops:
  0.6 12.0 %copy-start.5 = (s32[1024,50]{0,1:T(8,128)S(1)}, s32[1024,50]{0,1:T(8,128)}, u32[]{:S(2)}) copy-start(s32[1024,50]{0,1:T(8,128)} %param.14) | copy-start | bytes 614404
  5.2 8.6 %copy-start.4 = (f32[1024,50]{0,1:T(8,128)S(1)}, f32[1024,50]{0,1:T(8,128)}, u32[]{:S(2)}) copy-start(f32[1024,50]{0,1:T(8,128)} %param.15) | copy-start | bytes 614404
  5.2 33.5 %all-to-all-start = ((bf16[8,64,1024]{2,1,0:T(8,128)(2,1)}), bf16[8,64,1024]{2,1,0:T(8,128)(2,1)S(1)}, u32[]{:S(2)}, u32[]{:S(2)}) async-start(bf16[8,64,1024]{2,1,0:T(8,128)(2,1)} %bitcast.15), calls=%async_computation | async-start | bytes 2097152 | tf_op jit(solution)/shard_map/all_to_all | solution.py:789
  12.9 2.1 %copy-start.6 = (s32[1024]{0:T(1024)S(1)}, s32[1024]{0:T(1024)}, u32[]{:S(2)}) copy-start(s32[1024]{0:T(1024)} %param.13) | copy-start | bytes 12292
  38.7 1.0 copy-start.3
  62.5 4.4 %collective-permute-start = (bf16[1024,1024]{1,0:T(8,128)(2,1)}, bf16[1024,1024]{1,0:T(8,128)(2,1)S(1)}, u32[]{:S(2)}, u32[]{:S(2)}) collective-permute-start(bf16[1024,1024]{1,0:T(8,128)(2,1)} %get-tuple-element.141), channel_id=1, source_target_pairs={{0,1},{1,0},{2,3},{3,2},{4,5},{5,4},{6,7},{7,6},{8,9},{9,8},{10,11... | collective-permute-start | bytes 6291464 | tf_op jit(solution)/shard_map/ppermute | solution.py:535
  67.0 1.6 copy-start
  69.0 24.8 %collective-permute-start.1 = (bf16[512,1024]{1,0:T(8,128)(2,1)S(1)}, bf16[512,1024]{1,0:T(8,128)(2,1)}, u32[]{:S(2)}, u32[]{:S(2)}) collective-permute-start(bf16[512,1024]{1,0:T(8,128)(2,1)S(1)} %get-tuple-element.144), channel_id=1, source_target_pairs={{0,4},{1,3},{2,6},{3,1},{4,0},{5,7},{6,2},{7,5},{8,12},{9,11},{10,... | collective-permute-start | bytes 3145736 | tf_op jit(solution)/shard_map/ppermute | solution.py:555
  71.1 31.4 %all-to-all-start.1 = ((bf16[8,64,1024]{2,1,0:T(8,128)(2,1)}), bf16[8,64,1024]{2,1,0:T(8,128)(2,1)}, u32[]{:S(2)}, u32[]{:S(2)}) async-start(bf16[8,64,1024]{2,1,0:T(8,128)(2,1)} %bitcast.17), calls=%async_computation.1 | async-start | bytes 2097152 | tf_op jit(solution)/shard_map/all_to_all | solution.py:835
  96.2 6.3 %collective-permute-start.3 = (bf16[784,1024]{1,0:T(8,128)(2,1)}, bf16[784,1024]{1,0:T(8,128)(2,1)S(1)}, u32[]{:S(2)}, u32[]{:S(2)}) collective-permute-start(bf16[784,1024]{1,0:T(8,128)(2,1)} %get-tuple-element.163), channel_id=1, source_target_pairs={{0,1},{1,0},{2,3},{3,2},{4,5},{5,4},{6,7},{7,6},{8,9},{9,8},{10,11... | collective-permute-start | bytes 4816904 | tf_op jit(solution)/shard_map/ppermute | solution.py:535
  96.8 9.5 %collective-permute-start.2 = (bf16[256,1024]{1,0:T(8,128)(2,1)}, bf16[256,1024]{1,0:T(8,128)(2,1)}, u32[]{:S(2)}, u32[]{:S(2)}) collective-permute-start(bf16[256,1024]{1,0:T(8,128)(2,1)} %get-tuple-element.250), channel_id=1, source_target_pairs={{0,2},{1,5},{2,0},{3,7},{4,6},{5,1},{6,4},{7,3},{8,10},{9,13},{10,... | collective-permute-start | bytes 1572872 | tf_op jit(solution)/shard_map/ppermute | solution.py:555
  102.5 1.4 copy-start.1
  104.4 12.4 %collective-permute-start.5 = (bf16[400,1024]{1,0:T(8,128)(2,1)S(1)}, bf16[400,1024]{1,0:T(8,128)(2,1)S(1)}, u32[]{:S(2)}, u32[]{:S(2)}) collective-permute-start(bf16[400,1024]{1,0:T(8,128)(2,1)S(1)} %get-tuple-element.170), channel_id=1, source_target_pairs={{0,4},{1,3},{2,6},{3,1},{4,0},{5,7},{6,2},{7,5},{8,12},{9,11},{10,... | collective-permute-start | bytes 2457608 | tf_op jit(solution)/shard_map/ppermute | solution.py:555
  107.4 10.3 %collective-permute-start.4 = (bf16[128,1024]{1,0:T(8,128)(2,1)S(1)}, bf16[128,1024]{1,0:T(8,128)(2,1)S(1)}, u32[]{:S(2)}, u32[]{:S(2)}) collective-permute-start(bf16[128,1024]{1,0:T(8,128)(2,1)S(1)} %get-tuple-element.253), channel_id=1, source_target_pairs={{0,8},{1,17},{2,10},{3,19},{4,12},{5,21},{6,14},{7,23},{8,0},{9,25... | collective-permute-start | bytes 786440 | tf_op jit(solution)/shard_map/ppermute | solution.py:555
  117.1 8.2 %collective-permute-start.7 = (bf16[208,1024]{1,0:T(8,128)(2,1)S(1)}, bf16[208,1024]{1,0:T(8,128)(2,1)S(1)}, u32[]{:S(2)}, u32[]{:S(2)}) collective-permute-start(bf16[208,1024]{1,0:T(8,128)(2,1)S(1)} %pad_maximum_fusion.1), channel_id=1, source_target_pairs={{0,2},{1,5},{2,0},{3,7},{4,6},{5,1},{6,4},{7,3},{8,10},{9,13},{10,... | collective-permute-start | bytes 1277960 | tf_op jit(solution)/shard_map/ppermute | solution.py:555
  117.8 7.9 %collective-permute-start.6 = (bf16[64,1024]{1,0:T(8,128)(2,1)S(1)}, bf16[64,1024]{1,0:T(8,128)(2,1)S(1)}, u32[]{:S(2)}, u32[]{:S(2)}) collective-permute-start(bf16[64,1024]{1,0:T(8,128)(2,1)S(1)} %get-tuple-element.257), channel_id=1, source_target_pairs={{0,16},{1,9},{2,18},{3,11},{4,20},{5,13},{6,22},{7,15},{8,24},{9,1... | collective-permute-start | bytes 393224 | tf_op jit(solution)/shard_map/ppermute | solution.py:555
  125.5 10.6 %collective-permute-start.10 = (bf16[112,1024]{1,0:T(8,128)(2,1)S(1)}, bf16[112,1024]{1,0:T(8,128)(2,1)S(1)}, u32[]{:S(2)}, u32[]{:S(2)}) collective-permute-start(bf16[112,1024]{1,0:T(8,128)(2,1)S(1)} %pad_maximum_fusion.2), channel_id=1, source_target_pairs={{0,8},{1,17},{2,10},{3,19},{4,12},{5,21},{6,14},{7,23},{8,0},{9,25... | collective-permute-start | bytes 688136 | tf_op jit(solution)/shard_map/ppermute | solution.py:555
  125.7 7.9 %collective-permute-start.8 = (bf16[64,1024]{1,0:T(8,128)(2,1)S(1)}, bf16[64,1024]{1,0:T(8,128)(2,1)S(1)}, u32[]{:S(2)}, u32[]{:S(2)}) collective-permute-start(bf16[64,1024]{1,0:T(8,128)(2,1)S(1)} %add_convert_fusion.4), channel_id=1, source_target_pairs={{0,16},{1,9},{2,18},{3,11},{4,20},{5,13},{6,22},{7,15},{8,24},{9,1... | collective-permute-start | bytes 393224 | tf_op jit(solution)/shard_map/ppermute | solution.py:555
  133.6 13.0 %collective-permute-start.9 = (bf16[128,1024]{1,0:T(8,128)(2,1)S(1)}, bf16[128,1024]{1,0:T(8,128)(2,1)S(1)}, u32[]{:S(2)}, u32[]{:S(2)}) collective-permute-start(bf16[128,1024]{1,0:T(8,128)(2,1)S(1)} %constant_dynamic-update-slice_fusion), channel_id=1, source_target_pairs={{0,8},{1,17},{2,10},{3,19},{4,12},{5,21},{6,14},{7,23},{8,0},{9,25... | collective-permute-start | bytes 786440 | tf_op jit(solution)/shard_map/ppermute | solution.py:555
  136.3 7.2 %collective-permute-start.11 = (bf16[64,1024]{1,0:T(8,128)(2,1)S(1)}, bf16[64,1024]{1,0:T(8,128)(2,1)S(1)}, u32[]{:S(2)}, u32[]{:S(2)}) collective-permute-start(bf16[64,1024]{1,0:T(8,128)(2,1)S(1)} %pad_maximum_fusion.3), channel_id=1, source_target_pairs={{0,16},{1,9},{2,18},{3,11},{4,20},{5,13},{6,22},{7,15},{8,24},{9,1... | collective-permute-start | bytes 393224 | tf_op jit(solution)/shard_map/ppermute | solution.py:555
  143.5 5.7 %collective-permute-start.13 = (bf16[48,1024]{1,0:T(8,128)(2,1)S(1)}, bf16[48,1024]{1,0:T(8,128)(2,1)S(1)}, u32[]{:S(2)}, u32[]{:S(2)}) collective-permute-start(bf16[48,1024]{1,0:T(8,128)(2,1)S(1)} %add_convert_fusion.6), channel_id=1, source_target_pairs={{0,16},{1,9},{2,18},{3,11},{4,20},{5,13},{6,22},{7,15},{8,24},{9,1... | collective-permute-start | bytes 294920 | tf_op jit(solution)/shard_map/ppermute | solution.py:555
  146.6 11.1 %collective-permute-start.12 = (bf16[256,1024]{1,0:T(8,128)(2,1)S(1)}, bf16[256,1024]{1,0:T(8,128)(2,1)S(1)}, u32[]{:S(2)}, u32[]{:S(2)}) collective-permute-start(bf16[256,1024]{1,0:T(8,128)(2,1)S(1)} %constant_dynamic-update-slice_fusion.2), channel_id=1, source_target_pairs={{0,2},{1,5},{2,0},{3,7},{4,6},{5,1},{6,4},{7,3},{8,10},{9,13},{10,... | collective-permute-start | bytes 1572872 | tf_op jit(solution)/shard_map/ppermute | solution.py:555
  149.2 8.5 %collective-permute-start.14 = (bf16[96,1024]{1,0:T(8,128)(2,1)S(1)}, bf16[96,1024]{1,0:T(8,128)(2,1)S(1)}, u32[]{:S(2)}, u32[]{:S(2)}) collective-permute-start(bf16[96,1024]{1,0:T(8,128)(2,1)S(1)} %constant_dynamic-update-slice_fusion.4), channel_id=1, source_target_pairs={{0,8},{1,17},{2,10},{3,19},{4,12},{5,21},{6,14},{7,23},{8,0},{9,25... | collective-permute-start | bytes 589832 | tf_op jit(solution)/shard_map/ppermute | solution.py:555
  157.8 17.5 %collective-permute-start.17 = (bf16[512,1024]{1,0:T(8,128)(2,1)S(1)}, bf16[512,1024]{1,0:T(8,128)(2,1)S(1)}, u32[]{:S(2)}, u32[]{:S(2)}) collective-permute-start(bf16[512,1024]{1,0:T(8,128)(2,1)S(1)} %constant_dynamic-update-slice_fusion.8), channel_id=1, source_target_pairs={{0,4},{1,3},{2,6},{3,1},{4,0},{5,7},{6,2},{7,5},{8,12},{9,11},{10,... | collective-permute-start | bytes 3145736 | tf_op jit(solution)/shard_map/ppermute | solution.py:555
  159.4 13.7 %collective-permute-start.15 = (bf16[192,1024]{1,0:T(8,128)(2,1)S(1)}, bf16[192,1024]{1,0:T(8,128)(2,1)S(1)}, u32[]{:S(2)}, u32[]{:S(2)}) collective-permute-start(bf16[192,1024]{1,0:T(8,128)(2,1)S(1)} %constant_dynamic-update-slice_fusion.6), channel_id=1, source_target_pairs={{0,2},{1,5},{2,0},{3,7},{4,6},{5,1},{6,4},{7,3},{8,10},{9,13},{10,... | collective-permute-start | bytes 1179656 | tf_op jit(solution)/shard_map/ppermute | solution.py:555
  161.3 11.9 %copy-start.2 = (s32[3]{0:T(128)S(1)}, s32[3]{0:T(128)}, u32[]{:S(2)}) copy-start(s32[3]{0:T(128)} %pad_add_fusion.refs_1_.refs_0_.bits) | copy-start | bytes 40
  175.4 10.2 %collective-permute-start.18 = (bf16[1024,1024]{1,0:T(8,128)(2,1)S(1)}, bf16[1024,1024]{1,0:T(8,128)(2,1)S(1)}, u32[]{:S(2)}, u32[]{:S(2)}) collective-permute-start(bf16[1024,1024]{1,0:T(8,128)(2,1)S(1)} %constant_dynamic-update-slice_fusion.13.held), channel_id=1, source_target_pairs={{0,1},{1,0},{2,3},{3,2},{4,5},{5,4},{6,7},{7,6},{8,9},{9,8},{10,11... | collective-permute-start | bytes 6291464 | tf_op jit(solution)/shard_map/ppermute | solution.py:535
  175.5 5.3 %collective-permute-start.19 = (bf16[400,1024]{1,0:T(8,128)(2,1)S(1)}, bf16[400,1024]{1,0:T(8,128)(2,1)S(1)}, u32[]{:S(2)}, u32[]{:S(2)}) collective-permute-start(bf16[400,1024]{1,0:T(8,128)(2,1)S(1)} %constant_dynamic-update-slice_fusion.10.held), channel_id=1, source_target_pairs={{0,1},{1,0},{2,3},{3,2},{4,5},{5,4},{6,7},{7,6},{8,9},{9,8},{10,11... | collective-permute-start | bytes 2457608 | tf_op jit(solution)/shard_map/ppermute | solution.py:535
  176.1 12.5 %collective-permute-start.16 = (bf16[384,1024]{1,0:T(8,128)(2,1)S(1)}, bf16[384,1024]{1,0:T(8,128)(2,1)S(1)}, u32[]{:S(2)}, u32[]{:S(2)}) collective-permute-start(bf16[384,1024]{1,0:T(8,128)(2,1)S(1)} %pad_maximum_fusion), channel_id=1, source_target_pairs={{0,4},{1,3},{2,6},{3,1},{4,0},{5,7},{6,2},{7,5},{8,12},{9,11},{10,... | collective-permute-start | bytes 2359304 | tf_op jit(solution)/shard_map/ppermute | solution.py:555
  188.6 2.5 %collective-permute-start.20 = (bf16[384,1024]{1,0:T(8,128)(2,1)S(1)}, bf16[384,1024]{1,0:T(8,128)(2,1)S(1)}, u32[]{:S(2)}, u32[]{:S(2)}) collective-permute-start(bf16[384,1024]{1,0:T(8,128)(2,1)S(1)} %collective-permute-done.16.held), channel_id=1, source_target_pairs={{0,1},{1,0},{2,3},{3,2},{4,5},{5,4},{6,7},{7,6},{8,9},{9,8},{10,11... | collective-permute-start | bytes 2359304 | tf_op jit(solution)/shard_map/ppermute | solution.py:535

commit v5 on v4

--- a/solution.py
+++ b/solution.py
@@ -215,10 +215,10 @@
 def combine_kernel(
     live, bits, weight, q_bias, far_hbm, incoming_hbm, proj_hbm, q_hbm, agg_hbm, base_hbm, w_hbm,
     cotangent_hbm, hidden_hbm,
-    embedding_hbm, dpre2_hbm, dagg_hbm, to_peers_hbm, w_sent_hbm, w_kept_hbm, far_hidden_hbm,
+    embedding_hbm, dpre2_hbm, dagg_hbm, to_peers_hbm, w_sent_hbm, w_kept, far_hidden_hbm,
     far_dpre_hbm, far_lowered_hbm, far_slope_hbm, bias,
     far, incoming, proj, q_weight, agg, base, w_low, cotangent, hidden, mean, dpre2, dagg, to_peers,
-    w_sent, w_kept, far_hidden, far_slope, far_lowered, arrived,
+    w_sent, far_hidden, far_slope, far_lowered, arrived,
 ):
     copies = Copies(arrived)
     rows, width = agg.shape
@@ -322,7 +322,7 @@
         far_out += [copies.start(to_peers, to_peers_hbm), copies.start(far_dpre, far_dpre_hbm)]
     got_hidden.wait()
     stride = width // PLACES
-    for target, target_hbm, mark, low in ((w_sent, w_sent_hbm, 2, 1), (w_kept, w_kept_hbm, 1, 0)):
+    for target, target_hbm, mark, low in ((w_sent, w_sent_hbm, 2, 1), (w_kept, None, 1, 0)):
 
         @pl.when(bits[0] == low)
         def _():
@@ -332,7 +332,8 @@
         def _():
             write_pieces(bits[mark], [(mean, 0, dpre2)], width, target, stride, 0)
 
-        far_out += [copies.start(target, target_hbm)]
+        if target_hbm is not None:
+            far_out += [copies.start(target, target_hbm)]
     for copy in far_out:
         copy.wait()
     for out in outs:
@@ -804,7 +805,7 @@
         + buffers(((width, width), BF16), ((rows, rows), BF16), ((rows, halo), BF16))
         + buffers((low, BF16), (low, BF16), (low, F32), (low, BF16), (low, F32), (narrow, BF16))
         + semaphores(9 + 2 * (rows // BLOCK)),
-        tokens=(outgoing,),
+        tokens=(outgoing, bits),
     )(names, weights, kinds, q_bias_row, w_bias_row, features, proj_board, q_weight, w_weight)
 
     weight = (1.0 / jnp.sum(importance, axis=1)).reshape(rows, 1)
@@ -821,13 +822,14 @@
         + (shape(far_low, BF16), shape(far_low, BF16), shape(far_narrow, BF16))
         + (shape(far_low if spot < halo else (8, LANES), F32), shape((8, width), F32)),
         [SMEM, SMEM, whole(rows, 1), whole(1, width)] + [ANY] * 9,
-        (ANY,) * 10 + (whole(8, width),),
+        (ANY,) * 5 + (VMEM,) + (ANY,) * 4 + (whole(8, width),),
         buffers(((rows, halo), BF16), (far_low, BF16), ((lowered, width), BF16))
         + buffers(((width, width), BF16), (low, BF16), (low, F32), ((width, width), BF16))
         + buffers((low, BF16), (low, BF16), (low, BF16), (low, BF16), (low, BF16))
-        + buffers(((spot, width), BF16), (w_dims, BF16), (w_dims, BF16), ((spot, width), BF16))
+        + buffers(((spot, width), BF16), (w_dims, BF16), ((spot, width), BF16))
         + buffers(((spot, width), F32), ((spot, lowered), BF16))
-        + semaphores(15 + 6 * (rows // BLOCK)),
+        + semaphores(14 + 6 * (rows // BLOCK)),
+        limit=56,
     )(
         live_rows, bits, weight, q_bias_row, far, incoming, proj_board, q_weight, agg, base, w_weight,
         cotangent, hidden,

time: 194 us -> 193 us (level)
  no operation moved by 1% of the time
where the time goes in v5:
time: 193 us; the launch traced here: 192 us
  Pallas kernels  91.1 us (47%)
  starting transfers between devices  43.9 us (23%)
  waiting for transfers between devices  40.4 us (21%)
  local copies, waits for them, and re-layouts  10.1 us (5%)
  other arithmetic  5.08 us (3%)
    pallas_call x5, Pallas kernels, call(): return lambda *operands: built(*operands, *tokens)  77.2 us
    ppermute x16, starting transfers between devices, cross(): return lax.ppermute(value, ('dom', 'rep'), pairs)  30.6 us
    ppermute x16, waiting for transfers between devices, cross(): return lax.ppermute(value, ('dom', 'rep'), pairs)  28.8 us
    pallas_call x6, Pallas kernels, ordered(): pl.pallas_call(functools.partial(ordered_kernel, count=len(sizes), other=...  13 us
    ppermute x5, waiting for transfers between devices, swap(): return lax.ppermute(value, axis, [(s, s ^ mask) for s in range(size)])  7.62 us
    all_to_all x1, starting transfers between devices, per_device(): lax.all_to_all(outgoing, 'dom', split_axis=0, concat_axis=0, tiled=True)  7.4 us
    unnamed x24, local copies, waits for them, and re-layouts  4.63 us
    all_to_all x1, starting transfers between devices, per_device(): lax.all_to_all(to_peers, 'dom', split_axis=0, concat_axis=0, tiled=True)  4.54 us
  transfers between devices with their start and end apart: 23, of which 11 were waited for; matrix products, arithmetic and copies ran while one was open for 6% of the time, Pallas kernels for 32%

profile of v5, /device:TPU:0, one launch (start us, length us, event | category | flops | bytes accessed | tf_op | source)
XLA Modules:
  0.0 192.3 jit_solution(598244011445423153)
XLA Ops:
  0.6 4.6 %shard_map.171.refs_9_ = bf16[512,1024]{1,0:T(8,128)(2,1)} custom-call(s32[1,512]{1,0:T(1,128)} %bitcast.23, s32[1,1024]{1,0:T(1,128)} %bitcast.18, bf16[1024,1024]{1,0:T(8,128)(2,1)} %refs_5_.1), custom_call_target="tpu_custom_call" | custom-call | tf_op jit(solution)/shard_map/pallas_call | solution.py:63
  5.2 7.4 %all-to-all-start = ((bf16[8,64,1024]{2,1,0:T(8,128)(2,1)}), bf16[8,64,1024]{2,1,0:T(8,128)(2,1)S(1)}, u32[]{:S(2)}, u32[]{:S(2)}) async-start(bf16[8,64,1024]{2,1,0:T(8,128)(2,1)} %bitcast.15), calls=%async_computation | async-start | bytes 2097152 | tf_op jit(solution)/shard_map/all_to_all | solution.py:790
  12.9 0.9 reshape.50.refs_0_
  14.1 0.9 reshape.51.refs_1_
  14.9 1.1 copy.30.refs_2_
  16.0 1.1 copy.31.refs_2_
  17.7 0.6 pad_add_fusion.refs_10_.refs_1_.refs_0_.bits
  18.3 20.4 %shard_map.172 = (bf16[1024,1024]{1,0:T(8,128)(2,1)}, bf16[1024,512]{1,0:T(8,128)(2,1)}, bf16[1024,1024]{1,0:T(8,128)(2,1)}, f32[1024,1024]{1,0:T(8,128)}, bf16[...) custom-call(s32[128,512]{1,0:T(8,128)} %reshape.50.refs_0_, ...), custom_call_target="tpu_custom_call" | custom-call | tf_op jit(solution)/shard_map/pallas_call | solution.py:63
  38.7 1.0 copy-done.3
  39.7 22.3 %shard_map.173 = (f32[1024,1024]{1,0:T(8,128)}, bf16[1024,1024]{1,0:T(8,128)(2,1)}, bf16[1024,1024]{1,0:T(8,128)(2,1)}, bf16[512,1024]{1,0:T(8,128)(2,1)}, bf16[...) custom-call(s32[1]{0:T(128)S(6)} %copy.49.refs_0_, ...), custom_call_target="tpu_custom_call" | custom-call | tf_op jit(solution)/shard_map/pallas_call | solution.py:63
  62.0 4.4 %collective-permute-done.refs_1_ = bf16[1024,1024]{1,0:T(8,128)(2,1)S(1)} collective-permute-done((bf16[1024,1024]{1,0:T(8,128)(2,1)}, bf16[1024,1024]{1,0:T(8,128)(2,1)S(1)}, u32[]{:S(2)}, u32[]{:S(2)}) %collective-permute-start) | collective-permute-done | bytes 2097184 | tf_op jit(solution)/shard_map/ppermute | solution.py:536
  66.4 1.6 copy-done
  68.4 2.1 %collective-permute-start.1 = (bf16[512,1024]{1,0:T(8,128)(2,1)S(1)}, bf16[512,1024]{1,0:T(8,128)(2,1)}, u32[]{:S(2)}, u32[]{:S(2)}) collective-permute-start(bf16[512,1024]{1,0:T(8,128)(2,1)S(1)} %get-tuple-element.144), channel_id=1, source_target_pairs={{0,4},{1,3},{2,6},{3,1},{4,0},{5,7},{6,2},{7,5},{8,12},{9,11},{10,... | collective-permute-start | bytes 3145736 | tf_op jit(solution)/shard_map/ppermute | solution.py:556
  70.5 4.5 %all-to-all-start.1 = ((bf16[8,64,1024]{2,1,0:T(8,128)(2,1)}), bf16[8,64,1024]{2,1,0:T(8,128)(2,1)}, u32[]{:S(2)}, u32[]{:S(2)}) async-start(bf16[8,64,1024]{2,1,0:T(8,128)(2,1)} %bitcast.17), calls=%async_computation.1 | async-start | bytes 2097152 | tf_op jit(solution)/shard_map/all_to_all | solution.py:837
  75.1 18.2 %shard_map.175 = (bf16[1024,1024]{1,0:T(8,128)(2,1)}, bf16[1024,1024]{1,0:T(8,128)(2,1)}, bf16[784,1024]{1,0:T(8,128)(2,1)}, bf16[768,1024]{1,0:T(8,128)(2,1)}) custom-call(s32[3]{0:T(128)} %pad_add_fusion.refs_10_.refs_1_.refs_0_.bits, f32[8,1024]{1,0:T(8,128)} %get-tuple-element.146.refs_1_, bf16[1024,1024]{1,0:T(8,128)(2,1)} %get-tuple-element.147.refs_2_, ...), custom_call_target="tpu_custom_call" | custom-call | bytes 209715200 | tf_op jit(solution)/shard_map/pallas_call | solution.py:63
  93.3 2.4 %convert_add_fusion = (f32[256,1024]{1,0:T(8,128)S(1)}, bf16[256,1024]{1,0:T(8,128)(2,1)}) fusion(f32[512,1024]{1,0:T(8,128)S(1)} %get-tuple-element.161, bf16[512,1024]{1,0:T(8,128)(2,1)} %collective-permute-done.1), kind=kLoop, calls=%fused_computation | loop fusion | flops 1310720 | bytes 4718592 | tf_op jit(solution)/shard_map/add | solution.py:654
  96.2 1.0 collective-permute-start.2
  97.2 0.8 slice.162.refs_2_
  97.9 4.0 %all-to-all-done.1 = bf16[8,64,1024]{2,1,0:T(8,128)(2,1)} async-done(((bf16[8,64,1024]{2,1,0:T(8,128)(2,1)}), bf16[8,64,1024]{2,1,0:T(8,128)(2,1)}, u32[]{:S(2)}, u32[]{:S(2)}) %all-to-all-start.1) | async-done | bytes 1048608 | tf_op jit(solution)/shard_map/all_to_all | solution.py:837
  101.9 1.4 copy-done.1
  103.8 1.6 collective-permute-start.5
  105.7 1.2 add_convert_fusion.2
  106.9 3.0 %collective-permute-start.4 = (bf16[128,1024]{1,0:T(8,128)(2,1)S(1)}, bf16[128,1024]{1,0:T(8,128)(2,1)S(1)}, u32[]{:S(2)}, u32[]{:S(2)}) collective-permute-start(bf16[128,1024]{1,0:T(8,128)(2,1)S(1)} %get-tuple-element.253), channel_id=1, source_target_pairs={{0,8},{1,17},{2,10},{3,19},{4,12},{5,21},{6,14},{7,23},{8,0},{9,25... | collective-permute-start | bytes 786440 | tf_op jit(solution)/shard_map/ppermute | solution.py:556
  109.8 6.4 %collective-permute-done.5 = bf16[400,1024]{1,0:T(8,128)(2,1)S(1)} collective-permute-done((bf16[400,1024]{1,0:T(8,128)(2,1)S(1)}, bf16[400,1024]{1,0:T(8,128)(2,1)S(1)}, u32[]{:S(2)}, u32[]{:S(2)}) %collective-permute-start.5) | collective-permute-done | bytes 819232 | tf_op jit(solution)/shard_map/ppermute | solution.py:556
  117.2 1.4 collective-permute-start.6
  118.6 6.1 %collective-permute-done.7 = bf16[208,1024]{1,0:T(8,128)(2,1)S(1)} collective-permute-done((bf16[208,1024]{1,0:T(8,128)(2,1)S(1)}, bf16[208,1024]{1,0:T(8,128)(2,1)S(1)}, u32[]{:S(2)}, u32[]{:S(2)}) %collective-permute-start.7) | collective-permute-done | bytes 426016 | tf_op jit(solution)/shard_map/ppermute | solution.py:556
  125.1 2.9 %collective-permute-start.8 = (bf16[64,1024]{1,0:T(8,128)(2,1)S(1)}, bf16[64,1024]{1,0:T(8,128)(2,1)S(1)}, u32[]{:S(2)}, u32[]{:S(2)}) collective-permute-start(bf16[64,1024]{1,0:T(8,128)(2,1)S(1)} %add_convert_fusion.4), channel_id=1, source_target_pairs={{0,16},{1,9},{2,18},{3,11},{4,20},{5,13},{6,22},{7,15},{8,24},{9,1... | collective-permute-start | bytes 393224 | tf_op jit(solution)/shard_map/ppermute | solution.py:556
  128.0 5.0 %collective-permute-done.8 = bf16[64,1024]{1,0:T(8,128)(2,1)S(1)} collective-permute-done((bf16[64,1024]{1,0:T(8,128)(2,1)S(1)}, bf16[64,1024]{1,0:T(8,128)(2,1)S(1)}, u32[]{:S(2)}, u32[]{:S(2)}) %collective-permute-start.8) | collective-permute-done | bytes 131104 | tf_op jit(solution)/shard_map/ppermute | solution.py:556
  133.0 2.5 %collective-permute-start.9 = (bf16[128,1024]{1,0:T(8,128)(2,1)S(1)}, bf16[128,1024]{1,0:T(8,128)(2,1)S(1)}, u32[]{:S(2)}, u32[]{:S(2)}) collective-permute-start(bf16[128,1024]{1,0:T(8,128)(2,1)S(1)} %constant_dynamic-update-slice_fusion), channel_id=1, source_target_pairs={{0,8},{1,17},{2,10},{3,19},{4,12},{5,21},{6,14},{7,23},{8,0},{9,25... | collective-permute-start | bytes 786440 | tf_op jit(solution)/shard_map/ppermute | solution.py:556
  135.7 1.1 collective-permute-start.11
  136.9 6.0 %collective-permute-done.11 = bf16[64,1024]{1,0:T(8,128)(2,1)S(1)} collective-permute-done((bf16[64,1024]{1,0:T(8,128)(2,1)S(1)}, bf16[64,1024]{1,0:T(8,128)(2,1)S(1)}, u32[]{:S(2)}, u32[]{:S(2)}) %collective-permute-start.11) | collective-permute-done | bytes 131104 | tf_op jit(solution)/shard_map/ppermute | solution.py:556
  142.9 3.1 %collective-permute-start.13 = (bf16[48,1024]{1,0:T(8,128)(2,1)S(1)}, bf16[48,1024]{1,0:T(8,128)(2,1)S(1)}, u32[]{:S(2)}, u32[]{:S(2)}) collective-permute-start(bf16[48,1024]{1,0:T(8,128)(2,1)S(1)} %add_convert_fusion.6), channel_id=1, source_target_pairs={{0,16},{1,9},{2,18},{3,11},{4,20},{5,13},{6,22},{7,15},{8,24},{9,1... | collective-permute-start | bytes 294920 | tf_op jit(solution)/shard_map/ppermute | solution.py:556
  146.1 1.6 collective-permute-start.12
  147.6 1.0 collective-permute-done.13
  148.6 4.8 %collective-permute-start.14 = (bf16[96,1024]{1,0:T(8,128)(2,1)S(1)}, bf16[96,1024]{1,0:T(8,128)(2,1)S(1)}, u32[]{:S(2)}, u32[]{:S(2)}) collective-permute-start(bf16[96,1024]{1,0:T(8,128)(2,1)S(1)} %constant_dynamic-update-slice_fusion.4), channel_id=1, source_target_pairs={{0,8},{1,17},{2,10},{3,19},{4,12},{5,21},{6,14},{7,23},{8,0},{9,25... | collective-permute-start | bytes 589832 | tf_op jit(solution)/shard_map/ppermute | solution.py:556
  153.5 3.6 %collective-permute-done.14 = bf16[96,1024]{1,0:T(8,128)(2,1)S(1)} collective-permute-done((bf16[96,1024]{1,0:T(8,128)(2,1)S(1)}, bf16[96,1024]{1,0:T(8,128)(2,1)S(1)}, u32[]{:S(2)}, u32[]{:S(2)}) %collective-permute-start.14) | collective-permute-done | bytes 196640 | tf_op jit(solution)/shard_map/ppermute | solution.py:556
  157.2 1.6 collective-permute-start.17
  158.8 1.8 collective-permute-start.15
  160.7 11.8 %shard_map.177 = f32[1024,1024]{1,0:T(8,128)} custom-call(s32[1,512]{1,0:T(1,128)} %bitcast.24, f32[1024,128]{1,0:T(8,128)} %get-tuple-element.200.refs_1_, bf16[512,1024]{1,0:T(8,128)(2,1)} %bitcast.12.refs_2_, bf16[1024,1024]{1,0:T(8,128)(2,1)} %get-tuple-element.202.refs_3_, f32[1024,1024]{1,0:T(8,128)} %get-tuple-element.203.refs_4_, ...), custom_call_target="tpu_custom_call" | custom-call | bytes 209715200 | tf_op jit(solution)/shard_map/pallas_call | solution.py:63
  172.6 1.8 shard_map.178
  175.5 1.5 collective-permute-start.16
  177.0 3.3 %collective-permute-done.19.held = bf16[400,1024]{1,0:T(8,128)(2,1)S(1)} collective-permute-done((bf16[400,1024]{1,0:T(8,128)(2,1)S(1)}, bf16[400,1024]{1,0:T(8,128)(2,1)S(1)}, u32[]{:S(2)}, u32[]{:S(2)}) %collective-permute-start.19) | collective-permute-done | bytes 819232 | tf_op jit(solution)/shard_map/ppermute | solution.py:536
  180.3 1.8 shard_map.179
  182.0 3.0 %shard_map.180.refs_0_ = f32[2048,1024]{1,0:T(8,128)} custom-call(s32[3]{0:T(128)S(1)} %copy-done.2, bf16[1024,1024]{1,0:T(8,128)(2,1)S(1)} %constant_dynamic-update-slice_fusion.13.held), custom_call_target="tpu_custom_call" | custom-call | tf_op jit(solution)/shard_map/pallas_call | solution.py:518
  185.0 3.0 %shard_map.181 = f32[2048,1024]{1,0:T(8,128)} custom-call(s32[3]{0:T(128)S(1)} %copy-done.2, bf16[1024,1024]{1,0:T(8,128)(2,1)S(1)} %collective-permute-done.18.held, f32[2048,1024]{1,0:T(8,128)} %shard_map.180.refs_0_), custom_call_target="tpu_custom_call", output_to_operand_aliasing={{}: (2, {})} | custom-call | tf_op jit(solution)/shard_map/pallas_call | solution.py:518
  188.2 0.6 fusion.16
  188.8 1.8 shard_map.182
  190.6 1.8 shard_map.183
  (89 shorter events, 5.5 us)
Async XLA Ops:
  0.6 12.0 %copy-start.5 = (s32[1024,50]{0,1:T(8,128)S(1)}, s32[1024,50]{0,1:T(8,128)}, u32[]{:S(2)}) copy-start(s32[1024,50]{0,1:T(8,128)} %param.14) | copy-start | bytes 614404
  5.2 8.6 %copy-start.4 = (f32[1024,50]{0,1:T(8,128)S(1)}, f32[1024,50]{0,1:T(8,128)}, u32[]{:S(2)}) copy-start(f32[1024,50]{0,1:T(8,128)} %param.15) | copy-start | bytes 614404
  5.2 33.4 %all-to-all-start = ((bf16[8,64,1024]{2,1,0:T(8,128)(2,1)}), bf16[8,64,1024]{2,1,0:T(8,128)(2,1)S(1)}, u32[]{:S(2)}, u32[]{:S(2)}) async-start(bf16[8,64,1024]{2,1,0:T(8,128)(2,1)} %bitcast.15), calls=%async_computation | async-start | bytes 2097152 | tf_op jit(solution)/shard_map/all_to_all | solution.py:790
  12.9 2.1 %copy-start.6 = (s32[1024]{0:T(1024)S(1)}, s32[1024]{0:T(1024)}, u32[]{:S(2)}) copy-start(s32[1024]{0:T(1024)} %param.13) | copy-start | bytes 12292
  38.7 1.0 copy-start.3
  61.9 4.4 %collective-permute-start = (bf16[1024,1024]{1,0:T(8,128)(2,1)}, bf16[1024,1024]{1,0:T(8,128)(2,1)S(1)}, u32[]{:S(2)}, u32[]{:S(2)}) collective-permute-start(bf16[1024,1024]{1,0:T(8,128)(2,1)} %get-tuple-element.141), channel_id=1, source_target_pairs={{0,1},{1,0},{2,3},{3,2},{4,5},{5,4},{6,7},{7,6},{8,9},{9,8},{10,11... | collective-permute-start | bytes 6291464 | tf_op jit(solution)/shard_map/ppermute | solution.py:536
  66.4 1.6 copy-start
  68.4 24.8 %collective-permute-start.1 = (bf16[512,1024]{1,0:T(8,128)(2,1)S(1)}, bf16[512,1024]{1,0:T(8,128)(2,1)}, u32[]{:S(2)}, u32[]{:S(2)}) collective-permute-start(bf16[512,1024]{1,0:T(8,128)(2,1)S(1)} %get-tuple-element.144), channel_id=1, source_target_pairs={{0,4},{1,3},{2,6},{3,1},{4,0},{5,7},{6,2},{7,5},{8,12},{9,11},{10,... | collective-permute-start | bytes 3145736 | tf_op jit(solution)/shard_map/ppermute | solution.py:556
  70.5 31.4 %all-to-all-start.1 = ((bf16[8,64,1024]{2,1,0:T(8,128)(2,1)}), bf16[8,64,1024]{2,1,0:T(8,128)(2,1)}, u32[]{:S(2)}, u32[]{:S(2)}) async-start(bf16[8,64,1024]{2,1,0:T(8,128)(2,1)} %bitcast.17), calls=%async_computation.1 | async-start | bytes 2097152 | tf_op jit(solution)/shard_map/all_to_all | solution.py:837
  95.7 6.3 %collective-permute-start.3 = (bf16[784,1024]{1,0:T(8,128)(2,1)}, bf16[784,1024]{1,0:T(8,128)(2,1)S(1)}, u32[]{:S(2)}, u32[]{:S(2)}) collective-permute-start(bf16[784,1024]{1,0:T(8,128)(2,1)} %get-tuple-element.163), channel_id=1, source_target_pairs={{0,1},{1,0},{2,3},{3,2},{4,5},{5,4},{6,7},{7,6},{8,9},{9,8},{10,11... | collective-permute-start | bytes 4816904 | tf_op jit(solution)/shard_map/ppermute | solution.py:536
  96.2 9.5 %collective-permute-start.2 = (bf16[256,1024]{1,0:T(8,128)(2,1)}, bf16[256,1024]{1,0:T(8,128)(2,1)}, u32[]{:S(2)}, u32[]{:S(2)}) collective-permute-start(bf16[256,1024]{1,0:T(8,128)(2,1)} %get-tuple-element.250), channel_id=1, source_target_pairs={{0,2},{1,5},{2,0},{3,7},{4,6},{5,1},{6,4},{7,3},{8,10},{9,13},{10,... | collective-permute-start | bytes 1572872 | tf_op jit(solution)/shard_map/ppermute | solution.py:556
  101.9 1.4 copy-start.1
  103.8 12.4 %collective-permute-start.5 = (bf16[400,1024]{1,0:T(8,128)(2,1)S(1)}, bf16[400,1024]{1,0:T(8,128)(2,1)S(1)}, u32[]{:S(2)}, u32[]{:S(2)}) collective-permute-start(bf16[400,1024]{1,0:T(8,128)(2,1)S(1)} %get-tuple-element.170), channel_id=1, source_target_pairs={{0,4},{1,3},{2,6},{3,1},{4,0},{5,7},{6,2},{7,5},{8,12},{9,11},{10,... | collective-permute-start | bytes 2457608 | tf_op jit(solution)/shard_map/ppermute | solution.py:556
  106.9 10.3 %collective-permute-start.4 = (bf16[128,1024]{1,0:T(8,128)(2,1)S(1)}, bf16[128,1024]{1,0:T(8,128)(2,1)S(1)}, u32[]{:S(2)}, u32[]{:S(2)}) collective-permute-start(bf16[128,1024]{1,0:T(8,128)(2,1)S(1)} %get-tuple-element.253), channel_id=1, source_target_pairs={{0,8},{1,17},{2,10},{3,19},{4,12},{5,21},{6,14},{7,23},{8,0},{9,25... | collective-permute-start | bytes 786440 | tf_op jit(solution)/shard_map/ppermute | solution.py:556
  116.6 8.2 %collective-permute-start.7 = (bf16[208,1024]{1,0:T(8,128)(2,1)S(1)}, bf16[208,1024]{1,0:T(8,128)(2,1)S(1)}, u32[]{:S(2)}, u32[]{:S(2)}) collective-permute-start(bf16[208,1024]{1,0:T(8,128)(2,1)S(1)} %pad_maximum_fusion.1), channel_id=1, source_target_pairs={{0,2},{1,5},{2,0},{3,7},{4,6},{5,1},{6,4},{7,3},{8,10},{9,13},{10,... | collective-permute-start | bytes 1277960 | tf_op jit(solution)/shard_map/ppermute | solution.py:556
  117.2 7.9 %collective-permute-start.6 = (bf16[64,1024]{1,0:T(8,128)(2,1)S(1)}, bf16[64,1024]{1,0:T(8,128)(2,1)S(1)}, u32[]{:S(2)}, u32[]{:S(2)}) collective-permute-start(bf16[64,1024]{1,0:T(8,128)(2,1)S(1)} %get-tuple-element.257), channel_id=1, source_target_pairs={{0,16},{1,9},{2,18},{3,11},{4,20},{5,13},{6,22},{7,15},{8,24},{9,1... | collective-permute-start | bytes 393224 | tf_op jit(solution)/shard_map/ppermute | solution.py:556
  124.9 10.6 %collective-permute-start.10 = (bf16[112,1024]{1,0:T(8,128)(2,1)S(1)}, bf16[112,1024]{1,0:T(8,128)(2,1)S(1)}, u32[]{:S(2)}, u32[]{:S(2)}) collective-permute-start(bf16[112,1024]{1,0:T(8,128)(2,1)S(1)} %pad_maximum_fusion.2), channel_id=1, source_target_pairs={{0,8},{1,17},{2,10},{3,19},{4,12},{5,21},{6,14},{7,23},{8,0},{9,25... | collective-permute-start | bytes 688136 | tf_op jit(solution)/shard_map/ppermute | solution.py:556
  125.1 7.9 %collective-permute-start.8 = (bf16[64,1024]{1,0:T(8,128)(2,1)S(1)}, bf16[64,1024]{1,0:T(8,128)(2,1)S(1)}, u32[]{:S(2)}, u32[]{:S(2)}) collective-permute-start(bf16[64,1024]{1,0:T(8,128)(2,1)S(1)} %add_convert_fusion.4), channel_id=1, source_target_pairs={{0,16},{1,9},{2,18},{3,11},{4,20},{5,13},{6,22},{7,15},{8,24},{9,1... | collective-permute-start | bytes 393224 | tf_op jit(solution)/shard_map/ppermute | solution.py:556
  133.0 13.0 %collective-permute-start.9 = (bf16[128,1024]{1,0:T(8,128)(2,1)S(1)}, bf16[128,1024]{1,0:T(8,128)(2,1)S(1)}, u32[]{:S(2)}, u32[]{:S(2)}) collective-permute-start(bf16[128,1024]{1,0:T(8,128)(2,1)S(1)} %constant_dynamic-update-slice_fusion), channel_id=1, source_target_pairs={{0,8},{1,17},{2,10},{3,19},{4,12},{5,21},{6,14},{7,23},{8,0},{9,25... | collective-permute-start | bytes 786440 | tf_op jit(solution)/shard_map/ppermute | solution.py:556
  135.7 7.2 %collective-permute-start.11 = (bf16[64,1024]{1,0:T(8,128)(2,1)S(1)}, bf16[64,1024]{1,0:T(8,128)(2,1)S(1)}, u32[]{:S(2)}, u32[]{:S(2)}) collective-permute-start(bf16[64,1024]{1,0:T(8,128)(2,1)S(1)} %pad_maximum_fusion.3), channel_id=1, source_target_pairs={{0,16},{1,9},{2,18},{3,11},{4,20},{5,13},{6,22},{7,15},{8,24},{9,1... | collective-permute-start | bytes 393224 | tf_op jit(solution)/shard_map/ppermute | solution.py:556
  142.9 5.7 %collective-permute-start.13 = (bf16[48,1024]{1,0:T(8,128)(2,1)S(1)}, bf16[48,1024]{1,0:T(8,128)(2,1)S(1)}, u32[]{:S(2)}, u32[]{:S(2)}) collective-permute-start(bf16[48,1024]{1,0:T(8,128)(2,1)S(1)} %add_convert_fusion.6), channel_id=1, source_target_pairs={{0,16},{1,9},{2,18},{3,11},{4,20},{5,13},{6,22},{7,15},{8,24},{9,1... | collective-permute-start | bytes 294920 | tf_op jit(solution)/shard_map/ppermute | solution.py:556
  146.1 11.1 %collective-permute-start.12 = (bf16[256,1024]{1,0:T(8,128)(2,1)S(1)}, bf16[256,1024]{1,0:T(8,128)(2,1)S(1)}, u32[]{:S(2)}, u32[]{:S(2)}) collective-permute-start(bf16[256,1024]{1,0:T(8,128)(2,1)S(1)} %constant_dynamic-update-slice_fusion.2), channel_id=1, source_target_pairs={{0,2},{1,5},{2,0},{3,7},{4,6},{5,1},{6,4},{7,3},{8,10},{9,13},{10,... | collective-permute-start | bytes 1572872 | tf_op jit(solution)/shard_map/ppermute | solution.py:556
  148.6 8.5 %collective-permute-start.14 = (bf16[96,1024]{1,0:T(8,128)(2,1)S(1)}, bf16[96,1024]{1,0:T(8,128)(2,1)S(1)}, u32[]{:S(2)}, u32[]{:S(2)}) collective-permute-start(bf16[96,1024]{1,0:T(8,128)(2,1)S(1)} %constant_dynamic-update-slice_fusion.4), channel_id=1, source_target_pairs={{0,8},{1,17},{2,10},{3,19},{4,12},{5,21},{6,14},{7,23},{8,0},{9,25... | collective-permute-start | bytes 589832 | tf_op jit(solution)/shard_map/ppermute | solution.py:556
  157.2 17.5 %collective-permute-start.17 = (bf16[512,1024]{1,0:T(8,128)(2,1)S(1)}, bf16[512,1024]{1,0:T(8,128)(2,1)S(1)}, u32[]{:S(2)}, u32[]{:S(2)}) collective-permute-start(bf16[512,1024]{1,0:T(8,128)(2,1)S(1)} %constant_dynamic-update-slice_fusion.8), channel_id=1, source_target_pairs={{0,4},{1,3},{2,6},{3,1},{4,0},{5,7},{6,2},{7,5},{8,12},{9,11},{10,... | collective-permute-start | bytes 3145736 | tf_op jit(solution)/shard_map/ppermute | solution.py:556
  158.8 13.7 %collective-permute-start.15 = (bf16[192,1024]{1,0:T(8,128)(2,1)S(1)}, bf16[192,1024]{1,0:T(8,128)(2,1)S(1)}, u32[]{:S(2)}, u32[]{:S(2)}) collective-permute-start(bf16[192,1024]{1,0:T(8,128)(2,1)S(1)} %constant_dynamic-update-slice_fusion.6), channel_id=1, source_target_pairs={{0,2},{1,5},{2,0},{3,7},{4,6},{5,1},{6,4},{7,3},{8,10},{9,13},{10,... | collective-permute-start | bytes 1179656 | tf_op jit(solution)/shard_map/ppermute | solution.py:556
  160.7 11.9 %copy-start.2 = (s32[3]{0:T(128)S(1)}, s32[3]{0:T(128)}, u32[]{:S(2)}) copy-start(s32[3]{0:T(128)} %pad_add_fusion.refs_10_.refs_1_.refs_0_.bits) | copy-start | bytes 40
  174.9 10.2 %collective-permute-start.18 = (bf16[1024,1024]{1,0:T(8,128)(2,1)S(1)}, bf16[1024,1024]{1,0:T(8,128)(2,1)S(1)}, u32[]{:S(2)}, u32[]{:S(2)}) collective-permute-start(bf16[1024,1024]{1,0:T(8,128)(2,1)S(1)} %constant_dynamic-update-slice_fusion.13.held), channel_id=1, source_target_pairs={{0,1},{1,0},{2,3},{3,2},{4,5},{5,4},{6,7},{7,6},{8,9},{9,8},{10,11... | collective-permute-start | bytes 6291464 | tf_op jit(solution)/shard_map/ppermute | solution.py:536
  175.0 5.3 %collective-permute-start.19 = (bf16[400,1024]{1,0:T(8,128)(2,1)S(1)}, bf16[400,1024]{1,0:T(8,128)(2,1)S(1)}, u32[]{:S(2)}, u32[]{:S(2)}) collective-permute-start(bf16[400,1024]{1,0:T(8,128)(2,1)S(1)} %constant_dynamic-update-slice_fusion.10.held), channel_id=1, source_target_pairs={{0,1},{1,0},{2,3},{3,2},{4,5},{5,4},{6,7},{7,6},{8,9},{9,8},{10,11... | collective-permute-start | bytes 2457608 | tf_op jit(solution)/shard_map/ppermute | solution.py:536
  175.5 12.5 %collective-permute-start.16 = (bf16[384,1024]{1,0:T(8,128)(2,1)S(1)}, bf16[384,1024]{1,0:T(8,128)(2,1)S(1)}, u32[]{:S(2)}, u32[]{:S(2)}) collective-permute-start(bf16[384,1024]{1,0:T(8,128)(2,1)S(1)} %pad_maximum_fusion), channel_id=1, source_target_pairs={{0,4},{1,3},{2,6},{3,1},{4,0},{5,7},{6,2},{7,5},{8,12},{9,11},{10,... | collective-permute-start | bytes 2359304 | tf_op jit(solution)/shard_map/ppermute | solution.py:556
  188.0 2.5 %collective-permute-start.20 = (bf16[384,1024]{1,0:T(8,128)(2,1)S(1)}, bf16[384,1024]{1,0:T(8,128)(2,1)S(1)}, u32[]{:S(2)}, u32[]{:S(2)}) collective-permute-start(bf16[384,1024]{1,0:T(8,128)(2,1)S(1)} %collective-permute-done.16.held), channel_id=1, source_target_pairs={{0,1},{1,0},{2,3},{3,2},{4,5},{5,4},{6,7},{7,6},{8,9},{9,8},{10,11... | collective-permute-start | bytes 2359304 | tf_op jit(solution)/shard_map/ppermute | solution.py:536
